TPU v7x, 128 devices: a whole 4x4x4 slice. The times are simulated.
128 devices in a mesh: rows: 32 (over z_lo, y, x), seq: 4 (over z_hi, core).
Axes of the slice: x: 4, y: 4, z: 4 (z_hi: 2, z_lo: 2; z = z_hi * 2 + z_lo), core: 2. Of those that a mesh axis runs over, the one named last changes fastest.
Arguments:
- block_input: bfloat16 [32, 512, 768], P('rows', 'seq'), may hold values from -6 to 6
- out_cotangent: bfloat16 [32, 512, 768], P('rows', 'seq'), may hold values from -6 to 6
- image_lengths: int32 [32, 4], P('rows'), may hold values from 12 to 476, as said below
- span_order: int32 [32, 4], P('rows'), may hold values from 0 to 3, each once within a row
- attn_gain: float32 [768], replicated, may hold values from 0.25 to 1.75
- attn_shift: float32 [768], replicated, may hold values from -4 to 4
- qkv_weight: bfloat16 [768, 2304], replicated, may hold values from -0.21875 to 0.21875
- query_bias: float32 [768], replicated, may hold values from -4 to 4
- value_bias: float32 [768], replicated, may hold values from -4 to 4
- proj_weight: bfloat16 [768, 768], replicated, may hold values from -0.875 to 0.875
- proj_bias: float32 [768], replicated, may hold values from -4 to 4
- mlp_gain: float32 [768], replicated, may hold values from 0.25 to 1.75
- mlp_shift: float32 [768], replicated, may hold values from -4 to 4
- up_weight: bfloat16 [768, 3072], replicated, may hold values from -0.21875 to 0.21875
- up_bias: float32 [3072], replicated, may hold values from -4 to 4
- down_weight: bfloat16 [3072, 768], replicated, may hold values from -0.109375 to 0.109375
- down_bias: float32 [768], replicated, may hold values from -4 to 4
Outputs:
- block_output: bfloat16 [32, 512, 768], P('rows', 'seq')
- input_grad: bfloat16 [32, 512, 768], P('rows', 'seq')
- attn_gain_grad: float32 [768], replicated
- attn_shift_grad: float32 [768], replicated
- qkv_weight_grad: float32 [768, 2304], replicated
- query_bias_grad: float32 [768], replicated
- value_bias_grad: float32 [768], replicated
- proj_weight_grad: float32 [768, 768], replicated
- proj_bias_grad: float32 [768], replicated
- mlp_gain_grad: float32 [768], replicated
- mlp_shift_grad: float32 [768], replicated
- up_weight_grad: float32 [768, 3072], replicated
- up_bias_grad: float32 [3072], replicated
- down_weight_grad: float32 [3072, 768], replicated
- down_bias_grad: float32 [768], replicated
Inputs may be any that keep to these rules, and one draw needn't show every extreme that they name: `image_lengths`: the 4 lengths of each row sum to 512. In each row one of them, at a place drawn for that row, holds the rest of the row and is 386 or more, so that this image covers tokens of every block of the row; each of the others is 12, 18 or 32. Each row of span_order is an ordering of the numbers 0 to 4 - 1; the device at index j of seq holds the row's tokens span_order[row, j] * 128 to span_order[row, j] * 128 + 127.
All inputs are finite; a program needn't handle non-finite values.
Results may differ from a plain program's by a relative error of at most 0.02.
Values may be sent and summed in bfloat16 or wider, within the bound.
A program may use at most 192 MiB of HBM per device.

v0:
```python
from functools import partial

import jax
import jax.numpy as jnp
from jax import lax
from jax.sharding import PartitionSpec as P

HEADS = 12
HEAD_DIM = 64


epsilon = 1e-06


def segment_ids(image_lengths, span_order, span_len):
    part_count = span_order.shape[1]
    places = jnp.arange(part_count * span_len, dtype=jnp.int32)
    span_index = places // span_len
    matches = span_index[None, :, None] == jnp.arange(part_count, dtype=jnp.int32)[None, None, :]
    picked = jnp.sum(jnp.where(matches, span_order[:, None, :], 0), axis=2, dtype=jnp.int32)
    anchor = picked * span_len + places[None, :] % span_len
    image_ends = jnp.cumsum(image_lengths, axis=1, dtype=jnp.int32)[:, :-1]
    return jnp.sum(
        (anchor[:, :, None] >= image_ends[:, None, :]).astype(jnp.int32), axis=2, dtype=jnp.int32
    )


def layer_norm(values, gain_vec, shift_vec):
    mean_val = jnp.mean(values, axis=-1, keepdims=True)
    centred = values - mean_val
    factor = lax.rsqrt(jnp.mean(centred * centred, axis=-1, keepdims=True) + epsilon)
    normed = centred * factor
    return (normed * gain_vec + shift_vec, normed, factor)


def norm_back(upstream, normed, factor, gain_vec):
    scaled_grad = upstream * gain_vec
    return factor * (
        scaled_grad
        - jnp.mean(scaled_grad, axis=-1, keepdims=True)
        - normed * jnp.mean(scaled_grad * normed, axis=-1, keepdims=True)
    )


def weight_product(left, right):
    return jnp.einsum("td,te->de", left, right, preferred_element_type=jnp.float32)


def times_transposed(left, right):
    return jnp.einsum("te,de->td", left, right, preferred_element_type=jnp.float32)


def pairs_joined(stacked, row_count, length, width):
    return stacked.transpose(1, 2, 0, 3).reshape(row_count, length, width)


def body(
    block_input,
    out_cotangent,
    image_lengths,
    span_order,
    attn_gain,
    attn_shift,
    qkv_weight,
    query_bias,
    value_bias,
    proj_weight,
    proj_bias,
    mlp_gain,
    mlp_shift,
    up_weight,
    up_bias,
    down_weight,
    down_bias,
):
    row_count, span_len, model_width = block_input.shape
    seq_parts = lax.axis_size("seq")
    full_len = span_len * seq_parts
    token_count = row_count * span_len
    pair_count = HEADS // 2
    pair_width = 2 * HEAD_DIM
    head_scale = HEAD_DIM ** (-0.5)
    pair_numbers = jnp.arange(pair_count, dtype=jnp.int32)
    segments = segment_ids(image_lengths, span_order, span_len)
    own_segments = lax.dynamic_slice_in_dim(segments, lax.axis_index("seq") * span_len, span_len, 1)
    same_image = own_segments[:, :, None] == segments[:, None, :]
    flat_input = block_input.reshape(token_count, model_width).astype(jnp.float32)
    attn_normed, attn_hat, attn_factor = layer_norm(flat_input, attn_gain, attn_shift)
    attn_low = attn_normed.astype(jnp.bfloat16)
    qkv_out = jnp.dot(attn_low, qkv_weight, preferred_element_type=jnp.float32)
    queries = (
        (qkv_out[:, :model_width] + query_bias)
        .astype(jnp.bfloat16)
        .reshape(row_count, span_len, model_width)
    )
    keys_local = (
        qkv_out[:, model_width : 2 * model_width]
        .astype(jnp.bfloat16)
        .reshape(row_count, span_len, model_width)
    )
    values_local = (
        (qkv_out[:, 2 * model_width :] + value_bias)
        .astype(jnp.bfloat16)
        .reshape(row_count, span_len, model_width)
    )
    keys_whole, values_whole = (
        lax.all_gather(keys_local, "seq", axis=1, tiled=True),
        lax.all_gather(values_local, "seq", axis=1, tiled=True),
    )

    def pair_slice(source, pair_index, source_len):
        picked = lax.dynamic_slice_in_dim(source, pair_index * pair_width, pair_width, 2)
        return picked.reshape(row_count, source_len, 2, HEAD_DIM)

    def pair_scores(pair_index, key_source):
        query_part = pair_slice(queries, pair_index, span_len)
        key_part = pair_slice(key_source, pair_index, full_len)
        scores = (
            jnp.einsum("rqhd,rkhd->rhqk", query_part, key_part, preferred_element_type=jnp.float32)
            * head_scale
        )
        return (jnp.where(same_image[:, None], scores, -1e30), query_part, key_part)

    def attend_pair(pair_index):
        scores, query_part, key_part = pair_scores(pair_index, keys_whole)
        row_max = jnp.max(scores, axis=3, keepdims=True)
        exp_scores = jnp.exp(scores - row_max)
        row_sum = jnp.sum(exp_scores, axis=3, keepdims=True)
        weights = (exp_scores / row_sum).astype(jnp.bfloat16)
        value_part = pair_slice(values_whole, pair_index, full_len)
        attended = jnp.einsum(
            "rhqk,rkhd->rqhd", weights, value_part, preferred_element_type=jnp.float32
        )
        return (
            attended.reshape(row_count, span_len, pair_width).astype(jnp.bfloat16),
            row_max + jnp.log(row_sum),
        )

    attended_pairs, log_sums = lax.map(attend_pair, pair_numbers)
    attended_low = attended_pairs.transpose(1, 2, 0, 3).reshape(token_count, model_width)
    resid = (
        flat_input
        + jnp.dot(attended_low, proj_weight, preferred_element_type=jnp.float32)
        + proj_bias
    )
    mlp_normed, mlp_hat, mlp_factor = layer_norm(resid, mlp_gain, mlp_shift)
    mlp_low = mlp_normed.astype(jnp.bfloat16)
    up_pre = jnp.dot(mlp_low, up_weight, preferred_element_type=jnp.float32) + up_bias
    hidden, gelu_back = jax.vjp(partial(jax.nn.gelu, approximate=False), up_pre)
    hidden_low = hidden.astype(jnp.bfloat16)
    block_output = (
        resid + jnp.dot(hidden_low, down_weight, preferred_element_type=jnp.float32) + down_bias
    )
    block_output = block_output.astype(jnp.bfloat16).reshape(row_count, span_len, model_width)
    cotangent = out_cotangent.reshape(token_count, model_width)
    cotangent_full = cotangent.astype(jnp.float32)
    down_weight_grad = weight_product(hidden_low, cotangent)
    down_bias_grad = jnp.sum(cotangent_full, axis=0)
    hidden_grad = times_transposed(cotangent, down_weight)
    up_grad = gelu_back(hidden_grad)[0]
    up_bias_grad = jnp.sum(up_grad, axis=0)
    up_low = up_grad.astype(jnp.bfloat16)
    up_weight_grad = weight_product(mlp_low, up_low)
    mlp_grad = times_transposed(up_low, up_weight)
    mlp_gain_grad = jnp.sum(mlp_grad * mlp_hat, axis=0)
    mlp_shift_grad = jnp.sum(mlp_grad, axis=0)
    resid_grad = cotangent_full + norm_back(mlp_grad, mlp_hat, mlp_factor, mlp_gain)
    proj_bias_grad = jnp.sum(resid_grad, axis=0)
    resid_low = resid_grad.astype(jnp.bfloat16)
    proj_weight_grad = weight_product(attended_low, resid_low)
    attended_grad = times_transposed(resid_low, proj_weight).astype(jnp.bfloat16)
    attended_grad = attended_grad.reshape(row_count, span_len, model_width)
    keys_again, values_again = (
        lax.all_gather(keys_local, "seq", axis=1, tiled=True),
        lax.all_gather(values_local, "seq", axis=1, tiled=True),
    )

    def query_side_pair(pair_index):
        scores, query_part, key_part = pair_scores(pair_index, keys_again)
        probs = jnp.exp(scores - log_sums[pair_index])
        grad_part = pair_slice(attended_grad, pair_index, span_len)
        value_part = pair_slice(values_again, pair_index, full_len)
        prob_grad = jnp.einsum(
            "rqhd,rkhd->rhqk", grad_part, value_part, preferred_element_type=jnp.float32
        )
        totals = jnp.sum(probs * prob_grad, axis=3, keepdims=True)
        score_low = (probs * (prob_grad - totals)).astype(jnp.bfloat16)
        query_grad = (
            jnp.einsum("rhqk,rkhd->rqhd", score_low, key_part, preferred_element_type=jnp.float32)
            * head_scale
        )
        return (probs, score_low, query_part, grad_part, query_grad, totals)

    def pair_backward(pair_index):
        probs, score_low, query_part, grad_part, query_grad, totals = query_side_pair(pair_index)
        weights = probs.astype(jnp.bfloat16)
        value_grad = jnp.einsum(
            "rhqk,rqhd->rkhd", weights, grad_part, preferred_element_type=jnp.float32
        )
        key_grad = (
            jnp.einsum("rhqk,rqhd->rkhd", score_low, query_part, preferred_element_type=jnp.float32)
            * head_scale
        )
        return (
            query_grad.reshape(row_count, span_len, pair_width),
            key_grad.reshape(row_count, full_len, pair_width),
            value_grad.reshape(row_count, full_len, pair_width),
        )

    query_pairs, key_pairs, value_pairs = lax.map(pair_backward, pair_numbers)
    key_value_term = jnp.concatenate(
        (
            pairs_joined(key_pairs, row_count, full_len, model_width),
            pairs_joined(value_pairs, row_count, full_len, model_width),
        ),
        axis=2,
    )
    key_value_grad = (
        lax.psum_scatter(
            key_value_term.astype(jnp.bfloat16), "seq", scatter_dimension=1, tiled=True
        )
        .astype(jnp.float32)
        .reshape(token_count, 2 * model_width)
    )
    query_grad = query_pairs.transpose(1, 2, 0, 3).reshape(token_count, model_width)
    query_bias_grad = jnp.sum(query_grad, axis=0)
    value_bias_grad = jnp.sum(key_value_grad[:, model_width:], axis=0)
    qkv_low = jnp.concatenate((query_grad, key_value_grad), axis=1).astype(jnp.bfloat16)
    qkv_weight_grad = weight_product(attn_low, qkv_low)
    attn_grad = times_transposed(qkv_low, qkv_weight)
    attn_gain_grad = jnp.sum(attn_grad * attn_hat, axis=0)
    attn_shift_grad = jnp.sum(attn_grad, axis=0)
    input_grad = resid_grad + norm_back(attn_grad, attn_hat, attn_factor, attn_gain)
    input_grad = input_grad.astype(jnp.bfloat16).reshape(row_count, span_len, model_width)
    summed = lax.psum(
        (
            attn_gain_grad,
            attn_shift_grad,
            qkv_weight_grad,
            query_bias_grad,
            value_bias_grad,
            proj_weight_grad,
            proj_bias_grad,
            mlp_gain_grad,
            mlp_shift_grad,
            up_weight_grad,
            up_bias_grad,
            down_weight_grad,
            down_bias_grad,
        ),
        ("rows", "seq"),
    )
    return (
        block_output,
        input_grad,
        summed[0],
        summed[1],
        summed[2],
        summed[3],
        summed[4],
        summed[5],
        summed[6],
        summed[7],
        summed[8],
        summed[9],
        summed[10],
        summed[11],
        summed[12],
    )


def solution(mesh):
    return jax.shard_map(
        body,
        mesh=mesh,
        in_specs=(
            P("rows", "seq", None),
            P("rows", "seq", None),
            P("rows", None),
            P("rows", None),
            P(),
            P(),
            P(),
            P(),
            P(),
            P(),
            P(),
            P(),
            P(),
            P(),
            P(),
            P(),
            P(),
        ),
        out_specs=(
            P("rows", "seq", None),
            P("rows", "seq", None),
            P(),
            P(),
            P(),
            P(),
            P(),
            P(),
            P(),
            P(),
            P(),
            P(),
            P(),
            P(),
            P(),
        ),
        check_vma=False,
    )
```

profile of v0, /device:TPU:1, one launch (start us, length us, event | category | flops | bytes accessed | tf_op | source)
XLA Modules:
  0.0 510.1 jit_solution(15808423685647162365)
XLA Ops:
  7.3 1.0 reduce_window_sum.11
  8.3 1.0 convert_reduce_fusion.1
  9.3 1.1 fusion.38
  11.3 1.6 fusion.70
  14.4 1.7 copy.47
  16.2 13.9 %all-gather.1 = bf16[512,768]{1,0:T(8,128)(2,1)} all-gather(bf16[128,768]{1,0:T(8,128)(2,1)} %slice.41), channel_id=3, replica_groups=mesh['rows'=32,'seq'=4] {'seq'}, dimensions={0}, use_global_device_ids=true | all-gather | bytes 983040 | tf_op jit(solution)/shard_map/all_gather | solution.py:107
  30.1 2.3 copy.48
  32.4 10.9 %all-gather = bf16[512,768]{1,0:T(8,128)(2,1)} all-gather(bf16[128,768]{1,0:T(8,128)(2,1)} %get-tuple-element.309), channel_id=2, replica_groups=mesh['rows'=32,'seq'=4] {'seq'}, dimensions={0}, use_global_device_ids=true | all-gather | bytes 983040 | tf_op jit(solution)/shard_map/all_gather | solution.py:108
  43.2 2.3 copy.46
  46.2 35.4 %while.28 = (s32[]{:T(128)}, bf16[6,1,128,128]{2,3,1,0:T(8,128)(2,1)}, f32[6,1,2,128,1]{3,2,4,1,0:T(2,128)}, s32[6]{0:T(128)S(1)}, bf16[1,512,768]{1,2,0:T(8,128...) while((s32[]{:T(128)}, ...), condition=%wide.region_8.9_spmd.clone, body=%wide.region_5.8_spmd.clone.sunk | while | flops 34684676 | bytes 2697935 | solution.py:139
  49.0 1.0 constant_dynamic-slice_fusion.14
  54.9 1.0 constant_dynamic-slice_fusion.14
  60.8 1.0 constant_dynamic-slice_fusion.14
  66.7 1.0 constant_dynamic-slice_fusion.14
  72.6 1.0 constant_dynamic-slice_fusion.14
  78.5 1.0 constant_dynamic-slice_fusion.14
  81.7 1.9 fusion.74
  83.9 7.5 %multiply_convert_fusion.1 = (bf16[128,3072]{1,0:T(8,128)(2,1)}, f32[128,3072]{1,0:T(8,128)S(1)}) fusion(f32[3072]{0:T(1024)S(1)} %copy-done.36, bf16[768,3072]{1,0:T(8,128)(2,1)} %param.34, f32[128,768]{1,0:T(8,128)S(1)} %get-tuple-element.312, f32[768]{0:T(1024)S(1)} %copy-done.18, f32[768]{0:T(1024)S(1)} %copy-done.15, f32[128]{0:T(128)S(1)} %add_rsqrt_fusion, ...), kind=kOutput, calls=%fused_computation.40 | convolution fusion | flops 630423552 | bytes 7490560 | tf_op jit(solution)/shard_map/dot_general | solution.py:148
  91.5 5.5 %fusion.75 = (f32[3072]{0:T(1024)}, bf16[128,3072]{1,0:T(8,128)(2,1)S(1)}) fusion(f32[128,3072]{1,0:T(8,128)S(1)} %get-tuple-element.314, bf16[3072,768]{1,0:T(8,128)(2,1)S(1)} %bitcast.226, bf16[1,128,768]{2,1,0:T(8,128)(2,1)S(1)} %copy-done.13), kind=kOutput, calls=%fused_computation.145 | convolution fusion | flops 632681472 | bytes 7286784 | tf_op jit(solution)/shard_map/te,de->td/dot_general | solution.py:50
  97.0 2.3 multiply_reduce_fusion.1
  101.0 1.2 fusion.21
  102.2 81.8 %while.29 = (s32[]{:T(128)}, f32[6,1,128,128]{2,3,1,0:T(8,128)}, bf16[6,1,512,128]{2,3,1,0:T(8,128)(2,1)}, bf16[6,1,512,128]{2,3,1,0:T(8,128)(2,1)}, s32[6]{0:T(...) while((s32[]{:T(128)}, f32[6,1,128,128]{2,3,1,0:T(8,128)}, ...), condition=%wide.region_15.16_spmd.clone, body=%wide.region_13.15_spmd.clone.sunk | while | flops 85278464 | bytes 6430769 | solution.py:210
  106.0 1.4 constant_dynamic-slice_fusion.17
  107.4 1.5 copy.60
  110.4 0.9 constant_dynamic-slice_fusion.18
  111.3 0.9 constant_dynamic-slice_fusion.16
  112.3 1.1 fusion.136
  119.7 1.4 constant_dynamic-slice_fusion.17
  121.1 1.5 copy.60
  124.1 0.9 constant_dynamic-slice_fusion.18
  125.9 1.1 fusion.136
  133.3 1.4 constant_dynamic-slice_fusion.17
  134.7 1.5 copy.60
  139.5 1.1 fusion.136
  146.9 1.4 constant_dynamic-slice_fusion.17
  148.3 1.5 copy.60
  153.2 1.1 fusion.136
  160.6 1.4 constant_dynamic-slice_fusion.17
  161.9 1.5 copy.60
  166.8 1.1 fusion.136
  174.2 1.4 constant_dynamic-slice_fusion.17
  175.6 1.5 copy.60
  180.4 1.1 fusion.136
  184.0 2.6 pad_maximum_fusion
  186.6 8.3 %copy.53 = bf16[1,512,1536]{2,0,1:T(2,128)(2,1)} copy(bf16[1,512,1536]{1,2,0:T(8,128)(2,1)} %pad_maximum_fusion) | data formatting | bytes 3145728
  195.0 3.4 copy.58
  198.6 1.7 bitcast_convert_fusion
  200.3 3.0 fusion.55
  203.4 5.2 %fusion.49 = f32[3072,768]{1,0:T(8,128)} fusion(bf16[128,3072]{1,0:T(8,128)(2,1)S(1)} %copy-done.7, bf16[1,128,768]{2,1,0:T(8,128)(2,1)S(1)} %copy-done.14), kind=kOutput, calls=%fused_computation.107 | convolution fusion | flops 603979776 | bytes 10420224 | tf_op jit(solution)/shard_map/td,te->de/dot_general | solution.py:46
  208.5 5.3 %fusion.41 = f32[768,3072]{1,0:T(8,128)} fusion(bf16[128,3072]{1,0:T(8,128)(2,1)S(1)} %copy-done.9, f32[128,768]{1,0:T(8,128)S(1)} %copy-done.2, f32[768]{0:T(1024)S(1)} %copy-done.18, f32[768]{0:T(1024)S(1)} %copy-done.15, f32[128]{0:T(128)S(1)} %copy-done.28, f32[128]{0:T(128)S(1)} %copy-done.23), kind=kOutput, calls=%fused_computation.94 | convolution fusion | flops 604471296 | bytes 10624000 | tf_op jit(solution)/shard_map/td,te->de/dot_general | solution.py:46
  213.8 19.8 %reduce-scatter.4.cloned.1.call-done = bf16[128,1536]{1,0:T(8,128)(2,1)} async-done(((bf16[512,1536]{1,0:T(8,128)(2,1)}), bf16[128,1536]{1,0:T(8,128)(2,1)}) %reduce-scatter.4.cloned.1.call-update) | async-done | bytes 393232
  233.6 2.3 reshape_bitcast_fusion
  235.9 2.9 copy.54
  238.8 5.3 %fusion.45 = f32[768,2304]{1,0:T(8,128)} fusion(bf16[128,1536]{0,1:T(8,128)(2,1)} %bitcast.231, bf16[128,768]{0,1:T(8,128)(2,1)} %bitcast.239, bf16[1,128,768]{2,1,0:T(8,128)(2,1)} %param.21, f32[768]{0:T(1024)S(1)} %copy-done.17, f32[768]{0:T(1024)S(1)} %copy-done.16, f32[128]{0:T(128)S(1)} %copy-done.30, f32[128]{0:T(128)S(1)} %copy-done.25), kind=kOutput, calls=%fused_computation.100 | convolution fusion | flops 454754304 | bytes 7871488 | tf_op jit(solution)/shard_map/td,te->de/dot_general | solution.py:46
  244.2 1.8 bitcast_reduce_fusion
  246.0 4.2 fusion.22
  250.9 2.7 fusion.37
  253.6 67.0 %all-reduce = (f32[768]{0:T(1024)}, f32[768]{0:T(1024)}, f32[768]{0:T(1024)}, f32[768]{0:T(1024)}, f32[768]{0:T(1024)}, /*index=5*/f32[768]{0:T(1024)}, f32[768]{0:T(1024)}, f32[3072]{0:T(1024)}, f32[768]{0:T(1024)}) all-reduce(f32[768]{0:T(1024)} %get-tuple-element.237, ...), channel_id=1, replica_groups=mesh['rows'=32,'seq'=4] {'rows','seq'}, use_global_device_ids=true, to_apply=%region_20.21 | all-reduce | flops 9216 | bytes 73728 | tf_op jit(solution)/shard_map/psum | solution.py:235
  321.9 2.1 fusion.48
  324.1 158.2 %all-reduce.4.cloned.1.call-done = (f32[768,2304]{1,0:T(8,128)}, f32[768,768]{1,0:T(8,128)}, f32[768,3072]{1,0:T(8,128)}, f32[3072,768]{1,0:T(8,128)}) async-done(((f32[768,2304]{1,0:T(8,128)}, f32[768,768]{1,0:T(8,128)}, f32[768,3072]{1,0:T(8,128)}, f32[3072,768]{1,0:T(8,128)}), (f32[768,2304]{1,0:T(8,128)}, f32[768,768]{1,0:T(8,128)}, f32[768,3072]{1,0:T(8,128)}, ...) | async-done | bytes 28311568 | tf_op jit(solution)/shard_map/psum | solution.py:235
  482.2 6.6 %copy.91 = f32[768,2304]{1,0:T(8,128)} copy(f32[768,2304]{1,0:T(8,128)} %get-tuple-element.561) | data formatting | bytes 14155776
  488.8 1.4 copy.92
  490.2 9.3 %copy.93 = f32[768,3072]{1,0:T(8,128)} copy(f32[768,3072]{1,0:T(8,128)} %get-tuple-element.568) | data formatting | bytes 18874368
  499.5 3.7 copy.94
  (277 shorter events, 72.1 us)
Async XLA Ops:
  7.2 4.1 copy-start
  7.2 226.4 %reduce-scatter.4.cloned.1.call-start = ((), (), s32[]{:S(2)}) async-start(), calls=%async_computation.1 | async-start | bytes 1966080
  9.3 3.6 copy-start.24
  10.5 2.4 copy-start.29
  11.2 2.4 copy-start.32
  11.3 2.4 copy-start.33
  46.2 35.5 %copy-start.34 = (f32[768]{0:T(1024)S(1)}, f32[768]{0:T(1024)}, u32[]{:S(2)}) copy-start(f32[768]{0:T(1024)} %param.31) | copy-start | bytes 9220
  81.7 2.2 copy-start.15
  81.7 2.2 copy-start.18
  81.7 2.2 copy-start.36
  81.7 9.8 %slice-start.5 = ((s8[4718592]{0:T(1024)(128)(4,1)}), s8[4194304]{0:T(1024)(128)(4,1)S(1)}, s32[]{:S(2)}) async-start(s8[4718592]{0:T(1024)(128)(4,1)} %bitcast.225), calls=%async_computation.8 | async-start | bytes 8388608
  83.6 15.7 %copy-start.1 = (f32[128,768]{1,0:T(8,128)}, f32[128,768]{1,0:T(8,128)S(1)}, u32[]{:S(2)}) copy-start(f32[128,768]{1,0:T(8,128)S(1)} %get-tuple-element.312) | copy-start | bytes 1179652
  83.7 15.7 %copy-start.22 = (f32[128]{0:T(128)}, f32[128]{0:T(128)S(1)}, u32[]{:S(2)}) copy-start(f32[128]{0:T(128)S(1)} %broadcast_multiply_fusion.4) | copy-start | bytes 1540
  83.9 15.5 %copy-start.27 = (f32[128]{0:T(128)}, f32[128]{0:T(128)S(1)}, u32[]{:S(2)}) copy-start(f32[128]{0:T(128)S(1)} %add_rsqrt_fusion) | copy-start | bytes 1540
  83.9 7.6 %slice-start.6 = ((s8[4718592]{0:T(1024)(128)(4,1)}), s8[524288]{0:T(1024)(128)(4,1)S(1)}, s32[]{:S(2)}) async-start(s8[4718592]{0:T(1024)(128)(4,1)} %bitcast.225), calls=%async_computation.9 | async-start | bytes 1048576
  83.9 7.6 %copy-start.13 = (bf16[1,128,768]{2,1,0:T(8,128)(2,1)S(1)}, bf16[1,128,768]{2,1,0:T(8,128)(2,1)}, u32[]{:S(2)}) copy-start(bf16[1,128,768]{2,1,0:T(8,128)(2,1)} %param.22) | copy-start | bytes 589828
  83.9 13.1 %slice-start.3 = ((s8[4718592]{0:T(1024)(128)(4,1)}), s8[4194304]{0:T(1024)(128)(4,1)S(1)}, s32[]{:S(2)}) async-start(s8[4718592]{0:T(1024)(128)(4,1)} %bitcast.223), calls=%async_computation.6 | async-start | bytes 8388608
  91.5 5.5 %slice-start.4 = ((s8[4718592]{0:T(1024)(128)(4,1)}), s8[524288]{0:T(1024)(128)(4,1)S(1)}, s32[]{:S(2)}) async-start(s8[4718592]{0:T(1024)(128)(4,1)} %bitcast.223), calls=%async_computation.7 | async-start | bytes 1048576
  97.0 2.3 copy-start.8
  99.3 1.6 copy-start.6
  100.2 0.8 copy-start.5
  102.2 3.2 copy-start.37
  112.3 1.6 copy-start.4
  113.8 2.1 copy-start.38
  115.8 3.2 copy-start.37
  125.9 1.6 copy-start.4
  127.4 2.1 copy-start.38
  129.5 3.2 copy-start.37
  139.5 1.6 copy-start.4
  141.0 2.1 copy-start.38
  143.1 3.2 copy-start.37
  153.1 1.6 copy-start.4
  154.7 2.1 copy-start.38
  156.7 3.2 copy-start.37
  166.8 1.6 copy-start.4
  168.3 2.1 copy-start.38
  170.4 3.2 copy-start.37
  180.4 1.6 copy-start.4
  182.0 2.1 copy-start.38
  198.4 283.9 %all-reduce.4.cloned.1.call-start = ((), (), s32[]{:S(2)}) async-start(), calls=%async_computation.2 | async-start | bytes 56623104 | tf_op jit(solution)/shard_map/psum | solution.py:235
  200.3 3.0 copy-start.7
  200.3 3.0 copy-start.14
  203.3 5.2 %copy-start.2 = (f32[128,768]{1,0:T(8,128)S(1)}, f32[128,768]{1,0:T(8,128)}, u32[]{:S(2)}) copy-start(f32[128,768]{1,0:T(8,128)} %copy-done.1) | copy-start | bytes 1179652
  203.3 5.2 %copy-start.9 = (bf16[128,3072]{1,0:T(8,128)(2,1)S(1)}, bf16[128,3072]{1,0:T(8,128)(2,1)}, u32[]{:S(2)}) copy-start(bf16[128,3072]{1,0:T(8,128)(2,1)} %copy-done.8) | copy-start | bytes 2359300
  203.3 5.2 %copy-start.23 = (f32[128]{0:T(128)S(1)}, f32[128]{0:T(128)}, u32[]{:S(2)}) copy-start(f32[128]{0:T(128)} %copy-done.22) | copy-start | bytes 1540
  203.4 5.2 %copy-start.28 = (f32[128]{0:T(128)S(1)}, f32[128]{0:T(128)}, u32[]{:S(2)}) copy-start(f32[128]{0:T(128)} %copy-done.27) | copy-start | bytes 1540
  213.8 25.0 %copy-start.16 = (f32[768]{0:T(1024)S(1)}, f32[768]{0:T(1024)}, u32[]{:S(2)}) copy-start(f32[768]{0:T(1024)} %param.25) | copy-start | bytes 9220
  213.8 25.0 %copy-start.17 = (f32[768]{0:T(1024)S(1)}, f32[768]{0:T(1024)}, u32[]{:S(2)}) copy-start(f32[768]{0:T(1024)} %param.26) | copy-start | bytes 9220
  213.8 25.0 %copy-start.25 = (f32[128]{0:T(128)S(1)}, f32[128]{0:T(128)}, u32[]{:S(2)}) copy-start(f32[128]{0:T(128)} %copy-done.24) | copy-start | bytes 1540
  213.8 25.0 %copy-start.30 = (f32[128]{0:T(128)S(1)}, f32[128]{0:T(128)}, u32[]{:S(2)}) copy-start(f32[128]{0:T(128)} %copy-done.29) | copy-start | bytes 1540
  244.1 1.8 copy-start.35
  245.9 4.2 copy-start.10
  245.9 4.9 copy-start.3
  245.9 4.9 copy-start.12
  245.9 4.9 copy-start.26
  245.9 4.9 copy-start.31
  250.9 2.7 copy-start.19
  250.9 2.7 copy-start.20
  250.9 2.7 copy-start.21
  482.2 6.6 %copy-start.11 = (f32[768,768]{1,0:T(8,128)S(1)}, f32[768,768]{1,0:T(8,128)}, u32[]{:S(2)}) copy-start(f32[768,768]{1,0:T(8,128)} %get-tuple-element.564) | copy-start | bytes 7077892
  488.8 10.7 %slice-start = ((s8[9437184]{0:T(1024)(128)(4,1)}), s8[4194304]{0:T(1024)(128)(4,1)S(1)}, s32[]{:S(2)}) async-start(s8[9437184]{0:T(1024)(128)(4,1)} %bitcast.215), calls=%async_computation.3 | async-start | bytes 8388608
  490.2 9.3 %slice-start.1 = ((s8[9437184]{0:T(1024)(128)(4,1)}), s8[4194304]{0:T(1024)(128)(4,1)S(1)}, s32[]{:S(2)}) async-start(s8[9437184]{0:T(1024)(128)(4,1)} %bitcast.215), calls=%async_computation.4 | async-start | bytes 8388608
  490.2 9.3 %slice-start.2 = ((s8[9437184]{0:T(1024)(128)(4,1)}), s8[1048576]{0:T(1024)(128)(4,1)S(1)}, s32[]{:S(2)}) async-start(s8[9437184]{0:T(1024)(128)(4,1)} %bitcast.215), calls=%async_computation.5 | async-start | bytes 2097152
Sparse Core Ops, SparseCore 0:
  198.5 35.0 reduce-scatter.3
  244.3 237.8 all-reduce.3
where the time goes:
time: 514 us; the launch traced here: 510 us
  waiting for transfers between devices  178 us (35%)
  local copies, waits for them, and re-layouts  112 us (22%)
  blocking collectives  91.8 us (18%)
  matrix products  62.3 us (12%)
  other arithmetic  30.7 us (6%)
  loops' own time  20.2 us (4%)
  between operations  14.5 us (3%)
    psum x1, waiting for transfers between devices, body(): lax.psum((attn_gain_grad, attn_shift_grad, qkv_weight_grad, query_bias_gr...  158 us
    psum x1, blocking collectives, body(): lax.psum((attn_gain_grad, attn_shift_grad, qkv_weight_grad, query_bias_gr...  67 us
    unnamed x97, local copies, waits for them, and re-layouts  45.2 us
    dynamic_slice x42, local copies, waits for them, and re-layouts, pair_slice(): lax.dynamic_slice_in_dim(source, pair_index * pair_width, pair_width, 2)  43.2 us
    unnamed x3, waiting for transfers between devices  19.8 us
    dot_general x4, matrix products, weight_product(): jnp.einsum('td,te->de', left, right, preferred_element_type=jnp.float32)  18.8 us
    another operation x1, loops' own time, body(): query_pairs, key_pairs, value_pairs = lax.map(pair_backward, pair_numbers)  16.1 us
    all_gather x1, blocking collectives, body(): lax.all_gather(keys_local, 'seq', axis=1, tiled=True)  13.9 us
  transfers between devices with their start and end apart: 2, of which 2 were waited for; matrix products, arithmetic and copies ran while one was open for 5% of the time, Pallas kernels for 0%

commit v1 on v0

--- a/solution.py
+++ b/solution.py
@@ -3,6 +3,8 @@
 import jax
 import jax.numpy as jnp
 from jax import lax
+from jax.experimental import pallas as pl
+from jax.experimental.pallas import tpu as pltpu
 from jax.sharding import PartitionSpec as P
 
 HEADS = 12
@@ -52,6 +54,194 @@
 
 def pairs_joined(stacked, row_count, length, width):
     return stacked.transpose(1, 2, 0, 3).reshape(row_count, length, width)
+
+
+MESH = pl.DeviceIdType.MESH
+DIMS = 6
+SETS = 3
+STEPS = 10
+
+
+def place():
+    row, seq = lax.axis_index("rows"), lax.axis_index("seq")
+    x, y, z_lo = row % 4, (row // 4) % 4, row // 16
+    z_hi, core = seq // 2, seq % 2
+    z = z_hi * 2 + z_lo
+
+    def device(x, y, z, core):
+        return ((z % 2) * 16 + y * 4 + x, (z // 2) * 2 + core)
+
+    near = lambda v: v + 1 - 2 * (v % 2)
+    far = lambda v: 3 - v
+    partners = (
+        device(near(x), y, z, core),
+        device(far(x), y, z, core),
+        device(x, near(y), z, core),
+        device(x, far(y), z, core),
+        device(x, y, near(z), core),
+        device(x, y, far(z), core),
+    )
+    first = lambda v: (v % 2 + v // 2) % 2
+    bits = (first(x), x // 2, first(y), y // 2, first(z), z // 2)
+    sibling = device(x, y, z, 1 - core)
+    return partners, bits, sibling, core
+
+
+def add_into(target, source):
+    target[...] = (target[...].astype(jnp.float32) + source[...].astype(jnp.float32)).astype(
+        jnp.bfloat16
+    )
+
+
+class Exchange:
+    def __init__(self, grads, whole, landing, send_sem, recv_sem):
+        self.partners, self.bits, self.sibling, self.core = place()
+        self.grads, self.whole, self.landing = grads, whole, landing
+        self.send_sem, self.recv_sem = send_sem, recv_sem
+        self.copies = {}
+
+    def dim(self, k, s):
+        return (k + s) % DIMS
+
+    def rows(self, k, s):
+        low = 128 * k
+        for t in range(min(s, 3)):
+            low = low + self.bits[self.dim(k, t)] * (64 >> t)
+        return low
+
+    def block(self, w, k, s, mine, whole=False):
+        held = self.whole.at[w, self.core] if whole else self.grads.at[w]
+        bit = self.bits[self.dim(k, s)]
+        pick = bit if mine else 1 - bit
+        if s < 3:
+            size = 64 >> s
+            low = pl.multiple_of(self.rows(k, s) + pick * size, 16)
+            return held.at[pl.ds(low, size)]
+        low = pl.multiple_of(self.rows(k, 3), 16)
+        return held.at[pl.ds(low, 16), pl.ds(pl.multiple_of(pick * 768, 128), 768)]
+
+    def slot(self, w, k, s):
+        if s < 3:
+            return self.landing.at[w, k, pl.ds((0, 64, 96)[s], 64 >> s)]
+        return self.landing.at[w, k, pl.ds((112, 112, 128)[s - 3], 16), pl.ds((0, 768, 0)[s - 3], 768)]
+
+    def start(self, w, k, s):
+        if s < 4:
+            src, dst, d = self.block(w, k, s, False), self.slot(w, k, s), self.dim(k, s)
+        elif s < 6:
+            src, dst, d = self.block(w, k, 3, True), self.slot(w, k, s), self.dim(k, s)
+        else:
+            t = 9 - s
+            src = dst = self.block(w, k, t, True, True)
+            d = self.dim(k, t)
+        copy = pltpu.make_async_remote_copy(
+            src_ref=src,
+            dst_ref=dst,
+            send_sem=self.send_sem.at[w, k, s],
+            recv_sem=self.recv_sem.at[w, k, s],
+            device_id=self.partners[d],
+            device_id_type=MESH,
+        )
+        copy.start()
+        self.copies[w, k, s] = copy
+
+    def across(self, w, k, part):
+        src = self.block(w, k, 0, part == 0, True)
+        copy = pltpu.make_async_remote_copy(
+            src_ref=src,
+            dst_ref=src,
+            send_sem=self.send_sem.at[w, k, STEPS + part],
+            recv_sem=self.recv_sem.at[w, k, STEPS + part],
+            device_id=self.sibling,
+            device_id_type=MESH,
+        )
+        copy.start()
+        self.copies[w, k, STEPS + part] = copy
+
+    def finish(self, w, s):
+        for k in range(DIMS):
+            self.copies[w, k, s].wait()
+            if s < 4:
+                add_into(self.block(w, k, s, True), self.slot(w, k, s))
+            elif s < 6:
+                add_into(self.block(w, k, 3, True), self.slot(w, k, s))
+            if s == 5:
+                self.block(w, k, 3, True, True)[...] = self.block(w, k, 3, True)[...]
+            if s < STEPS - 1:
+                self.start(w, k, s + 1)
+                if s == STEPS - 2:
+                    self.across(w, k, 0)
+            else:
+                self.across(w, k, 1)
+
+    def done(self, w):
+        for k in range(DIMS):
+            self.copies[w, k, STEPS].wait()
+            self.copies[w, k, STEPS + 1].wait()
+
+
+def reduce_kernel(parts, grads_out, grads, whole, halves, landing, send_sem, recv_sem, half_sem, local_sem):
+    ex = Exchange(grads, whole, landing, send_sem, recv_sem)
+    barrier = pltpu.get_barrier_semaphore()
+    for device in ex.partners + (ex.sibling,):
+        pl.semaphore_signal(barrier, inc=1, device_id=device, device_id_type=MESH)
+    load = pltpu.make_async_copy(parts.at[:, ex.core], grads, local_sem)
+    load.start()
+    pl.semaphore_wait(barrier, DIMS + 1)
+    load.wait()
+    copies = []
+    for w in range(SETS):
+        copy = pltpu.make_async_remote_copy(
+            src_ref=parts.at[w, 1 - ex.core],
+            dst_ref=halves.at[w],
+            send_sem=half_sem.at[0, w],
+            recv_sem=half_sem.at[1, w],
+            device_id=ex.sibling,
+            device_id_type=MESH,
+        )
+        copy.start()
+        copies.append(copy)
+    for w in range(SETS):
+        copies[w].wait()
+
+        def add(i, carry):
+            rows = pl.ds(pl.multiple_of(i * 64, 64), 64)
+            add_into(grads.at[w, rows], halves.at[w, rows])
+            return carry
+
+        lax.fori_loop(0, 12, add, 0)
+        for k in range(DIMS):
+            ex.start(w, k, 0)
+    for s in range(STEPS):
+        for w in range(SETS):
+            ex.finish(w, s)
+    for w in range(SETS):
+        ex.done(w)
+    store = pltpu.make_async_copy(whole, grads_out, local_sem)
+    store.start()
+    store.wait()
+
+
+def reduce_grads(parts):
+    return pl.pallas_call(
+        reduce_kernel,
+        out_shape=jax.ShapeDtypeStruct((SETS, 2, 768, 1536), jnp.bfloat16),
+        in_specs=[pl.BlockSpec(memory_space=pl.ANY)],
+        out_specs=pl.BlockSpec(memory_space=pl.ANY),
+        scratch_shapes=[
+            pltpu.VMEM((SETS, 768, 1536), jnp.bfloat16),
+            pltpu.VMEM((SETS, 2, 768, 1536), jnp.bfloat16),
+            pltpu.VMEM((SETS, 768, 1536), jnp.bfloat16),
+            pltpu.VMEM((SETS, DIMS, 144, 1536), jnp.bfloat16),
+            pltpu.SemaphoreType.DMA((SETS, DIMS, STEPS + 2)),
+            pltpu.SemaphoreType.DMA((SETS, DIMS, STEPS + 2)),
+            pltpu.SemaphoreType.DMA((2, SETS)),
+            pltpu.SemaphoreType.DMA,
+        ],
+        compiler_params=pltpu.CompilerParams(
+            collective_id=0, has_side_effects=True, vmem_limit_bytes=48 << 20
+        ),
+    )(parts)
 
 
 def body(
@@ -232,23 +422,53 @@
     attn_shift_grad = jnp.sum(attn_grad, axis=0)
     input_grad = resid_grad + norm_back(attn_grad, attn_hat, attn_factor, attn_gain)
     input_grad = input_grad.astype(jnp.bfloat16).reshape(row_count, span_len, model_width)
-    summed = lax.psum(
+    low = jnp.bfloat16
+    down_parts = down_weight_grad.reshape(2, 2, 768, 768).transpose(0, 2, 1, 3).reshape(2, 768, 1536)
+    up_parts = up_weight_grad.reshape(768, 2, 1536).transpose(1, 0, 2)
+    attn_parts = jnp.concatenate(
+        (
+            qkv_weight_grad.reshape(768, 2, 1152).transpose(1, 0, 2),
+            proj_weight_grad.reshape(768, 2, 384).transpose(1, 0, 2),
+        ),
+        axis=2,
+    )
+    total = reduce_grads(
+        jnp.stack((down_parts.astype(low), up_parts.astype(low), attn_parts.astype(low)))
+    )
+    down_sum = (
+        total[0].reshape(2, 768, 2, 768).transpose(0, 2, 1, 3).reshape(3072, 768).astype(jnp.float32)
+    )
+    up_sum = total[1].transpose(1, 0, 2).reshape(768, 3072).astype(jnp.float32)
+    qkv_sum = total[2, :, :, :1152].transpose(1, 0, 2).reshape(768, 2304).astype(jnp.float32)
+    proj_sum = total[2, :, :, 1152:].transpose(1, 0, 2).reshape(768, 768).astype(jnp.float32)
+    vectors = lax.psum(
         (
             attn_gain_grad,
             attn_shift_grad,
-            qkv_weight_grad,
             query_bias_grad,
             value_bias_grad,
-            proj_weight_grad,
             proj_bias_grad,
             mlp_gain_grad,
             mlp_shift_grad,
-            up_weight_grad,
             up_bias_grad,
-            down_weight_grad,
             down_bias_grad,
         ),
         ("rows", "seq"),
+    )
+    summed = (
+        vectors[0],
+        vectors[1],
+        qkv_sum,
+        vectors[2],
+        vectors[3],
+        proj_sum,
+        vectors[4],
+        vectors[5],
+        vectors[6],
+        up_sum,
+        vectors[7],
+        down_sum,
+        vectors[8],
     )
     return (
         block_output,

time: 514 us -> 509 us (level)
  waiting for transfers between devices: 178 us -> 0.03 us
  Pallas kernels: 0 us -> 81.9 us
  local copies, waits for them, and re-layouts: 112 us -> 175 us
  other arithmetic: 30.7 us -> 62.6 us
    psum x1 -> x0, waiting for transfers between devices: 158 us -> none  [body(): lax.psum((attn_gain_grad, attn_shift_grad, qkv_weight_grad, query_bias_gr...]
    pallas_call x0 -> x1, Pallas kernels: none -> 81.9 us  [reduce_grads(): pl.pallas_call(reduce_kernel, out_shape=jax.ShapeDtypeStruct((SETS, 2, 76...]
    convert_element_type x0 -> x8, local copies, waits for them, and re-layouts: none -> 60 us  [the longest x2 20.5 us: body(): total[0].reshape(2, 768, 2, 768).transpose(0, 2, 1, 3).reshape(3072, 768)]
    convert_element_type x0 -> x3, other arithmetic: none -> 20.2 us  [the longest x1 13.3 us: body(): total[0].reshape(2, 768, 2, 768).transpose(0, 2, 1, 3).reshape(3072, 768)]
    unnamed x3 -> x2, waiting for transfers between devices: 19.8 us -> 0.03 us
    another operation x3 -> x4, other arithmetic: 1.69 us -> 11.3 us  [the longest x1 10.6 us: body(): jnp.stack((down_parts.astype(low), up_parts.astype(low), attn_parts.astyp...]
    dot_general x4, matrix products: 18.8 us -> 13.5 us  [weight_product(): jnp.einsum('td,te->de', left, right, preferred_element_type=jnp.float32)]
    unnamed x97 -> x90, local copies, waits for them, and re-layouts: 45.2 us -> 44.2 us
  transfers between devices with their start and end apart: 2 -> 1, of which waited for: 2 -> 0; matrix products, arithmetic and copies ran while one was open for 5% -> 9% of each run, Pallas kernels for 0% -> 0%
where the time goes in v1:
time: 509 us; the launch traced here: 504 us
  local copies, waits for them, and re-layouts  175 us (34%)
  blocking collectives  88.6 us (17%)
  Pallas kernels  81.9 us (16%)
  other arithmetic  62.6 us (12%)
  matrix products  60.5 us (12%)
  loops' own time  20.2 us (4%)
  between operations  14.5 us (3%)
    pallas_call x1, Pallas kernels, reduce_grads(): pl.pallas_call(reduce_kernel, out_shape=jax.ShapeDtypeStruct((SETS, 2, 76...  81.9 us
    psum x1, blocking collectives, body(): lax.psum((attn_gain_grad, attn_shift_grad, query_bias_grad, value_bias_gr...  63.8 us
    unnamed x90, local copies, waits for them, and re-layouts  44.2 us
    dynamic_slice x42, local copies, waits for them, and re-layouts, pair_slice(): lax.dynamic_slice_in_dim(source, pair_index * pair_width, pair_width, 2)  43.1 us
    convert_element_type x2, local copies, waits for them, and re-layouts, body(): total[0].reshape(2, 768, 2, 768).transpose(0, 2, 1, 3).reshape(3072, 768)  20.5 us
    another operation x1, loops' own time, body(): query_pairs, key_pairs, value_pairs = lax.map(pair_backward, pair_numbers)  16.1 us
    all_gather x1, blocking collectives, body(): lax.all_gather(keys_local, 'seq', axis=1, tiled=True)  13.9 us
    dot_general x4, matrix products, weight_product(): jnp.einsum('td,te->de', left, right, preferred_element_type=jnp.float32)  13.5 us
  transfers between devices with their start and end apart: 1, of which 0 were waited for; matrix products, arithmetic and copies ran while one was open for 9% of the time, Pallas kernels for 0%

profile of v1, /device:TPU:1, one launch (start us, length us, event | category | flops | bytes accessed | tf_op | source)
XLA Modules:
  0.0 503.8 jit_solution(12349796179078742721)
XLA Ops:
  9.3 1.1 fusion.58
  11.3 1.6 fusion.72
  14.4 1.7 copy.94
  16.2 13.9 %all-gather.1 = bf16[512,768]{1,0:T(8,128)(2,1)} all-gather(bf16[128,768]{1,0:T(8,128)(2,1)} %slice.61), channel_id=3, replica_groups=mesh['rows'=32,'seq'=4] {'seq'}, dimensions={0}, use_global_device_ids=true | all-gather | bytes 983040 | tf_op jit(solution)/shard_map/all_gather | solution.py:297
  30.1 2.3 copy.95
  32.4 10.9 %all-gather = bf16[512,768]{1,0:T(8,128)(2,1)} all-gather(bf16[128,768]{1,0:T(8,128)(2,1)} %get-tuple-element.373), channel_id=2, replica_groups=mesh['rows'=32,'seq'=4] {'seq'}, dimensions={0}, use_global_device_ids=true | all-gather | bytes 983040 | tf_op jit(solution)/shard_map/all_gather | solution.py:298
  43.3 2.3 copy.93
  46.2 35.4 %while.28 = (s32[]{:T(128)}, bf16[6,1,128,128]{2,3,1,0:T(8,128)(2,1)}, f32[6,1,2,128,1]{3,2,4,1,0:T(2,128)}, s32[6]{0:T(128)S(1)}, bf16[1,512,768]{1,2,0:T(8,128...) while((s32[]{:T(128)}, ...), condition=%wide.region_8.9_spmd.clone, body=%wide.region_5.8_spmd.clone.sunk | while | flops 34684676 | bytes 2697935 | solution.py:329
  81.7 1.9 fusion.102
  83.9 7.5 %fusion.16 = (bf16[3072,128]{0,1:T(8,128)(2,1)}, f32[128,3072]{1,0:T(8,128)S(1)}) fusion(f32[3072]{0:T(1024)S(1)} %copy-done.32, bf16[768,3072]{1,0:T(8,128)(2,1)} %param.34, f32[128,768]{1,0:T(8,128)S(1)} %get-tuple-element.378, f32[768]{0:T(1024)S(1)} %copy-done.15, f32[768]{0:T(1024)S(1)} %copy-done.14, f32[128]{0:T(128)S(1)} %add_rsqrt_fusion, ...), kind=kOutput, calls=%fused_computation.49 | convolution fusion | flops 630423552 | bytes 7490560 | tf_op jit(solution)/shard_map/dot_general | solution.py:338
  91.5 5.5 %fusion.103 = (f32[3072]{0:T(1024)}, bf16[128,3072]{1,0:T(8,128)(2,1)S(1)}) fusion(f32[128,3072]{1,0:T(8,128)S(1)} %get-tuple-element.384, bf16[3072,768]{1,0:T(8,128)(2,1)S(1)} %bitcast.363, bf16[1,128,768]{2,1,0:T(8,128)(2,1)S(1)} %copy-done.12), kind=kOutput, calls=%fused_computation.188 | convolution fusion | flops 632681472 | bytes 7286784 | tf_op jit(solution)/shard_map/te,de->td/dot_general | solution.py:52
  97.0 2.3 multiply_reduce_fusion.1
  99.4 1.5 convert_bitcast_fusion.4
  100.9 1.2 fusion.40
  102.1 81.8 %while.29 = (s32[]{:T(128)}, f32[6,1,128,128]{2,3,1,0:T(8,128)}, bf16[6,1,512,128]{2,3,1,0:T(8,128)(2,1)}, bf16[6,1,512,128]{2,3,1,0:T(8,128)(2,1)}, s32[6]{0:T(...) while((s32[]{:T(128)}, f32[6,1,128,128]{2,3,1,0:T(8,128)}, ...), condition=%wide.region_15.16_spmd.clone, body=%wide.region_13.15_spmd.clone.sunk | while | flops 85278464 | bytes 6430769 | solution.py:400
  105.9 1.4 constant_dynamic-slice_fusion.17
  107.3 1.5 copy.133
  112.2 1.1 fusion.165
  119.6 1.4 constant_dynamic-slice_fusion.17
  120.9 1.5 copy.133
  125.8 1.1 fusion.165
  133.2 1.4 constant_dynamic-slice_fusion.17
  134.6 1.5 copy.133
  139.4 1.1 fusion.165
  146.8 1.4 constant_dynamic-slice_fusion.17
  148.2 1.5 copy.133
  153.0 1.1 fusion.165
  160.4 1.4 constant_dynamic-slice_fusion.17
  161.8 1.5 copy.133
  174.1 1.4 constant_dynamic-slice_fusion.17
  175.4 1.5 copy.133
  183.8 2.6 pad_maximum_fusion
  186.5 8.3 %copy.126 = bf16[1,512,1536]{2,0,1:T(2,128)(2,1)} copy(bf16[1,512,1536]{1,2,0:T(8,128)(2,1)} %pad_maximum_fusion) | data formatting | bytes 3145728
  194.8 3.4 copy.131
  198.2 2.3 copy.120
  200.5 1.7 copy.125
  202.3 4.9 convolution_convert_fusion.1
  207.2 6.7 %copy.103 = bf16[768,3072]{0,1:T(8,128)(2,1)} copy(bf16[768,3072]{1,0:T(8,128)(2,1)} %convolution_convert_fusion.1) | data formatting | bytes 9437184 | tf_op jit(solution)/shard_map/convert_element_type | solution.py:436
  213.9 6.6 %copy.104 = bf16[768,2,1536]{2,0,1:T(8,128)(2,1)} copy(bf16[768,2,1536]{0,2,1:T(8,128)(2,1)} %bitcast.326) | data formatting | bytes 9437184 | tf_op jit(solution)/shard_map/convert_element_type | solution.py:436
  220.5 4.8 convolution_convert_fusion.3
  225.3 6.6 %copy.122 = bf16[1,2,768,1536]{3,2,1,0:T(8,128)(2,1)} copy(bf16[1,2,768,1536]{2,3,1,0:T(8,128)(2,1)} %bitcast.327) | data formatting | bytes 9437184 | tf_op jit(solution)/shard_map/convert_element_type | solution.py:436
  231.9 1.9 bitcast_reduce_fusion
  233.9 2.5 fusion.36
  237.1 6.5 %fusion.41 = bf16[1,128,768]{2,1,0:T(8,128)(2,1)} fusion(f32[128,768]{1,0:T(8,128)S(1)} %copy-done.3, bf16[3072,768]{1,0:T(8,128)(2,1)} %param.36, f32[128,3072]{1,0:T(8,128)S(1)} %copy-done.38, f32[768]{0:T(1024)S(1)} %copy-done.33), kind=kOutput, calls=%fused_computation.94 | convolution fusion | flops 629833728 | bytes 6884352 | tf_op jit(solution)/shard_map/dot_general | solution.py:342
  243.6 2.3 reshape_bitcast_fusion
  245.9 2.9 copy.127
  248.8 1.7 convert_reduce_fusion.2
  250.5 3.9 fusion.57
  254.5 1.2 fusion.12
  255.7 10.6 %maximum_maximum_fusion.parts = bf16[3,2,768,1536]{3,2,1,0:T(8,128)(2,1)} fusion(bf16[1,2,768,384]{3,2,1,0:T(8,128)(2,1)S(1)} %copy-done.6, bf16[1,2,768,1152]{3,2,1,0:T(8,128)(2,1)S(1)} %fusion.12, bf16[1,2,768,1536]{3,2,1,0:T(8,128)(2,1)} %bitcast.325, bf16[1,2,768,1536]{3,2,1,0:T(8,128)(2,1)} %copy.122), kind=kLoop, calls=%fused_computation.34 | loop fusion | flops 56623104 | bytes 28311552 | tf_op jit(solution)/shard_map/stack | solution.py:436
  266.3 81.9 %shard_map.280 = bf16[3,2,768,1536]{3,2,1,0:T(8,128)(2,1)} custom-call(bf16[3,2,768,1536]{3,2,1,0:T(8,128)(2,1)} %maximum_maximum_fusion.parts), custom_call_target="tpu_custom_call" | custom-call | tf_op jit(solution)/shard_map/pallas_call | solution.py:226
  348.2 1.4 convert_bitcast_fusion.2
  349.6 5.4 %convert_bitcast_fusion.1 = f32[768,2,1152]{2,0,1:T(8,128)} fusion(bf16[3,2,768,1536]{3,2,1,0:T(8,128)(2,1)} %shard_map.280), kind=kLoop, calls=%fused_computation.36 | loop fusion | flops 1769472 | bytes 10616832 | tf_op jit(solution)/shard_map/convert_element_type | solution.py:442
  355.0 13.3 %slice_convert_fusion = (f32[1,2,768,1536]{3,2,1,0:T(8,128)}, f32[768,2,1536]{2,0,1:T(8,128)}) fusion(bf16[3,2,768,1536]{3,2,1,0:T(8,128)(2,1)} %shard_map.280), kind=kLoop, calls=%fused_computation.38 | loop fusion | flops 4718592 | bytes 28311552 | tf_op jit(solution)/shard_map/convert_element_type | solution.py:439
  369.5 2.0 copy.110
  371.5 3.0 copy.114
  374.5 8.0 %copy.109 = f32[768,2,1152]{0,2,1:T(8,128)} copy(f32[768,2,1152]{2,0,1:T(8,128)} %convert_bitcast_fusion.1) | data formatting | bytes 14155776 | tf_op jit(solution)/shard_map/convert_element_type | solution.py:442
  382.6 8.0 %copy.113 = f32[768,2304]{1,0:T(8,128)} copy(f32[768,2304]{0,1:T(8,128)} %bitcast.324) | data formatting | bytes 14155776
  390.5 12.1 %reshape.624 = f32[2,768,2,768]{3,2,1,0:T(2,128)} reshape(f32[1,2,768,1536]{3,2,1,0:T(8,128)} %get-tuple-element.370) | data formatting | bytes 18874368 | tf_op jit(solution)/shard_map/convert_element_type | solution.py:439
  402.7 8.3 %copy.112 = f32[2,2,768,768]{3,2,1,0:T(8,128)} copy(f32[2,2,768,768]{3,1,2,0:T(2,128)} %bitcast.320) | data formatting | bytes 18874368 | tf_op jit(solution)/shard_map/convert_element_type | solution.py:439
  411.0 9.6 %copy.111 = f32[768,2,1536]{0,2,1:T(8,128)} copy(f32[768,2,1536]{2,0,1:T(8,128)} %get-tuple-element.371) | data formatting | bytes 18874368 | tf_op jit(solution)/shard_map/convert_element_type | solution.py:441
  420.6 9.8 %copy.115 = f32[768,3072]{1,0:T(8,128)} copy(f32[768,3072]{0,1:T(8,128)} %bitcast.321) | data formatting | bytes 18874368
  430.4 2.7 fusion.101
  433.1 63.8 %all-reduce = (f32[768]{0:T(1024)}, f32[768]{0:T(1024)}, f32[768]{0:T(1024)}, f32[768]{0:T(1024)}, f32[768]{0:T(1024)}, /*index=5*/f32[768]{0:T(1024)}, f32[768]{0:T(1024)}, f32[3072]{0:T(1024)}, f32[768]{0:T(1024)}) all-reduce(f32[768]{0:T(1024)} %get-tuple-element.303, ...), channel_id=1, replica_groups=mesh['rows'=32,'seq'=4] {'rows','seq'}, use_global_device_ids=true, to_apply=%region_20.21 | all-reduce | flops 9216 | bytes 73728 | tf_op jit(solution)/shard_map/psum | solution.py:444
  (282 shorter events, 83.1 us)
Async XLA Ops:
  7.2 4.1 copy-start
  7.2 236.4 %reduce-scatter.4.cloned.1.call-start = ((), (), s32[]{:S(2)}) async-start(), calls=%async_computation.1 | async-start | bytes 1966080
  9.3 3.6 copy-start.25
  10.5 2.4 copy-start.27
  11.2 2.4 copy-start.29
  11.3 2.4 copy-start.30
  46.2 35.5 %copy-start.31 = (f32[768]{0:T(1024)S(1)}, f32[768]{0:T(1024)}, u32[]{:S(2)}) copy-start(f32[768]{0:T(1024)} %param.31) | copy-start | bytes 9220
  81.7 2.2 copy-start.14
  81.7 2.2 copy-start.15
  81.7 2.2 copy-start.32
  81.7 9.8 %slice-start.2 = ((s8[4718592]{0:T(1024)(128)(4,1)}), s8[4194304]{0:T(1024)(128)(4,1)S(1)}, s32[]{:S(2)}) async-start(s8[4718592]{0:T(1024)(128)(4,1)} %bitcast.362), calls=%async_computation.4 | async-start | bytes 8388608
  83.6 15.7 %copy-start.2 = (f32[128,768]{1,0:T(8,128)}, f32[128,768]{1,0:T(8,128)S(1)}, u32[]{:S(2)}) copy-start(f32[128,768]{1,0:T(8,128)S(1)} %get-tuple-element.378) | copy-start | bytes 1179652
  83.7 15.7 %copy-start.21 = (f32[128]{0:T(128)}, f32[128]{0:T(128)S(1)}, u32[]{:S(2)}) copy-start(f32[128]{0:T(128)S(1)} %broadcast_multiply_fusion.4) | copy-start | bytes 1540
  83.9 15.5 %copy-start.23 = (f32[128]{0:T(128)}, f32[128]{0:T(128)S(1)}, u32[]{:S(2)}) copy-start(f32[128]{0:T(128)S(1)} %add_rsqrt_fusion) | copy-start | bytes 1540
  83.9 7.6 %copy-start.12 = (bf16[1,128,768]{2,1,0:T(8,128)(2,1)S(1)}, bf16[1,128,768]{2,1,0:T(8,128)(2,1)}, u32[]{:S(2)}) copy-start(bf16[1,128,768]{2,1,0:T(8,128)(2,1)} %param.22) | copy-start | bytes 589828
  83.9 7.6 %slice-start.3 = ((s8[4718592]{0:T(1024)(128)(4,1)}), s8[524288]{0:T(1024)(128)(4,1)S(1)}, s32[]{:S(2)}) async-start(s8[4718592]{0:T(1024)(128)(4,1)} %bitcast.362), calls=%async_computation.5 | async-start | bytes 1048576
  83.9 13.1 %slice-start = ((s8[4718592]{0:T(1024)(128)(4,1)}), s8[4194304]{0:T(1024)(128)(4,1)S(1)}, s32[]{:S(2)}) async-start(s8[4718592]{0:T(1024)(128)(4,1)} %bitcast.341), calls=%async_computation.2 | async-start | bytes 8388608
  91.5 5.5 %copy-start.37 = (f32[128,3072]{1,0:T(8,128)}, f32[128,3072]{1,0:T(8,128)S(1)}, u32[]{:S(2)}) copy-start(f32[128,3072]{1,0:T(8,128)S(1)} %get-tuple-element.384) | copy-start | bytes 4718596
  91.5 5.5 %slice-start.1 = ((s8[4718592]{0:T(1024)(128)(4,1)}), s8[524288]{0:T(1024)(128)(4,1)S(1)}, s32[]{:S(2)}) async-start(s8[4718592]{0:T(1024)(128)(4,1)} %bitcast.341), calls=%async_computation.3 | async-start | bytes 1048576
  97.0 2.3 copy-start.9
  99.4 1.5 copy-start.7
  100.9 1.2 copy-start.8
  102.1 3.2 copy-start.34
  112.1 1.6 copy-start.4
  113.7 2.1 copy-start.35
  115.7 3.2 copy-start.34
  125.8 1.6 copy-start.4
  127.3 2.1 copy-start.35
  129.4 3.2 copy-start.34
  139.4 1.6 copy-start.4
  140.9 2.1 copy-start.35
  143.0 3.2 copy-start.34
  153.0 1.6 copy-start.4
  154.5 2.0 copy-start.35
  156.6 3.2 copy-start.34
  166.6 1.6 copy-start.4
  168.1 2.1 copy-start.35
  170.2 3.2 copy-start.34
  180.3 1.6 copy-start.4
  181.8 2.1 copy-start.35
  198.2 4.1 copy-start.22
  198.2 4.1 copy-start.24
  231.9 4.4 copy-start.11
  231.9 5.1 %copy-start.3 = (f32[128,768]{1,0:T(8,128)S(1)}, f32[128,768]{1,0:T(8,128)}, u32[]{:S(2)}) copy-start(f32[128,768]{1,0:T(8,128)} %copy-done.2) | copy-start | bytes 1179652
  231.9 5.1 %copy-start.33 = (f32[768]{0:T(1024)S(1)}, f32[768]{0:T(1024)}, u32[]{:S(2)}) copy-start(f32[768]{0:T(1024)} %param.37) | copy-start | bytes 9220
  231.9 5.1 %copy-start.38 = (f32[128,3072]{1,0:T(8,128)S(1)}, f32[128,3072]{1,0:T(8,128)}, u32[]{:S(2)}) copy-start(f32[128,3072]{1,0:T(8,128)} %copy-done.37) | copy-start | bytes 4718596
  243.6 6.9 %copy-start.16 = (f32[768]{0:T(1024)S(1)}, f32[768]{0:T(1024)}, u32[]{:S(2)}) copy-start(f32[768]{0:T(1024)} %param.25) | copy-start | bytes 9220
  243.6 6.9 %copy-start.26 = (f32[128]{0:T(128)S(1)}, f32[128]{0:T(128)}, u32[]{:S(2)}) copy-start(f32[128]{0:T(128)} %copy-done.25) | copy-start | bytes 1540
  243.6 6.9 %copy-start.28 = (f32[128]{0:T(128)S(1)}, f32[128]{0:T(128)}, u32[]{:S(2)}) copy-start(f32[128]{0:T(128)} %copy-done.27) | copy-start | bytes 1540
  250.5 3.9 copy-start.10
  250.5 3.9 copy-start.13
  250.5 4.0 copy-start.5
  250.5 4.0 copy-start.20
  254.5 1.3 copy-start.6
  355.0 13.3 %copy-start.36 = (f32[128]{0:T(128)S(1)}, f32[128]{0:T(128)}, u32[]{:S(2)}) copy-start(f32[128]{0:T(128)} %get-tuple-element.304) | copy-start | bytes 1540
  420.6 12.5 %copy-start.17 = (f32[768]{0:T(1024)S(1)}, f32[768]{0:T(1024)}, u32[]{:S(2)}) copy-start(f32[768]{0:T(1024)} %get-tuple-element.301) | copy-start | bytes 9220
  420.6 12.5 %copy-start.18 = (f32[768]{0:T(1024)S(1)}, f32[768]{0:T(1024)}, u32[]{:S(2)}) copy-start(f32[768]{0:T(1024)} %get-tuple-element.307) | copy-start | bytes 9220
  420.6 12.5 %copy-start.19 = (f32[768]{0:T(1024)S(1)}, f32[768]{0:T(1024)}, u32[]{:S(2)}) copy-start(f32[768]{0:T(1024)} %get-tuple-element.376) | copy-start | bytes 9220
  420.6 76.3 %copy-start.1 = (bf16[768,2304]{1,0:T(8,128)(2,1)S(1)}, bf16[768,2304]{1,0:T(8,128)(2,1)}, u32[]{:S(2)}) copy-start(bf16[768,2304]{1,0:T(8,128)(2,1)} %param.27) | copy-start | bytes 10616836
Sparse Core Ops, SparseCore 0:
  198.3 35.1 reduce-scatter.3

commit v2 on v0

v2 whole, which is shorter than its diff:
```python
from types import SimpleNamespace

import jax
import jax.numpy as jnp
from jax import lax
from jax.experimental import pallas as pl
from jax.experimental.pallas import tpu as pltpu
from jax.sharding import PartitionSpec as P

MESH = pl.DeviceIdType.MESH
BF, F32 = jnp.bfloat16, jnp.float32
WIDTH = 768
HIDDEN = 3072
HALF = HIDDEN // 2
TOK = 128
LEN = 512
PAIRS = 6
SCALE = 64**-0.5
EPSILON = 1e-6

DIMS = 6
SETS = 3
STEPS = 10

TAIL = (
    0.14361835615286447,
    0.14366105191010822,
    0.12424683572786965,
    0.09467827005043768,
    0.003990377379362003,
    0.09912410558005538,
    -0.21460327937017376,
    0.13425173188400444,
    -0.02896737861797067,
)
DENSITY = 0.3989422804014327


def rows_of(start, size):
    return pl.ds(pl.multiple_of(start, size), size)


def dot(a, b):
    return lax.dot_general(a, b, (((1,), (0,)), ((), ())), preferred_element_type=F32)


def dot_rt(a, b):
    return lax.dot_general(a, b, (((1,), (1,)), ((), ())), preferred_element_type=F32)


def dot_lt(a, b):
    return lax.dot_general(a, b, (((0,), (0,)), ((), ())), preferred_element_type=F32)


def place():
    row, seq = lax.axis_index("rows"), lax.axis_index("seq")
    x, y, z_lo = row % 4, (row // 4) % 4, row // 16
    z_hi, core = seq // 2, seq % 2
    z = z_hi * 2 + z_lo

    def device(x, y, z, core):
        return ((z % 2) * 16 + y * 4 + x, (z // 2) * 2 + core)

    near = lambda v: v + 1 - 2 * (v % 2)
    far = lambda v: 3 - v
    first = lambda v: (v % 2 + v // 2) % 2
    return SimpleNamespace(
        seq=seq,
        core=core,
        chip=z_hi,
        partners=(
            device(near(x), y, z, core),
            device(far(x), y, z, core),
            device(x, near(y), z, core),
            device(x, far(y), z, core),
            device(x, y, near(z), core),
            device(x, y, far(z), core),
        ),
        bits=(first(x), x // 2, first(y), y // 2, first(z), z // 2),
        sibling=(row, z_hi * 2 + 1 - core),
        across=(row, (1 - z_hi) * 2 + core),
    )


class Exchange:
    def __init__(self, at, grads, whole, landing, send_sem, recv_sem):
        self.at = at
        self.grads, self.whole, self.landing = grads, whole, landing
        self.send_sem, self.recv_sem = send_sem, recv_sem
        self.copies = {}

    def dim(self, k, s):
        return (k + s) % DIMS

    def rows(self, k, s):
        low = TOK * k
        for t in range(min(s, 3)):
            low = low + self.at.bits[self.dim(k, t)] * (64 >> t)
        return low

    def block(self, w, k, s, mine, whole=False):
        held = self.whole.at[w, self.at.core] if whole else self.grads.at[w]
        bit = self.at.bits[self.dim(k, s)]
        pick = bit if mine else 1 - bit
        if s < 3:
            size = 64 >> s
            return held.at[pl.ds(pl.multiple_of(self.rows(k, s) + pick * size, 16), size)]
        return held.at[
            pl.ds(pl.multiple_of(self.rows(k, 3), 16), 16),
            pl.ds(pl.multiple_of(pick * WIDTH, 128), WIDTH),
        ]

    def slot(self, w, k, s):
        if s < 3:
            return self.landing.at[w, k, pl.ds((0, 64, 96)[s], 64 >> s)]
        return self.landing.at[
            w, k, pl.ds((112, 112, 128)[s - 3], 16), pl.ds((0, WIDTH, 0)[s - 3], WIDTH)
        ]

    def send(self, w, k, s, src, dst, device):
        copy = pltpu.make_async_remote_copy(
            src_ref=src,
            dst_ref=dst,
            send_sem=self.send_sem.at[w, k, s],
            recv_sem=self.recv_sem.at[w, k, s],
            device_id=device,
            device_id_type=MESH,
        )
        copy.start()
        self.copies[w, k, s] = copy

    def start(self, w, k, s):
        if s < 4:
            src, dst, d = self.block(w, k, s, False), self.slot(w, k, s), self.dim(k, s)
        elif s < 6:
            src, dst, d = self.block(w, k, 3, True), self.slot(w, k, s), self.dim(k, s)
        else:
            src = dst = self.block(w, k, 9 - s, True, True)
            d = self.dim(k, 9 - s)
        self.send(w, k, s, src, dst, self.at.partners[d])

    def over(self, w, k, part):
        half = self.block(w, k, 0, part == 0, True)
        self.send(w, k, STEPS + part, half, half, self.at.sibling)

    def finish(self, w, s):
        for k in range(DIMS):
            self.copies[w, k, s].wait()
            if s < 6:
                kept, slot = self.block(w, k, min(s, 3), True), self.slot(w, k, s)
                total = (kept[...].astype(F32) + slot[...].astype(F32)).astype(BF)
                if s < 5:
                    kept[...] = total
                else:
                    self.block(w, k, 3, True, True)[...] = total
            if s < STEPS - 1:
                self.start(w, k, s + 1)
                if s == STEPS - 2:
                    self.over(w, k, 0)
            else:
                self.over(w, k, 1)


def normalize(load, gain, shift, normed, factor, result, base):
    def step(i, carry):
        rows = rows_of(i * 16, 16)
        v = load(rows)
        c = v - jnp.mean(v, axis=1, keepdims=True)
        f = lax.rsqrt(jnp.mean(c * c, axis=1, keepdims=True) + EPSILON)
        n = c * f
        normed[rows, :] = n
        factor[rows, :] = f
        result[rows_of(base + i * 16, 16), :] = (n * gain[...] + shift[...]).astype(BF)
        return carry

    lax.fori_loop(0, TOK // 16, step, 0)


def folded(v):
    return jnp.sum(v.reshape(2, 8, WIDTH), axis=0)


def norm_back(load_grad, load_rest, gain, normed, factor, vec, where, keep):
    zero = jnp.zeros((8, WIDTH), F32)

    def step(i, carry):
        rows = rows_of(i * 16, 16)
        e, n = load_grad(rows), normed[rows, :]
        g = e * gain[...]
        a = jnp.mean(g, axis=1, keepdims=True)
        b = jnp.mean(g * n, axis=1, keepdims=True)
        back = load_rest(rows) + factor[rows, :] * (g - a - n * b)
        keep(rows, back)
        return carry[0] + folded(e * n), carry[1] + folded(e), carry[2] + folded(back)

    sums = lax.fori_loop(0, TOK // 16, step, (zero, zero, zero))
    for row, total in zip(where, sums):
        vec[row : row + 1, :] = jnp.sum(total, axis=0, keepdims=True)


def scratch():
    v = pltpu.VMEM
    dma = pltpu.SemaphoreType.DMA
    return dict(
        qkv_w=v((WIDTH, 3 * WIDTH), BF),
        proj_w=v((WIDTH, WIDTH), BF),
        up_w=v((WIDTH, HALF), BF),
        down_w=v((HALF, WIDTH), BF),
        normed_in=v((LEN, WIDTH), BF),
        queries=v((LEN, WIDTH), BF),
        keys=v((LEN, WIDTH), BF),
        values=v((LEN, WIDTH), BF),
        hat1=v((TOK, WIDTH), F32),
        fac1=v((TOK, 1), F32),
        bias=v((TOK, LEN), F32),
        probs=v((PAIRS, 2 * TOK, LEN), F32),
        attended_full=v((TOK, WIDTH), F32),
        attended=v((2 * TOK, WIDTH), BF),
        resid=v((TOK, WIDTH), F32),
        hat2=v((TOK, WIDTH), F32),
        fac2=v((TOK, 1), F32),
        mlp_in=v((2 * TOK, WIDTH), BF),
        cot2=v((2 * TOK, WIDTH), BF),
        hidden_grad=v((2 * TOK, HALF), F32),
        hidden=v((2 * TOK, HALF), BF),
        up_low=v((2 * TOK, HALF), BF),
        mlp_part=v((2 * TOK, WIDTH), F32),
        mlp_came=v((TOK, WIDTH), F32),
        out_part=v((2 * TOK, WIDTH), F32),
        out_came=v((TOK, WIDTH), F32),
        resid_grad=v((TOK, WIDTH), F32),
        resid_low=v((TOK, WIDTH), BF),
        attended_grad=v((LEN, WIDTH), BF),
        stat=v((TOK, 128), F32),
        stats=v((4, 32, 128), F32),
        qkv_low=v((TOK, 3 * WIDTH), BF),
        qkv_half=v((2 * TOK, 1152), BF),
        resid_half=v((2 * TOK, 384), BF),
        key_grad=v((TOK, WIDTH), F32),
        value_grad=v((TOK, WIDTH), F32),
        scores=v((2 * TOK, LEN), F32),
        scores2=v((2 * TOK, 256), F32),
        low1=v((2 * TOK, LEN), BF),
        low2=v((2 * TOK, 256), BF),
        pre=v((2 * TOK, 256), F32),
        up_bias_half=v((1, HALF), F32),
        vec=v((16, WIDTH), F32),
        lines=v((8, WIDTH), F32),
        vec_came=v((DIMS + 1, 16, WIDTH), F32),
        grads=v((SETS, WIDTH, HALF), BF),
        whole=v((SETS, 2, WIDTH, HALF), BF),
        landing=v((SETS, DIMS, 144, HALF), BF),
        send_sem=dma((SETS, DIMS, STEPS + 2)),
        recv_sem=dma((SETS, DIMS, STEPS + 2)),
        side_send=dma((16,)),
        side_recv=dma((16,)),
        vec_send=dma((DIMS + 1,)),
        vec_recv=dma((DIMS + 1,)),
        load_sem=dma((4,)),
        out_sem=dma((SETS, 2)),
    )


NAMES = tuple(scratch())


def kernel(
    lengths,
    order,
    x,
    cot,
    attn_gain,
    attn_shift,
    query_bias,
    value_bias,
    proj_bias,
    mlp_gain,
    mlp_shift,
    up_bias,
    down_bias,
    qkv_weight,
    proj_weight,
    up_weight,
    down_weight,
    block_output,
    input_grad,
    whole_out,
    vec_out,
    *refs,
):
    m = SimpleNamespace(**dict(zip(NAMES, refs)))
    at = place()
    core, seq = at.core, at.seq
    ex = Exchange(at, m.grads, m.whole, m.landing, m.send_sem, m.recv_sem)

    barrier = pltpu.get_barrier_semaphore()
    for device in at.partners + (at.sibling, at.across):
        pl.semaphore_signal(barrier, inc=1, device_id=device, device_id_type=MESH)

    loads = [
        pltpu.make_async_copy(src, dst, m.load_sem.at[i])
        for i, (src, dst) in enumerate(
            (
                (qkv_weight, m.qkv_w),
                (down_weight.at[rows_of(core * HALF, HALF)], m.down_w),
                (proj_weight, m.proj_w),
                (up_weight.at[:, rows_of(core * HALF, HALF)], m.up_w),
            )
        )
    ]
    for load in loads:
        load.start()

    def side(i, src, dst, device):
        copy = pltpu.make_async_remote_copy(
            src_ref=src,
            dst_ref=dst,
            send_sem=m.side_send.at[i],
            recv_sem=m.side_recv.at[i],
            device_id=device,
            device_id_type=MESH,
        )
        copy.start()
        return copy

    own = rows_of(seq * TOK, TOK)
    two = rows_of(core * TOK, TOK)
    two_other = rows_of((1 - core) * TOK, TOK)
    far_block = (1 - at.chip) * 2 + core
    far = rows_of(far_block * TOK, TOK)

    vectors = (attn_gain, attn_shift, query_bias, value_bias, proj_bias, mlp_gain, mlp_shift, down_bias)
    for i, vector in enumerate(vectors):
        m.lines[i : i + 1, :] = vector[...][None]
    attn_gain, attn_shift, query_bias, value_bias, proj_bias, mlp_gain, mlp_shift, down_bias = (
        m.lines.at[i : i + 1] for i in range(8)
    )

    normalize(
        lambda rows: x[0, rows, :].astype(F32), attn_gain, attn_shift, m.hat1, m.fac1, m.normed_in, seq * TOK
    )
    m.cot2[two, :] = cot[0]
    ends = [lengths[0, 0]]
    for i in (1, 2):
        ends.append(ends[-1] + lengths[0, i])
    segment = lambda t: sum((t >= end).astype(jnp.int32) for end in ends)
    mine = segment(lax.broadcasted_iota(jnp.int32, (TOK, TOK), 0) + order[0, seq] * TOK)
    for j in range(4):
        other = segment(lax.broadcasted_iota(jnp.int32, (TOK, TOK), 1) + order[0, j] * TOK)
        m.bias[:, j * TOK : (j + 1) * TOK] = jnp.where(mine == other, 0.0, -1e30)
    m.up_bias_half[...] = jnp.where(core == 0, up_bias[:HALF], up_bias[HALF:])[None]
    m.vec[...] = jnp.zeros((16, WIDTH), F32)
    m.vec[7:8, :] = jnp.sum(
        jnp.sum(cot[0].astype(F32).reshape(TOK // 8, 8, WIDTH), axis=0), axis=0, keepdims=True
    )
    m.stat[...] = jnp.zeros((TOK, 128), F32)
    lane = lax.broadcasted_iota(jnp.int32, (1, 128), 1)
    low_lanes = (lane < 64).astype(BF)
    high_lanes = (lane >= 64).astype(BF)

    def both(v):
        return jnp.concatenate((v * low_lanes, v * high_lanes), axis=0)

    def joined(v):
        return jnp.where(lane < 64, v[:TOK], v[TOK:])

    pl.semaphore_wait(barrier, DIMS + 2)
    in_sib = side(0, m.normed_in.at[own], m.normed_in.at[own], at.sibling)
    in_far = side(1, m.normed_in.at[own], m.normed_in.at[own], at.across)
    cot_sib = side(3, m.cot2.at[two], m.cot2.at[two], at.sibling)

    def project(base):
        rows = rows_of(base, 2 * TOK)

        def step(i, carry):
            tile = lambda part: rows_of(i * 256, 256) if part == 0 else pl.ds(
                pl.multiple_of(part * WIDTH + i * 256, 256), 256
            )
            cols = tile(0)
            a = m.normed_in[rows, :]
            m.keys[rows, cols] = dot(a, m.qkv_w[:, tile(1)]).astype(BF)
            m.values[rows, cols] = (dot(a, m.qkv_w[:, tile(2)]) + value_bias[:, cols]).astype(BF)
            m.queries[rows, cols] = ((dot(a, m.qkv_w[:, tile(0)]) + query_bias[:, cols]) * SCALE).astype(BF)
            return carry

        lax.fori_loop(0, 3, step, 0)

    loads[0].wait()
    in_sib.wait()
    project(at.chip * 2 * TOK)
    loads[1].wait()
    cot_sib.wait()

    def hidden_back(i, carry):
        cols = rows_of(i * 256, 256)
        m.hidden_grad[:, cols] = dot_rt(m.cot2[...], m.down_w[cols, :])
        return carry

    lax.fori_loop(0, HALF // 256, hidden_back, 0)
    in_far.wait()
    in_pass = side(2, m.normed_in.at[far], m.normed_in.at[far], at.sibling)
    in_pass.wait()
    project((1 - at.chip) * 2 * TOK)

    def attend(i, carry):
        cols = rows_of(i * 128, 128)
        m.scores[...] = dot_rt(both(m.queries[own, cols]), m.keys[:, cols])

        def soften(r, carry):
            rows = rows_of(r * 32, 32)
            token = rows_of((r % 4) * 32, 32)
            s = m.scores[rows, :] + m.bias[token, :]
            top = jnp.max(s, axis=1, keepdims=True)
            e = jnp.exp(s - top)
            total = jnp.sum(e, axis=1, keepdims=True)
            p = e * (1.0 / total)
            m.probs[i, rows, :] = p
            m.low1[rows, :] = p.astype(BF)
            head = 2 * i + r // 4
            m.stat[token, :] = jnp.where(lane == head, top + jnp.log(total), m.stat[token, :])
            return carry

        lax.fori_loop(0, 8, soften, 0, unroll=2)
        out = joined(dot(m.low1[...], m.values[:, cols]))
        m.attended_full[:, cols] = out
        m.attended[two, cols] = out.astype(BF)
        return carry

    lax.fori_loop(0, PAIRS, attend, 0)

    loads[2].wait()

    def project_out(i, carry):
        cols = rows_of(i * 256, 256)
        m.resid[:, cols] = (
            x[0, :, cols].astype(F32) + dot(m.attended[two, :], m.proj_w[:, cols]) + proj_bias[:, cols]
        )
        return carry

    lax.fori_loop(0, 3, project_out, 0)
    normalize(lambda rows: m.resid[rows, :], mlp_gain, mlp_shift, m.hat2, m.fac2, m.mlp_in, core * TOK)
    mlp_sib = side(4, m.mlp_in.at[two], m.mlp_in.at[two], at.sibling)
    att_sib = side(5, m.attended.at[two], m.attended.at[two], at.sibling)
    loads[3].wait()
    mlp_sib.wait()

    def feed(i, carry):
        cols = rows_of(i * 256, 256)
        m.pre[...] = dot(m.mlp_in[...], m.up_w[:, cols])

        def act(r, total):
            rows = rows_of(r * 32, 32)
            u = m.pre[rows, :] + m.up_bias_half[:, cols]
            t = 1.0 / (1.0 + 0.36 * jnp.abs(u))
            tail = jnp.full_like(t, TAIL[-1])
            for c in TAIL[-2::-1]:
                tail = tail * t + c
            e = jnp.exp(-0.5 * (u * u))
            tail = tail * (t * e)
            phi = jnp.where(u >= 0, 1.0 - tail, tail)
            m.hidden[rows, cols] = (u * phi).astype(BF)
            g = m.hidden_grad[rows, cols] * (phi + u * (DENSITY * e))
            m.up_low[rows, cols] = g.astype(BF)
            return total + jnp.sum(g.reshape(4, 8, 256), axis=0)

        total = lax.fori_loop(0, 8, act, jnp.zeros((8, 256), F32), unroll=2)
        m.up_bias_half[:, cols] = jnp.sum(total, axis=0, keepdims=True)
        return carry

    lax.fori_loop(0, HALF // 256, feed, 0)
    for k in range(DIMS):
        for h in range(2):
            first = h * WIDTH + k * TOK
            m.grads[0, k * TOK : (k + 1) * TOK, h * WIDTH : (h + 1) * WIDTH] = dot_lt(
                m.hidden[:, first : first + TOK], m.cot2[...]
            ).astype(BF)
        ex.start(0, k, 0)
    for k in range(DIMS):
        m.grads[1, k * TOK : (k + 1) * TOK, :] = dot_lt(
            m.mlp_in[:, k * TOK : (k + 1) * TOK], m.up_low[...]
        ).astype(BF)
        ex.start(1, k, 0)
    for h in range(2):
        for t in range(2):
            m.vec[8 + 2 * h + t : 9 + 2 * h + t, :] = jnp.where(
                core == h, m.up_bias_half[:, t * WIDTH : (t + 1) * WIDTH], 0.0
            )

    def mlp_back(i, carry):
        cols = rows_of(i * 256, 256)
        m.mlp_part[:, cols] = dot_rt(m.up_low[...], m.up_w[cols, :])
        return carry

    lax.fori_loop(0, 3, mlp_back, 0)
    part_sib = side(6, m.mlp_part.at[two_other], m.mlp_came, at.sibling)

    def feed_out(i, carry):
        cols = rows_of(i * 256, 256)
        m.out_part[:, cols] = dot(m.hidden[...], m.down_w[:, cols])
        return carry

    lax.fori_loop(0, 3, feed_out, 0)
    out_sib = side(7, m.out_part.at[two_other], m.out_came, at.sibling)
    part_sib.wait()

    def keep_resid(rows, back):
        m.resid_grad[rows, :] = back
        m.resid_low[rows, :] = back.astype(BF)

    norm_back(
        lambda rows: m.mlp_part[rows_of_shift(rows, core * TOK), :] + m.mlp_came[rows, :],
        lambda rows: cot[0, rows, :].astype(F32),
        mlp_gain,
        m.hat2,
        m.fac2,
        m.vec,
        (5, 6, 4),
        keep_resid,
    )

    def attended_back(i, carry):
        cols = rows_of(i * 256, 256)
        m.attended_grad[own, cols] = dot_rt(m.resid_low[...], m.proj_w[cols, :]).astype(BF)
        return carry

    lax.fori_loop(0, 3, attended_back, 0)
    grad_sib = side(8, m.attended_grad.at[own], m.attended_grad.at[own], at.sibling)
    grad_far = side(9, m.attended_grad.at[own], m.attended_grad.at[own], at.across)

    def means(i, carry):
        cols = rows_of(i * 128, 128)
        v = m.attended_grad[own, cols].astype(F32) * m.attended_full[:, cols]
        a = jnp.sum(jnp.where(lane < 64, v, 0.0), axis=1, keepdims=True)
        b = jnp.sum(jnp.where(lane < 64, 0.0, v), axis=1, keepdims=True)
        m.stat[...] = jnp.where(
            lane == 16 + 2 * i, a, jnp.where(lane == 17 + 2 * i, b, m.stat[...])
        )
        return carry

    lax.fori_loop(0, PAIRS, means, 0)
    m.stats[seq] = jnp.transpose(m.stat[...])[:32]
    stat_sib = side(11, m.stats.at[seq], m.stats.at[seq], at.sibling)
    stat_far = side(12, m.stats.at[seq], m.stats.at[seq], at.across)
    half = lambda c, size: pl.ds(pl.multiple_of(c * size, 128), size)
    m.resid_half[two, :] = m.resid_low[:, half(core, 384)]
    resid_sib = side(14, m.resid_low.at[:, half(1 - core, 384)], m.resid_half.at[two], at.sibling)

    ex.finish(0, 0)

    def query_side(i, carry):
        cols = rows_of(i * 128, 128)
        m.scores[...] = dot_rt(both(m.attended_grad[own, cols]), m.values[:, cols])

        def back(r, carry):
            rows = rows_of(r * 32, 32)
            head = 16 + 2 * i + r // 4
            stat = m.stat[rows_of((r % 4) * 32, 32), :]
            mean = jnp.sum(jnp.where(lane == head, stat, 0.0), axis=1, keepdims=True)
            m.low1[rows, :] = (m.probs[i, rows, :] * (m.scores[rows, :] - mean)).astype(BF)
            return carry

        lax.fori_loop(0, 8, back, 0, unroll=2)
        g = joined(dot(m.low1[...], m.keys[:, cols])) * SCALE
        m.vec[2:3, cols] = jnp.sum(g, axis=0, keepdims=True)
        m.qkv_low[:, cols] = g.astype(BF)
        return carry

    lax.fori_loop(0, PAIRS, query_side, 0)
    ex.finish(1, 0)

    def key_side(chip, first):
        rows_q = rows_of(chip * 256, 256)

        def step(i, carry):
            cols = rows_of(i * 128, 128)
            q, g = m.queries[rows_q, cols], m.attended_grad[rows_q, cols]
            m.scores[:, :256] = dot_rt(both(m.keys[own, cols]), q)
            m.scores2[...] = dot_rt(both(m.values[own, cols]), g)

            def back(r, carry):
                rows = rows_of(r * 32, 32)
                head = 2 * i + r // 4
                line = lambda h: jnp.concatenate(
                    (m.stats[chip * 2, pl.ds(h, 1), :], m.stats[chip * 2 + 1, pl.ds(h, 1), :]), axis=1
                )
                bias = m.bias[rows_of((r % 4) * 32, 32), rows_q]
                p = jnp.exp(m.scores[rows, :256] + bias - line(head))
                m.low1[rows, :256] = p.astype(BF)
                m.low2[rows, :] = (p * (m.scores2[rows, :] - line(16 + head))).astype(BF)
                return carry

            lax.fori_loop(0, 8, back, 0, unroll=2)
            dv = joined(dot(m.low1[:, :256], g))
            dk = joined(dot(m.low2[...], q))
            if first:
                m.value_grad[:, cols] = dv
                m.key_grad[:, cols] = dk
            else:
                dv = dv + m.value_grad[:, cols]
                dk = dk + m.key_grad[:, cols]
                m.vec[3:4, cols] = jnp.sum(dv, axis=0, keepdims=True)
                m.qkv_low[:, pl.ds(pl.multiple_of(WIDTH + i * 128, 128), 128)] = dk.astype(BF)
                m.qkv_low[:, pl.ds(pl.multiple_of(2 * WIDTH + i * 128, 128), 128)] = dv.astype(BF)
            return carry

        lax.fori_loop(0, PAIRS, step, 0)

    grad_sib.wait()
    stat_sib.wait()
    key_side(at.chip, True)
    ex.finish(0, 1)
    ex.finish(1, 1)

    grad_far.wait()
    grad_pass = side(10, m.attended_grad.at[far], m.attended_grad.at[far], at.sibling)
    stat_far.wait()
    stat_pass = side(13, m.stats.at[far_block], m.stats.at[far_block], at.sibling)
    ex.finish(0, 2)
    grad_pass.wait()
    stat_pass.wait()
    key_side(1 - at.chip, False)

    m.qkv_half[two, :] = m.qkv_low[:, half(core, 1152)]
    qkv_sib = side(15, m.qkv_low.at[:, half(1 - core, 1152)], m.qkv_half.at[two], at.sibling)
    ex.finish(1, 2)
    ex.finish(0, 3)

    att_sib.wait()
    resid_sib.wait()
    qkv_sib.wait()
    chip_rows = rows_of(at.chip * 2 * TOK, 2 * TOK)
    for k in range(DIMS):
        rows = slice(k * TOK, (k + 1) * TOK)
        m.grads[2, rows, :1152] = dot_lt(m.normed_in[chip_rows, rows], m.qkv_half[...]).astype(BF)
        m.grads[2, rows, 1152:] = dot_lt(m.attended[:, rows], m.resid_half[...]).astype(BF)
        ex.start(2, k, 0)

    def input_back(i, carry):
        cols = rows_of(i * 256, 256)
        m.mlp_came[:, cols] = dot_rt(m.qkv_low[...], m.qkv_w[cols, :])
        return carry

    lax.fori_loop(0, 3, input_back, 0)

    def keep_input(rows, back):
        input_grad[0, rows, :] = back.astype(BF)

    norm_back(
        lambda rows: m.mlp_came[rows, :],
        lambda rows: m.resid_grad[rows, :],
        attn_gain,
        m.hat1,
        m.fac1,
        m.vec,
        (0, 1),
        keep_input,
    )

    def vec_start(s):
        copy = pltpu.make_async_remote_copy(
            src_ref=m.vec,
            dst_ref=m.vec_came.at[s],
            send_sem=m.vec_send.at[s],
            recv_sem=m.vec_recv.at[s],
            device_id=(at.partners + (at.sibling,))[s],
            device_id_type=MESH,
        )
        copy.start()
        return copy

    vec_copy = [vec_start(0)]

    def vec_finish(s):
        vec_copy[0].wait()
        m.vec[...] = m.vec[...] + m.vec_came[s]
        if s < DIMS:
            vec_copy[0] = vec_start(s + 1)
        else:
            vec_out[...] = m.vec[...]

    ex.finish(1, 3)
    ex.finish(0, 4)
    out_sib.wait()

    def close(i, carry):
        rows = rows_of(i * 16, 16)
        block_output[0, rows, :] = (
            m.resid[rows, :]
            + (m.out_part[rows_of(core * TOK + i * 16, 16), :] + m.out_came[rows, :])
            + down_bias[...]
        ).astype(BF)
        return carry

    lax.fori_loop(0, TOK // 16, close, 0)

    events = [(1, 4), (0, 5), (2, 0), (1, 5), (0, 6), (2, 1), (1, 6), (0, 7), (2, 2), (1, 7), (0, 8), (2, 3), (1, 8)]
    events += [(2, 4), (0, 9), (2, 5), (1, 9), (2, 6), (2, 7), (2, 8), (2, 9)]
    for n, (w, s) in enumerate(events):
        ex.finish(w, s)
        if n % 2 == 0 and n // 2 <= DIMS:
            vec_finish(n // 2)

    stores = []
    for w in range(SETS):
        for k in range(DIMS):
            for part in range(2):
                ex.copies[w, k, STEPS + part].wait()
        store = pltpu.make_async_copy(m.whole.at[w], whole_out.at[w], m.out_sem.at[w, 0])
        store.start()
        stores.append(store)
    for store in stores:
        store.wait()


def rows_of_shift(rows, shift):
    return pl.ds(pl.multiple_of(rows.start + shift, 16), rows.size)


def spread_kernel(
    parts,
    vec,
    block_output_in,
    input_grad_in,
    block_output,
    input_grad,
    attn_gain,
    attn_shift,
    qkv,
    query_bias,
    value_bias,
    proj,
    proj_bias,
    mlp_gain,
    mlp_shift,
    up,
    up_bias,
    down,
    down_bias,
):
    for c in range(2):
        up[:, c * HALF : (c + 1) * HALF] = parts[1, c].astype(F32)
        qkv[:, c * 1152 : (c + 1) * 1152] = parts[2, c, :, :1152].astype(F32)
        proj[:, c * 384 : (c + 1) * 384] = parts[2, c, :, 1152:].astype(F32)
        for h in range(2):
            down[2 * c + h] = parts[0, c, :, h * WIDTH : (h + 1) * WIDTH].astype(F32)

    @pl.when(pl.program_id(0) == 0)
    def _():
        block_output[...] = block_output_in[...]
        input_grad[...] = input_grad_in[...]
        for row, ref in enumerate(
            (attn_gain, attn_shift, query_bias, value_bias, proj_bias, mlp_gain, mlp_shift, down_bias)
        ):
            ref[...] = vec[row]
        for t in range(4):
            up_bias[t * WIDTH : (t + 1) * WIDTH] = vec[8 + t]


def spread(parts, vec, block_output, input_grad):
    rows = 64
    line = lambda n: (jax.ShapeDtypeStruct((n,), F32), pl.BlockSpec((n,), lambda i: (0,)))
    flat = lambda n: (jax.ShapeDtypeStruct((WIDTH, n), F32), pl.BlockSpec((rows, n), lambda i: (i, 0)))
    tokens = (jax.ShapeDtypeStruct((1, TOK, WIDTH), BF), pl.BlockSpec((1, TOK, WIDTH), lambda i: (0, 0, 0)))
    outs = [
        tokens,
        tokens,
        line(WIDTH),
        line(WIDTH),
        flat(3 * WIDTH),
        line(WIDTH),
        line(WIDTH),
        flat(WIDTH),
        line(WIDTH),
        line(WIDTH),
        line(WIDTH),
        flat(HIDDEN),
        line(HIDDEN),
        (
            jax.ShapeDtypeStruct((4, WIDTH, WIDTH), F32),
            pl.BlockSpec((4, rows, WIDTH), lambda i: (0, i, 0)),
        ),
        line(WIDTH),
    ]
    return pl.pallas_call(
        spread_kernel,
        grid=(WIDTH // rows,),
        out_shape=[o[0] for o in outs],
        in_specs=[
            pl.BlockSpec((SETS, 2, rows, HALF), lambda i: (0, 0, i, 0)),
            pl.BlockSpec((16, WIDTH), lambda i: (0, 0)),
            tokens[1],
            tokens[1],
        ],
        out_specs=[o[1] for o in outs],
        compiler_params=pltpu.CompilerParams(vmem_limit_bytes=VMEM_LIMIT),
    )(parts, vec, block_output, input_grad)


def body(
    block_input,
    out_cotangent,
    image_lengths,
    span_order,
    attn_gain,
    attn_shift,
    qkv_weight,
    query_bias,
    value_bias,
    proj_weight,
    proj_bias,
    mlp_gain,
    mlp_shift,
    up_weight,
    up_bias,
    down_weight,
    down_bias,
):
    vmem = pl.BlockSpec(memory_space=pltpu.VMEM)
    smem = pl.BlockSpec(memory_space=pltpu.SMEM)
    hbm = pl.BlockSpec(memory_space=pl.ANY)
    held = scratch()
    block_output, input_grad, parts, vec = pl.pallas_call(
        kernel,
        out_shape=[
            jax.ShapeDtypeStruct((1, TOK, WIDTH), BF),
            jax.ShapeDtypeStruct((1, TOK, WIDTH), BF),
            jax.ShapeDtypeStruct((SETS, 2, WIDTH, HALF), BF),
            jax.ShapeDtypeStruct((16, WIDTH), F32),
        ],
        in_specs=[smem, smem] + [vmem] * 11 + [hbm] * 4,
        out_specs=[vmem, vmem, hbm, vmem],
        scratch_shapes=[held[name] for name in NAMES],
        compiler_params=pltpu.CompilerParams(
            collective_id=0, has_side_effects=True, vmem_limit_bytes=VMEM_LIMIT
        ),
    )(
        image_lengths,
        span_order,
        block_input,
        out_cotangent,
        attn_gain,
        attn_shift,
        query_bias,
        value_bias,
        proj_bias,
        mlp_gain,
        mlp_shift,
        up_bias,
        down_bias,
        qkv_weight,
        proj_weight,
        up_weight,
        down_weight,
    )
    outs = list(spread(parts, vec, block_output, input_grad))
    outs[13] = outs[13].reshape(HIDDEN, WIDTH)
    return tuple(outs)


VMEM_LIMIT = 62 << 20


def solution(mesh):
    tokens = P("rows", "seq", None)
    return jax.shard_map(
        body,
        mesh=mesh,
        in_specs=(tokens, tokens, P("rows", None), P("rows", None)) + (P(),) * 13,
        out_specs=(tokens, tokens) + (P(),) * 13,
        check_vma=False,
    )
```

time: 514 us -> 145 us (0.28)
  waiting for transfers between devices: 178 us -> 0 us
  Pallas kernels: 0 us -> 143 us
  local copies, waits for them, and re-layouts: 112 us -> 0 us
  blocking collectives: 91.8 us -> 0 us
  matrix products: 62.3 us -> 0 us
  other arithmetic: 30.7 us -> 0 us
  loops' own time: 20.2 us -> 0 us
  between operations: 14.5 us -> 0.66 us
    psum x1 -> x0, waiting for transfers between devices: 158 us -> none  [body(): lax.psum((attn_gain_grad, attn_shift_grad, qkv_weight_grad, query_bias_gr...]
    pallas_call x0 -> x2, Pallas kernels: none -> 143 us  [the longest x1 126 us: body(): pl.pallas_call(kernel, out_shape=[jax.ShapeDtypeStruct((1, TOK, WIDTH), B...]
    psum x1 -> x0, blocking collectives: 67 us -> none  [body(): lax.psum((attn_gain_grad, attn_shift_grad, qkv_weight_grad, query_bias_gr...]
    dot_general x54 -> x0, matrix products: 62.3 us -> none  [the longest x4 18.8 us: weight_product(): jnp.einsum('td,te->de', left, right, preferred_element_type=jnp.float32)]
    dynamic_slice x54 -> x0, local copies, waits for them, and re-layouts: 50.2 us -> none  [the longest x42 43.2 us: pair_slice(): lax.dynamic_slice_in_dim(source, pair_index * pair_width, pair_width, 2)]
    unnamed x97 -> x0, local copies, waits for them, and re-layouts: 45.2 us -> none
    all_gather x2 -> x0, blocking collectives: 24.8 us -> none  [the longest x1 13.9 us: body(): lax.all_gather(keys_local, 'seq', axis=1, tiled=True)]
    another operation x2 -> x0, loops' own time: 20.2 us -> none  [the longest x1 16.1 us: body(): query_pairs, key_pairs, value_pairs = lax.map(pair_backward, pair_numbers)]
  transfers between devices with their start and end apart: 2 -> 0, of which waited for: 2 -> 0; matrix products, arithmetic and copies ran while one was open for 5% -> 0% of each run, Pallas kernels for 0% -> 0%
where the time goes in v2:
time: 145 us; the launch traced here: 144 us
  Pallas kernels  143 us (99%)
    pallas_call x1, Pallas kernels, body(): pl.pallas_call(kernel, out_shape=[jax.ShapeDtypeStruct((1, TOK, WIDTH), B...  126 us
    pallas_call x1, Pallas kernels, spread(): pl.pallas_call(spread_kernel, grid=(WIDTH // rows,), out_shape=[o[0] for...  16.4 us

profile of v2, /device:TPU:1, one launch (start us, length us, event | category | flops | bytes accessed | tf_op | source)
XLA Modules:
  0.0 143.6 jit_solution(15172406572414213002)
XLA Ops:
  0.7 126.5 %shard_map.280 = (bf16[1,128,768]{2,1,0:T(8,128)(2,1)}, bf16[1,128,768]{2,1,0:T(8,128)(2,1)}, bf16[3,2,768,1536]{3,2,1,0:T(8,128)(2,1)}, f32[16,768]{1,0:T(8,128)}) custom-call(s32[1,4]{1,0:T(1,128)} %lengths.1, s32[1,4]{1,0:T(1,128)} %order.1, bf16[1,128,768]{2,1,0:T(8,128)(2,1)} %x.1, bf16[1,128,768]{2,1,0:T(8,128)(2,1)} %cot.1, f32[768]{0:T(1024)} %attn_gain.1, ...), custom_call_target="tpu_custom_call" | custom-call | tf_op jit(solution)/shard_map/pallas_call | solution.py:822
  127.2 16.4 %shard_map.281 = (bf16[1,128,768]{2,1,0:T(8,128)(2,1)}, bf16[1,128,768]{2,1,0:T(8,128)(2,1)}, f32[768]{0:T(1024)}, f32[768]{0:T(1024)}, f32[768,2304]{1,0:T(8,12...) custom-call(bf16[3,2,768,1536]{3,2,1,0:T(8,128)(2,1)} %get-tuple-ele, ...), custom_call_target="tpu_custom_call" | custom-call | tf_op jit(solution)/shard_map/pallas_call | solution.py:784

commit v3 on v2

v3 whole, which is shorter than its diff:
```python
from types import SimpleNamespace

import jax
import jax.numpy as jnp
from jax import lax
from jax.experimental import pallas as pl
from jax.experimental.pallas import tpu as pltpu
from jax.sharding import PartitionSpec as P

MESH = pl.DeviceIdType.MESH
BF, F32 = jnp.bfloat16, jnp.float32
WIDTH = 768
HIDDEN = 3072
HALF = HIDDEN // 2
TOK = 128
LEN = 512
PAIRS = 6
SCALE = 64**-0.5
EPSILON = 1e-6

DIMS = 6
STEPS = 10
DOWN, UP, PROJ, KEYS = range(4)
WIDTHS = (HALF, HALF, WIDTH, WIDTH)

TAIL = (
    0.14361835615286447,
    0.14366105191010822,
    0.12424683572786965,
    0.09467827005043768,
    0.003990377379362003,
    0.09912410558005538,
    -0.21460327937017376,
    0.13425173188400444,
    -0.02896737861797067,
)
DENSITY = 0.3989422804014327


def rows_of(start, size):
    return pl.ds(pl.multiple_of(start, size), size)


def dot(a, b):
    return lax.dot_general(a, b, (((1,), (0,)), ((), ())), preferred_element_type=F32)


def dot_rt(a, b):
    return lax.dot_general(a, b, (((1,), (1,)), ((), ())), preferred_element_type=F32)


def dot_lt(a, b):
    return lax.dot_general(a, b, (((0,), (0,)), ((), ())), preferred_element_type=F32)


def place():
    row, seq = lax.axis_index("rows"), lax.axis_index("seq")
    x, y, z_lo = row % 4, (row // 4) % 4, row // 16
    z_hi, core = seq // 2, seq % 2
    z = z_hi * 2 + z_lo

    def device(x, y, z, core):
        return ((z % 2) * 16 + y * 4 + x, (z // 2) * 2 + core)

    near = lambda v: v + 1 - 2 * (v % 2)
    far = lambda v: 3 - v
    first = lambda v: (v % 2 + v // 2) % 2
    return SimpleNamespace(
        seq=seq,
        core=core,
        chip=z_hi,
        partners=(
            device(near(x), y, z, core),
            device(far(x), y, z, core),
            device(x, near(y), z, core),
            device(x, far(y), z, core),
            device(x, y, near(z), core),
            device(x, y, far(z), core),
        ),
        bits=(first(x), x // 2, first(y), y // 2, first(z), z // 2),
        sibling=(row, z_hi * 2 + 1 - core),
        across=(row, (1 - z_hi) * 2 + core),
    )


class Exchange:
    def __init__(self, at, grads, whole, landing, send_sem, recv_sem):
        self.at = at
        self.grads, self.whole, self.landing = grads, whole, landing
        self.send_sem, self.recv_sem = send_sem, recv_sem
        self.copies = {}

    def dim(self, k, s):
        return (k + s) % DIMS

    def rows(self, k, s):
        low = TOK * k
        for t in range(min(s, 3)):
            low = low + self.at.bits[self.dim(k, t)] * (64 >> t)
        return low

    def block(self, w, k, s, mine, whole=False):
        held = self.whole[w].at[self.at.core] if whole else self.grads[w]
        bit = self.at.bits[self.dim(k, s)]
        pick = bit if mine else 1 - bit
        if s < 3:
            size = 64 >> s
            return held.at[pl.ds(pl.multiple_of(self.rows(k, s) + pick * size, 16), size)]
        width = WIDTHS[w] // 2
        return held.at[
            pl.ds(pl.multiple_of(self.rows(k, 3), 16), 16),
            pl.ds(pl.multiple_of(pick * width, 128), width),
        ]

    def slot(self, w, k, s):
        if s < 3:
            return self.landing[w].at[k, pl.ds((0, 64, 96)[s], 64 >> s)]
        width = WIDTHS[w] // 2
        return self.landing[w].at[k, pl.ds((112, 112, 128)[s - 3], 16), pl.ds((0, width, 0)[s - 3], width)]

    def send(self, w, k, s, src, dst, device):
        copy = pltpu.make_async_remote_copy(
            src_ref=src,
            dst_ref=dst,
            send_sem=self.send_sem.at[w, k, s],
            recv_sem=self.recv_sem.at[w, k, s],
            device_id=device,
            device_id_type=MESH,
        )
        copy.start()
        self.copies[w, k, s] = copy

    def start(self, w, k, s=0):
        if s < 4:
            src, dst, d = self.block(w, k, s, False), self.slot(w, k, s), self.dim(k, s)
        elif s < 6:
            src, dst, d = self.block(w, k, 3, True), self.slot(w, k, s), self.dim(k, s)
        else:
            src = dst = self.block(w, k, 9 - s, True, True)
            d = self.dim(k, 9 - s)
        self.send(w, k, s, src, dst, self.at.partners[d])

    def over(self, w, k, part):
        half = self.block(w, k, 0, part == 0, True)
        self.send(w, k, STEPS + part, half, half, self.at.sibling)

    def finish(self, w, s):
        for k in range(DIMS):
            self.copies[w, k, s].wait()
            if s < 6:
                kept, slot = self.block(w, k, min(s, 3), True), self.slot(w, k, s)
                total = (kept[...].astype(F32) + slot[...].astype(F32)).astype(BF)
                if s < 5:
                    kept[...] = total
                else:
                    self.block(w, k, 3, True, True)[...] = total
            if s < STEPS - 1:
                self.start(w, k, s + 1)
                if s == STEPS - 2:
                    self.over(w, k, 0)
            else:
                self.over(w, k, 1)


def normalize(load, gain, shift, normed, factor, result, base):
    def step(i, carry):
        rows = rows_of(i * 16, 16)
        v = load(rows)
        c = v - jnp.mean(v, axis=1, keepdims=True)
        f = lax.rsqrt(jnp.mean(c * c, axis=1, keepdims=True) + EPSILON)
        n = c * f
        normed[rows, :] = n
        factor[rows, :] = f
        result[rows_of(base + i * 16, 16), :] = (n * gain[...] + shift[...]).astype(BF)
        return carry

    lax.fori_loop(0, TOK // 16, step, 0, unroll=True)


def folded(v):
    return jnp.sum(v.reshape(2, 8, WIDTH), axis=0)


def norm_back(load_grad, load_rest, gain, normed, factor, vec, where, keep):
    zero = jnp.zeros((8, WIDTH), F32)

    def step(i, carry):
        rows = rows_of(i * 16, 16)
        e, n = load_grad(rows), normed[rows, :]
        g = e * gain[...]
        a = jnp.mean(g, axis=1, keepdims=True)
        b = jnp.mean(g * n, axis=1, keepdims=True)
        back = load_rest(rows) + factor[rows, :] * (g - a - n * b)
        keep(rows, back)
        return carry[0] + folded(e * n), carry[1] + folded(e), carry[2] + folded(back)

    sums = lax.fori_loop(0, TOK // 16, step, (zero, zero, zero), unroll=True)
    for row, total in zip(where, sums):
        vec[row : row + 1, :] = jnp.sum(total, axis=0, keepdims=True)


def scratch():
    v = pltpu.VMEM
    dma = pltpu.SemaphoreType.DMA
    sets = len(WIDTHS)
    return dict(
        qkv_w=v((WIDTH, 3 * WIDTH), BF),
        proj_w=v((WIDTH, WIDTH), BF),
        up_w=v((WIDTH, HALF), BF),
        down_w=v((HALF, WIDTH), BF),
        lines=v((8, WIDTH), F32),
        up_bias_half=v((1, HALF), F32),
        normed_in=v((LEN, WIDTH), BF),
        queries=v((LEN, WIDTH), BF),
        keys=v((LEN, WIDTH), BF),
        values=v((LEN, WIDTH), BF),
        key_ext=v((LEN, 128), BF),
        query_ext=v((LEN, 128), BF),
        stat=v((TOK, 128), F32),
        hat1=v((TOK, WIDTH), F32),
        fac1=v((TOK, 1), F32),
        attended_full=v((TOK, WIDTH), F32),
        attended=v((2 * TOK, WIDTH), BF),
        resid=v((TOK, WIDTH), F32),
        hat2=v((TOK, WIDTH), F32),
        fac2=v((TOK, 1), F32),
        mlp_in=v((2 * TOK, WIDTH), BF),
        cot2=v((2 * TOK, WIDTH), BF),
        hidden_grad=v((2 * TOK, HALF), F32),
        hidden=v((2 * TOK, HALF), BF),
        up_low=v((2 * TOK, HALF), BF),
        mlp_part=v((2 * TOK, WIDTH), F32),
        mlp_came=v((TOK, WIDTH), F32),
        out_part=v((2 * TOK, WIDTH), F32),
        out_came=v((TOK, WIDTH), F32),
        resid_grad=v((TOK, WIDTH), F32),
        resid_low=v((TOK, WIDTH), BF),
        attended_grad=v((LEN, WIDTH), BF),
        qkv_low=v((TOK, 3 * WIDTH), BF),
        resid_half=v((2 * TOK, 384), BF),
        query_half=v((2 * TOK, 384), BF),
        keys_half=v((2 * TOK, WIDTH), BF),
        key_grad=v((TOK, WIDTH), F32),
        value_grad=v((TOK, WIDTH), F32),
        attn_grad=v((TOK, WIDTH), F32),
        vec=v((16, WIDTH), F32),
        vec_came=v((DIMS + 1, 16, WIDTH), F32),
        grads_wide=v((2, WIDTH, HALF), BF),
        grads_slim=v((2, WIDTH, WIDTH), BF),
        landing_wide=v((2, DIMS, 144, HALF), BF),
        landing_slim=v((2, DIMS, 144, WIDTH), BF),
        send_sem=dma((sets, DIMS, STEPS + 2)),
        recv_sem=dma((sets, DIMS, STEPS + 2)),
        side_send=dma((18,)),
        side_recv=dma((18,)),
        vec_send=dma((DIMS + 1,)),
        vec_recv=dma((DIMS + 1,)),
        load_sem=dma((4,)),
    )


NAMES = tuple(scratch())


def kernel(
    lengths,
    order,
    x,
    cot,
    attn_gain,
    attn_shift,
    query_bias,
    value_bias,
    proj_bias,
    mlp_gain,
    mlp_shift,
    up_bias,
    down_bias,
    qkv_weight,
    proj_weight,
    up_weight,
    down_weight,
    block_output,
    input_grad,
    whole_wide,
    whole_slim,
    vec_out,
    *refs,
):
    m = SimpleNamespace(**dict(zip(NAMES, refs)))
    at = place()
    core, seq = at.core, at.seq
    pair_of = lambda wide, slim: (wide.at[0], wide.at[1], slim.at[0], slim.at[1])
    grads = pair_of(m.grads_wide, m.grads_slim)
    ex = Exchange(
        at,
        grads,
        pair_of(whole_wide, whole_slim),
        pair_of(m.landing_wide, m.landing_slim),
        m.send_sem,
        m.recv_sem,
    )

    barrier = pltpu.get_barrier_semaphore()
    for device in at.partners + (at.sibling, at.across):
        pl.semaphore_signal(barrier, inc=1, device_id=device, device_id_type=MESH)

    loads = [
        pltpu.make_async_copy(src, dst, m.load_sem.at[i])
        for i, (src, dst) in enumerate(
            (
                (qkv_weight, m.qkv_w),
                (down_weight.at[rows_of(core * HALF, HALF)], m.down_w),
                (proj_weight, m.proj_w),
                (up_weight.at[:, rows_of(core * HALF, HALF)], m.up_w),
            )
        )
    ]
    for load in loads:
        load.start()

    def side(i, src, dst, device):
        copy = pltpu.make_async_remote_copy(
            src_ref=src,
            dst_ref=dst,
            send_sem=m.side_send.at[i],
            recv_sem=m.side_recv.at[i],
            device_id=device,
            device_id_type=MESH,
        )
        copy.start()
        return copy

    own = rows_of(seq * TOK, TOK)
    two = rows_of(core * TOK, TOK)
    two_other = rows_of((1 - core) * TOK, TOK)
    far = rows_of(((1 - at.chip) * 2 + core) * TOK, TOK)
    chip_rows = lambda chip: rows_of(chip * 2 * TOK, 2 * TOK)
    cut = lambda start, size: pl.ds(pl.multiple_of(start, 128), size)

    vectors = (attn_gain, attn_shift, query_bias, value_bias, proj_bias, mlp_gain, mlp_shift, down_bias)
    for i, vector in enumerate(vectors):
        m.lines[i : i + 1, :] = vector[...][None]
    attn_gain, attn_shift, query_bias, value_bias, proj_bias, mlp_gain, mlp_shift, down_bias = (
        m.lines.at[i : i + 1] for i in range(8)
    )

    normalize(
        lambda rows: x[0, rows, :].astype(F32), attn_gain, attn_shift, m.hat1, m.fac1, m.normed_in, seq * TOK
    )
    m.cot2[two, :] = cot[0]

    pl.semaphore_wait(barrier, DIMS + 2)
    in_far = side(1, m.normed_in.at[own], m.normed_in.at[own], at.across)
    in_sib = side(0, m.normed_in.at[own], m.normed_in.at[own], at.sibling)
    cot_sib = side(3, m.cot2.at[two], m.cot2.at[two], at.sibling)

    ends = [lengths[0, 0]]
    for i in (1, 2):
        ends.append(ends[-1] + lengths[0, i])
    lane = lax.broadcasted_iota(jnp.int32, (1, 128), 1)
    token = lax.broadcasted_iota(jnp.int32, (TOK, 128), 0)

    def image(j):
        t = token + order[0, j] * TOK
        return sum((t >= end).astype(jnp.int32) for end in ends)

    for j in range(4):
        other = jnp.where(lane == image(j), 0.0, -1e30)
        m.key_ext[j * TOK : (j + 1) * TOK, :] = jnp.where(lane < 4, other, jnp.where(lane < 76, 1.0, 0.0)).astype(BF)
    image_own = jnp.where(lane == image(seq), 1.0, 0.0)
    m.query_ext[own, :] = image_own.astype(BF)
    m.up_bias_half[...] = jnp.where(core == 0, up_bias[:HALF], up_bias[HALF:])[None]
    m.vec[...] = jnp.zeros((16, WIDTH), F32)
    m.vec[7:8, :] = jnp.sum(
        jnp.sum(cot[0].astype(F32).reshape(TOK // 8, 8, WIDTH), axis=0), axis=0, keepdims=True
    )
    m.stat[...] = jnp.zeros((TOK, 128), F32)
    low_lanes = (lane < 64).astype(BF)
    high_lanes = (lane >= 64).astype(BF)

    def both(v):
        return jnp.concatenate((v * low_lanes, v * high_lanes), axis=0)

    def joined(v):
        return jnp.where(lane < 64, v[:TOK], v[TOK:])

    def beside(a, b):
        return jnp.concatenate((a, b), axis=1)

    def project(chip):
        rows = chip_rows(chip)
        a = m.normed_in[rows, :]
        m.keys[rows, :] = dot(a, m.qkv_w[:, WIDTH : 2 * WIDTH]).astype(BF)
        m.values[rows, :] = (dot(a, m.qkv_w[:, 2 * WIDTH :]) + value_bias[...]).astype(BF)
        m.queries[rows, :] = ((dot(a, m.qkv_w[:, :WIDTH]) + query_bias[...]) * SCALE).astype(BF)

    loads[0].wait()
    in_sib.wait()
    project(at.chip)
    loads[1].wait()
    cot_sib.wait()
    m.hidden_grad[...] = dot_rt(m.cot2[...], m.down_w[...])
    in_far.wait()
    in_pass = side(2, m.normed_in.at[far], m.normed_in.at[far], at.sibling)
    in_pass.wait()
    project(1 - at.chip)

    def attend(i, carry):
        cols = rows_of(i * 128, 128)
        ext = m.query_ext[own, :]
        s = dot_rt(
            beside(both(m.queries[own, cols]), jnp.concatenate((ext, ext), axis=0)),
            beside(m.keys[:, cols], m.key_ext[...]),
        )
        top = jnp.max(s, axis=1, keepdims=True)
        e = jnp.exp(s - top).astype(BF)
        out = dot(e, beside(m.values[:, cols], jnp.ones((LEN, 128), BF)))
        total = out[:, 128:]
        out = joined(out[:, :128] * (1.0 / total))
        m.attended_full[:, cols] = out
        m.attended[two, cols] = out.astype(BF)
        logs = top + jnp.log(total)
        m.stat[...] = jnp.where(
            lane == 2 * i, logs[:TOK], jnp.where(lane == 2 * i + 1, logs[TOK:], m.stat[...])
        )
        return carry

    lax.fori_loop(0, PAIRS, attend, 0, unroll=True)

    loads[2].wait()
    m.resid[...] = x[0].astype(F32) + dot(m.attended[two, :], m.proj_w[...]) + proj_bias[...]
    normalize(lambda rows: m.resid[rows, :], mlp_gain, mlp_shift, m.hat2, m.fac2, m.mlp_in, core * TOK)
    mlp_sib = side(4, m.mlp_in.at[two], m.mlp_in.at[two], at.sibling)
    att_sib = side(5, m.attended.at[two], m.attended.at[two], at.sibling)
    loads[3].wait()
    mlp_sib.wait()

    def feed(i, carry):
        cols = rows_of(i * 512, 512)
        u = dot(m.mlp_in[...], m.up_w[:, cols]) + m.up_bias_half[:, cols]
        t = 1.0 / (1.0 + 0.36 * jnp.abs(u))
        tail = jnp.full_like(t, TAIL[-1])
        for c in TAIL[-2::-1]:
            tail = tail * t + c
        e = jnp.exp(-0.5 * (u * u))
        tail = tail * (t * e)
        phi = jnp.where(u >= 0, 1.0 - tail, tail)
        m.hidden[:, cols] = (u * phi).astype(BF)
        g = m.hidden_grad[:, cols] * (phi + u * (DENSITY * e))
        m.up_low[:, cols] = g.astype(BF)
        m.up_bias_half[:, cols] = jnp.sum(
            jnp.sum(g.reshape(2 * TOK // 8, 8, 512), axis=0), axis=0, keepdims=True
        )
        return carry

    lax.fori_loop(0, HALF // 512, feed, 0)

    def block_of(k):
        return slice(k * TOK, (k + 1) * TOK)

    def start_up(ks):
        for k in ks:
            grads[UP][block_of(k), :] = dot_lt(m.mlp_in[:, block_of(k)], m.up_low[...]).astype(BF)
            ex.start(UP, k)

    for k in range(DIMS):
        for h in range(2):
            first = h * WIDTH + k * TOK
            grads[DOWN][block_of(k), h * WIDTH : (h + 1) * WIDTH] = dot_lt(
                m.hidden[:, first : first + TOK], m.cot2[...]
            ).astype(BF)
        ex.start(DOWN, k)
    m.mlp_part[...] = dot_rt(m.up_low[...], m.up_w[...])
    part_sib = side(6, m.mlp_part.at[two_other], m.mlp_came, at.sibling)
    start_up(range(4))
    for h in range(2):
        for t in range(2):
            m.vec[8 + 2 * h + t : 9 + 2 * h + t, :] = jnp.where(
                core == h, m.up_bias_half[:, t * WIDTH : (t + 1) * WIDTH], 0.0
            )
    part_sib.wait()

    def keep_resid(rows, back):
        m.resid_grad[rows, :] = back
        m.resid_low[rows, :] = back.astype(BF)

    norm_back(
        lambda rows: m.mlp_part[rows_of_shift(rows, core * TOK), :] + m.mlp_came[rows, :],
        lambda rows: cot[0, rows, :].astype(F32),
        mlp_gain,
        m.hat2,
        m.fac2,
        m.vec,
        (5, 6, 4),
        keep_resid,
    )
    back = dot_rt(m.resid_low[...], m.proj_w[...]).astype(BF)
    m.attended_grad[own, :] = back
    grad_far = side(9, m.attended_grad.at[own], m.attended_grad.at[own], at.across)
    grad_sib = side(8, m.attended_grad.at[own], m.attended_grad.at[own], at.sibling)

    def parts(v):
        found = []
        for _ in range(3):
            found.append(v.astype(BF))
            v = v - found[-1].astype(F32)
        return found

    feature = lax.broadcasted_iota(jnp.int32, (WIDTH, 128), 0)
    head_of = (feature // 64 + 16 == lax.broadcasted_iota(jnp.int32, (WIDTH, 128), 1)).astype(BF)
    sums = sum(dot(p, head_of) for p in parts(back.astype(F32) * m.attended_full[...]))
    ext = image_own
    for j, p in enumerate(parts(-(m.stat[...] + sums))):
        to = lax.broadcasted_iota(jnp.int32, (128, 128), 1)
        of = lax.broadcasted_iota(jnp.int32, (128, 128), 0)
        spot = jnp.where(of < 12, 4 + 3 * of + j, jnp.where((of >= 16) & (of < 28), 3 * of - 8 + j, -1))
        ext = ext + dot(p, (to == spot).astype(BF))
    m.query_ext[own, :] = ext.astype(BF)
    ext_far = side(12, m.query_ext.at[own], m.query_ext.at[own], at.across)
    ext_sib = side(11, m.query_ext.at[own], m.query_ext.at[own], at.sibling)
    start_up(range(4, DIMS))
    m.resid_half[two, :] = m.resid_low[:, cut(core * 384, 384)]
    resid_sib = side(14, m.resid_low.at[:, cut((1 - core) * 384, 384)], m.resid_half.at[two], at.sibling)

    def picks(i):
        a, b = lane - 4 - 6 * i, lane - 40 - 6 * i
        first = jnp.where((lane < 4) | ((a >= 0) & (a < 3)), 1.0, 0.0).astype(BF)
        second = jnp.where((lane < 4) | ((a >= 3) & (a < 6)), 1.0, 0.0).astype(BF)
        third = jnp.where((b >= 0) & (b < 3), 1.0, 0.0).astype(BF)
        fourth = jnp.where((b >= 3) & (b < 6), 1.0, 0.0).astype(BF)
        return (lambda v: jnp.concatenate((v * first, v * second), axis=0)), (
            lambda v: jnp.concatenate((v * third, v * fourth), axis=0)
        )

    def query_side(i, carry):
        cols = rows_of(i * 128, 128)
        of_scores, of_means = picks(i)
        ext, k = m.query_ext[own, :], m.keys[:, cols]
        p = jnp.exp(
            dot_rt(beside(both(m.queries[own, cols]), of_scores(ext)), beside(k, m.key_ext[...]))
        )
        y = dot_rt(
            beside(both(m.attended_grad[own, cols]), of_means(ext)),
            beside(m.values[:, cols], m.key_ext[...]),
        )
        g = joined(dot((p * y).astype(BF), k)) * SCALE
        m.vec[2:3, cols] = jnp.sum(g, axis=0, keepdims=True)
        m.qkv_low[:, cols] = g.astype(BF)
        return carry

    def key_side(chip, first):
        rows = chip_rows(chip)

        def step(i, carry):
            cols = rows_of(i * 128, 128)
            of_scores, of_means = picks(i)
            q, g, ext = m.queries[rows, cols], m.attended_grad[rows, cols], m.key_ext[own, :]
            other = m.query_ext[rows, :]
            p = jnp.exp(dot_rt(beside(both(m.keys[own, cols]), of_scores(ext)), beside(q, other)))
            y = dot_rt(beside(both(m.values[own, cols]), of_means(ext)), beside(g, other))
            dv = joined(dot(p.astype(BF), g))
            dk = joined(dot((p * y).astype(BF), q))
            if first:
                m.value_grad[:, cols] = dv
                m.key_grad[:, cols] = dk
            else:
                dv = dv + m.value_grad[:, cols]
                dk = dk + m.key_grad[:, cols]
                m.vec[3:4, cols] = jnp.sum(dv, axis=0, keepdims=True)
                m.qkv_low[:, cut(WIDTH + i * 128, 128)] = dk.astype(BF)
                m.qkv_low[:, cut(2 * WIDTH + i * 128, 128)] = dv.astype(BF)
            return carry

        lax.fori_loop(0, PAIRS, step, 0, unroll=3)

    def share(i, part, target):
        target.at[two][...] = m.qkv_low[:, cut(part * WIDTH + core * 384, 384)]
        return side(
            i, m.qkv_low.at[:, cut(part * WIDTH + (1 - core) * 384, 384)], target.at[two], at.sibling
        )

    lax.fori_loop(0, PAIRS, query_side, 0, unroll=3)
    query_sib = share(15, 0, m.query_half)
    ex.finish(DOWN, 0)
    grad_sib.wait()
    ext_sib.wait()
    key_side(at.chip, True)
    att_sib.wait()
    resid_sib.wait()
    query_sib.wait()
    for k in range(DIMS):
        grads[PROJ][block_of(k), :384] = dot_lt(m.attended[:, block_of(k)], m.resid_half[...]).astype(BF)
        grads[PROJ][block_of(k), 384:] = dot_lt(
            m.normed_in[chip_rows(at.chip), block_of(k)], m.query_half[...]
        ).astype(BF)
        ex.start(PROJ, k)
    ex.finish(DOWN, 1)
    grad_far.wait()
    grad_pass = side(10, m.attended_grad.at[far], m.attended_grad.at[far], at.sibling)
    ext_far.wait()
    ext_pass = side(13, m.query_ext.at[far], m.query_ext.at[far], at.sibling)
    ex.finish(UP, 0)
    grad_pass.wait()
    ext_pass.wait()
    key_side(1 - at.chip, False)
    key_sib = share(16, 1, m.keys_half.at[:, :384])
    value_sib = share(17, 2, m.keys_half.at[:, 384:])
    ex.finish(DOWN, 2)
    key_sib.wait()
    value_sib.wait()
    for k in range(DIMS):
        grads[KEYS][block_of(k), :] = dot_lt(
            m.normed_in[chip_rows(at.chip), block_of(k)], m.keys_half[...]
        ).astype(BF)
        ex.start(KEYS, k)
    ex.finish(PROJ, 0)
    ex.finish(UP, 1)
    ex.finish(DOWN, 3)

    m.attn_grad[...] = dot_rt(m.qkv_low[...], m.qkv_w[...])

    def keep_input(rows, back):
        input_grad[0, rows, :] = back.astype(BF)

    norm_back(
        lambda rows: m.attn_grad[rows, :],
        lambda rows: m.resid_grad[rows, :],
        attn_gain,
        m.hat1,
        m.fac1,
        m.vec,
        (0, 1),
        keep_input,
    )

    def vec_start(s):
        copy = pltpu.make_async_remote_copy(
            src_ref=m.vec,
            dst_ref=m.vec_came.at[s],
            send_sem=m.vec_send.at[s],
            recv_sem=m.vec_recv.at[s],
            device_id=(at.partners + (at.sibling,))[s],
            device_id_type=MESH,
        )
        copy.start()
        return copy

    vec_copy = [vec_start(0)]

    def vec_finish(s):
        vec_copy[0].wait()
        m.vec[...] = m.vec[...] + m.vec_came[s]
        if s < DIMS:
            vec_copy[0] = vec_start(s + 1)
        else:
            vec_out[...] = m.vec[...]

    ex.finish(PROJ, 1)
    ex.finish(KEYS, 0)
    m.out_part[...] = dot(m.hidden[...], m.down_w[...])
    out_sib = side(7, m.out_part.at[two_other], m.out_came, at.sibling)
    ex.finish(UP, 2)
    ex.finish(PROJ, 2)
    ex.finish(DOWN, 4)
    out_sib.wait()
    block_output[0] = (
        m.resid[...] + (m.out_part[two, :] + m.out_came[...]) + down_bias[...]
    ).astype(BF)

    for n, (w, s) in enumerate(LAST):
        ex.finish(w, s)
        if n % 3 == 0 and n // 3 <= DIMS:
            vec_finish(n // 3)

    for w in range(len(WIDTHS)):
        for k in range(DIMS):
            for part in range(2):
                ex.copies[w, k, STEPS + part].wait()


LAST = (
    (KEYS, 1), (PROJ, 3), (UP, 3), (DOWN, 5), (KEYS, 2), (PROJ, 4), (UP, 4),
    (DOWN, 6), (KEYS, 3), (PROJ, 5), (UP, 5), (PROJ, 6), (KEYS, 4), (UP, 6),
    (DOWN, 7), (PROJ, 7), (KEYS, 5), (UP, 7), (DOWN, 8), (KEYS, 6), (PROJ, 8),
    (UP, 8), (KEYS, 7), (DOWN, 9), (KEYS, 8), (PROJ, 9), (UP, 9), (KEYS, 9),
)


def rows_of_shift(rows, shift):
    return pl.ds(pl.multiple_of(rows.start + shift, 16), rows.size)


def spread_kernel(
    wide,
    slim,
    vec,
    block_output_in,
    input_grad_in,
    block_output,
    input_grad,
    attn_gain,
    attn_shift,
    qkv,
    query_bias,
    value_bias,
    proj,
    proj_bias,
    mlp_gain,
    mlp_shift,
    up,
    up_bias,
    down,
    down_bias,
):
    rows = rows_of(pl.program_id(0) * SPREAD_ROWS, SPREAD_ROWS)
    for c in range(2):
        up[:, c * HALF : (c + 1) * HALF] = wide[1, c, rows, :].astype(F32)
        proj[:, c * 384 : (c + 1) * 384] = slim[0, c, rows, :384].astype(F32)
        for part in range(3):
            first = part * WIDTH + c * 384
            source = slim[0, c, rows, 384:] if part == 0 else slim[1, c, rows, (part - 1) * 384 : part * 384]
            qkv[:, first : first + 384] = source.astype(F32)
        for h in range(2):
            down[2 * c + h] = wide[0, c, rows, h * WIDTH : (h + 1) * WIDTH].astype(F32)

    @pl.when(pl.program_id(0) == 0)
    def _():
        block_output[...] = block_output_in[...]
        input_grad[...] = input_grad_in[...]
        for row, ref in enumerate(
            (attn_gain, attn_shift, query_bias, value_bias, proj_bias, mlp_gain, mlp_shift, down_bias)
        ):
            ref[...] = vec[row]
        for t in range(4):
            up_bias[t * WIDTH : (t + 1) * WIDTH] = vec[8 + t]


SPREAD_ROWS = 64


def spread(*given):
    rows = SPREAD_ROWS
    line = lambda n: (jax.ShapeDtypeStruct((n,), F32), pl.BlockSpec((n,), lambda i: (0,)))
    flat = lambda n: (jax.ShapeDtypeStruct((WIDTH, n), F32), pl.BlockSpec((rows, n), lambda i: (i, 0)))
    tokens = (jax.ShapeDtypeStruct((1, TOK, WIDTH), BF), pl.BlockSpec((1, TOK, WIDTH), lambda i: (0, 0, 0)))
    outs = [
        tokens,
        tokens,
        line(WIDTH),
        line(WIDTH),
        flat(3 * WIDTH),
        line(WIDTH),
        line(WIDTH),
        flat(WIDTH),
        line(WIDTH),
        line(WIDTH),
        line(WIDTH),
        flat(HIDDEN),
        line(HIDDEN),
        (
            jax.ShapeDtypeStruct((4, WIDTH, WIDTH), F32),
            pl.BlockSpec((4, rows, WIDTH), lambda i: (0, i, 0)),
        ),
        line(WIDTH),
    ]
    return pl.pallas_call(
        spread_kernel,
        grid=(WIDTH // rows,),
        out_shape=[o[0] for o in outs],
        in_specs=[pl.BlockSpec(memory_space=pltpu.VMEM)] * len(given),
        out_specs=[o[1] for o in outs],
        compiler_params=pltpu.CompilerParams(vmem_limit_bytes=24 << 20),
    )(*(pltpu.with_memory_space_constraint(v, pltpu.VMEM) for v in given))


def body(
    block_input,
    out_cotangent,
    image_lengths,
    span_order,
    attn_gain,
    attn_shift,
    qkv_weight,
    query_bias,
    value_bias,
    proj_weight,
    proj_bias,
    mlp_gain,
    mlp_shift,
    up_weight,
    up_bias,
    down_weight,
    down_bias,
):
    vmem = pl.BlockSpec(memory_space=pltpu.VMEM)
    smem = pl.BlockSpec(memory_space=pltpu.SMEM)
    hbm = pl.BlockSpec(memory_space=pl.ANY)
    held = scratch()
    block_output, input_grad, wide, slim, vec = pl.pallas_call(
        kernel,
        out_shape=[
            pltpu.VMEM((1, TOK, WIDTH), BF),
            pltpu.VMEM((1, TOK, WIDTH), BF),
            pltpu.VMEM((2, 2, WIDTH, HALF), BF),
            pltpu.VMEM((2, 2, WIDTH, WIDTH), BF),
            pltpu.VMEM((16, WIDTH), F32),
        ],
        in_specs=[smem, smem] + [vmem] * 11 + [hbm] * 4,
        out_specs=[vmem] * 5,
        scratch_shapes=[held[name] for name in NAMES],
        compiler_params=pltpu.CompilerParams(
            collective_id=0, has_side_effects=True, vmem_limit_bytes=VMEM_LIMIT
        ),
    )(
        image_lengths,
        span_order,
        block_input,
        out_cotangent,
        attn_gain,
        attn_shift,
        query_bias,
        value_bias,
        proj_bias,
        mlp_gain,
        mlp_shift,
        up_bias,
        down_bias,
        qkv_weight,
        proj_weight,
        up_weight,
        down_weight,
    )
    outs = list(spread(wide, slim, vec, block_output, input_grad))
    outs[13] = outs[13].reshape(HIDDEN, WIDTH)
    return tuple(outs)


VMEM_LIMIT = 46 << 20


def solution(mesh):
    tokens = P("rows", "seq", None)
    return jax.shard_map(
        body,
        mesh=mesh,
        in_specs=(tokens, tokens, P("rows", None), P("rows", None)) + (P(),) * 13,
        out_specs=(tokens, tokens) + (P(),) * 13,
        check_vma=False,
    )
```

time: 145 us -> 117 us (0.81)
  Pallas kernels: 143 us -> 116 us
    pallas_call x1, Pallas kernels: 126 us -> 106 us  [body(): pl.pallas_call(kernel, out_shape=[pltpu.VMEM((1, TOK, WIDTH), BF), pltpu....]
    pallas_call x1, Pallas kernels: 16.4 us -> 10.1 us  [spread(): pl.pallas_call(spread_kernel, grid=(WIDTH // rows,), out_shape=[o[0] for...]
where the time goes in v3:
time: 117 us
  Pallas kernels  116 us (99%)
    pallas_call x1, Pallas kernels, body(): pl.pallas_call(kernel, out_shape=[pltpu.VMEM((1, TOK, WIDTH), BF), pltpu....  106 us
    pallas_call x1, Pallas kernels, spread(): pl.pallas_call(spread_kernel, grid=(WIDTH // rows,), out_shape=[o[0] for...  10.1 us

profile of v3, /device:TPU:1, one launch (start us, length us, event | category | flops | bytes accessed | tf_op | source)
XLA Modules:
  0.0 116.6 jit_solution(10875931829264711347)
XLA Ops:
  0.7 105.8 %shard_map.280 = (bf16[1,128,768]{2,1,0:T(8,128)(2,1)S(1)}, bf16[1,128,768]{2,1,0:T(8,128)(2,1)S(1)}, bf16[2,2,768,1536]{3,2,1,0:T(8,128)(2,1)S(1)}, bf16[2,2,768,768]{3,2,1,0:T(8,128)(2,1)S(1)}, f32[16,768]{1,0:T(8,128)S(1)}) custom-call(s32[1,4]{1,0:T(1,128)} %lengths.1, s32[1,4]{1,0:T(1,128)} %order.1, bf16[1,128,768]{2,1,0:T(8,128)(2,1)} %x.1, ...), custom_call_target="tpu_custom_call" | custom-call | tf_op jit(solution)/shard_map/pallas_call | solution.py:800
  106.4 10.1 %shard_map.281 = (bf16[1,128,768]{2,1,0:T(8,128)(2,1)}, bf16[1,128,768]{2,1,0:T(8,128)(2,1)}, f32[768]{0:T(1024)}, f32[768]{0:T(1024)}, f32[768,2304]{1,0:T(8,12...) custom-call(bf16[2,2,768,1536]{3,2,1,0:T(8,128)(2,1)S(1)} %get-tuple, ...), custom_call_target="tpu_custom_call" | custom-call | tf_op jit(solution)/shard_map/pallas_call | solution.py:767

commit v4 on v3

--- a/solution.py
+++ b/solution.py
@@ -84,10 +84,10 @@
 
 
 class Exchange:
-    def __init__(self, at, grads, whole, landing, send_sem, recv_sem):
+    def __init__(self, at, grads, whole, landing, send_sem, recv_sem, over_sem):
         self.at = at
         self.grads, self.whole, self.landing = grads, whole, landing
-        self.send_sem, self.recv_sem = send_sem, recv_sem
+        self.send_sem, self.recv_sem, self.over_sem = send_sem, recv_sem, over_sem
         self.copies = {}
 
     def dim(self, k, s):
@@ -118,18 +118,6 @@
         width = WIDTHS[w] // 2
         return self.landing[w].at[k, pl.ds((112, 112, 128)[s - 3], 16), pl.ds((0, width, 0)[s - 3], width)]
 
-    def send(self, w, k, s, src, dst, device):
-        copy = pltpu.make_async_remote_copy(
-            src_ref=src,
-            dst_ref=dst,
-            send_sem=self.send_sem.at[w, k, s],
-            recv_sem=self.recv_sem.at[w, k, s],
-            device_id=device,
-            device_id_type=MESH,
-        )
-        copy.start()
-        self.copies[w, k, s] = copy
-
     def start(self, w, k, s=0):
         if s < 4:
             src, dst, d = self.block(w, k, s, False), self.slot(w, k, s), self.dim(k, s)
@@ -138,28 +126,47 @@
         else:
             src = dst = self.block(w, k, 9 - s, True, True)
             d = self.dim(k, 9 - s)
-        self.send(w, k, s, src, dst, self.at.partners[d])
+        copy = pltpu.make_async_remote_copy(
+            src_ref=src,
+            dst_ref=dst,
+            send_sem=self.send_sem.at[w, k],
+            recv_sem=self.recv_sem.at[w, k, s],
+            device_id=self.at.partners[d],
+            device_id_type=MESH,
+        )
+        copy.start()
+        self.copies[w, k, s] = copy
 
     def over(self, w, k, part):
         half = self.block(w, k, 0, part == 0, True)
-        self.send(w, k, STEPS + part, half, half, self.at.sibling)
-
-    def finish(self, w, s):
-        for k in range(DIMS):
-            self.copies[w, k, s].wait()
-            if s < 6:
-                kept, slot = self.block(w, k, min(s, 3), True), self.slot(w, k, s)
-                total = (kept[...].astype(F32) + slot[...].astype(F32)).astype(BF)
-                if s < 5:
-                    kept[...] = total
-                else:
-                    self.block(w, k, 3, True, True)[...] = total
-            if s < STEPS - 1:
-                self.start(w, k, s + 1)
-                if s == STEPS - 2:
-                    self.over(w, k, 0)
+        self.crossing(w, half, half).start()
+
+    def crossing(self, w, src, dst):
+        return pltpu.make_async_remote_copy(
+            src_ref=src,
+            dst_ref=dst,
+            send_sem=self.over_sem.at[0, w],
+            recv_sem=self.over_sem.at[1, w],
+            device_id=self.at.sibling,
+            device_id_type=MESH,
+        )
+
+    def done(self, w):
+        self.crossing(w, self.whole[w].at[self.at.core], self.whole[w].at[1 - self.at.core]).wait()
+
+    def finish(self, w, k, s):
+        self.copies[w, k, s].wait()
+        if s < 6:
+            kept, slot = self.block(w, k, min(s, 3), True), self.slot(w, k, s)
+            total = (kept[...].astype(F32) + slot[...].astype(F32)).astype(BF)
+            if s < 5:
+                kept[...] = total
             else:
-                self.over(w, k, 1)
+                self.block(w, k, 3, True, True)[...] = total
+        if s < STEPS - 1:
+            self.start(w, k, s + 1)
+        if s >= STEPS - 2:
+            self.over(w, k, s - (STEPS - 2))
 
 
 def normalize(load, gain, shift, normed, factor, result, base):
@@ -249,8 +256,9 @@
         grads_slim=v((2, WIDTH, WIDTH), BF),
         landing_wide=v((2, DIMS, 144, HALF), BF),
         landing_slim=v((2, DIMS, 144, WIDTH), BF),
-        send_sem=dma((sets, DIMS, STEPS + 2)),
-        recv_sem=dma((sets, DIMS, STEPS + 2)),
+        send_sem=dma((sets, DIMS)),
+        recv_sem=dma((sets, DIMS, STEPS)),
+        over_sem=dma((2, sets)),
         side_send=dma((18,)),
         side_recv=dma((18,)),
         vec_send=dma((DIMS + 1,)),
@@ -299,6 +307,7 @@
         pair_of(m.landing_wide, m.landing_slim),
         m.send_sem,
         m.recv_sem,
+        m.over_sem,
     )
 
     barrier = pltpu.get_barrier_semaphore()
@@ -459,46 +468,58 @@
     def block_of(k):
         return slice(k * TOK, (k + 1) * TOK)
 
-    def start_up(ks):
-        for k in ks:
-            grads[UP][block_of(k), :] = dot_lt(m.mlp_in[:, block_of(k)], m.up_low[...]).astype(BF)
-            ex.start(UP, k)
-
-    for k in range(DIMS):
+    def start(w, k):
+        block = block_of(k)
+        if w == DOWN:
+            for h in range(2):
+                first = h * WIDTH + k * TOK
+                grads[w][block, h * WIDTH : (h + 1) * WIDTH] = dot_lt(
+                    m.hidden[:, first : first + TOK], m.cot2[...]
+                ).astype(BF)
+        elif w == UP:
+            grads[w][block, :] = dot_lt(m.mlp_in[:, block], m.up_low[...]).astype(BF)
+        elif w == PROJ:
+            grads[w][block, :384] = dot_lt(m.attended[:, block], m.resid_half[...]).astype(BF)
+            grads[w][block, 384:] = dot_lt(
+                m.normed_in[chip_rows(at.chip), block], m.query_half[...]
+            ).astype(BF)
+        else:
+            grads[w][block, :] = dot_lt(
+                m.normed_in[chip_rows(at.chip), block], m.keys_half[...]
+            ).astype(BF)
+        ex.start(w, k)
+
+    sides = {}
+
+    def mlp_back():
+        m.mlp_part[...] = dot_rt(m.up_low[...], m.up_w[...])
+        sides["part"] = side(6, m.mlp_part.at[two_other], m.mlp_came, at.sibling)
         for h in range(2):
-            first = h * WIDTH + k * TOK
-            grads[DOWN][block_of(k), h * WIDTH : (h + 1) * WIDTH] = dot_lt(
-                m.hidden[:, first : first + TOK], m.cot2[...]
-            ).astype(BF)
-        ex.start(DOWN, k)
-    m.mlp_part[...] = dot_rt(m.up_low[...], m.up_w[...])
-    part_sib = side(6, m.mlp_part.at[two_other], m.mlp_came, at.sibling)
-    start_up(range(4))
-    for h in range(2):
-        for t in range(2):
-            m.vec[8 + 2 * h + t : 9 + 2 * h + t, :] = jnp.where(
-                core == h, m.up_bias_half[:, t * WIDTH : (t + 1) * WIDTH], 0.0
-            )
-    part_sib.wait()
+            for t in range(2):
+                m.vec[8 + 2 * h + t : 9 + 2 * h + t, :] = jnp.where(
+                    core == h, m.up_bias_half[:, t * WIDTH : (t + 1) * WIDTH], 0.0
+                )
 
     def keep_resid(rows, back):
         m.resid_grad[rows, :] = back
         m.resid_low[rows, :] = back.astype(BF)
 
-    norm_back(
-        lambda rows: m.mlp_part[rows_of_shift(rows, core * TOK), :] + m.mlp_came[rows, :],
-        lambda rows: cot[0, rows, :].astype(F32),
-        mlp_gain,
-        m.hat2,
-        m.fac2,
-        m.vec,
-        (5, 6, 4),
-        keep_resid,
-    )
-    back = dot_rt(m.resid_low[...], m.proj_w[...]).astype(BF)
-    m.attended_grad[own, :] = back
-    grad_far = side(9, m.attended_grad.at[own], m.attended_grad.at[own], at.across)
-    grad_sib = side(8, m.attended_grad.at[own], m.attended_grad.at[own], at.sibling)
+    def resid_back():
+        sides["part"].wait()
+        norm_back(
+            lambda rows: m.mlp_part[rows_of_shift(rows, core * TOK), :] + m.mlp_came[rows, :],
+            lambda rows: cot[0, rows, :].astype(F32),
+            mlp_gain,
+            m.hat2,
+            m.fac2,
+            m.vec,
+            (5, 6, 4),
+            keep_resid,
+        )
+        m.attended_grad[own, :] = dot_rt(m.resid_low[...], m.proj_w[...]).astype(BF)
+        grad = m.attended_grad.at[own]
+        sides["grad_far"] = side(9, grad, grad, at.across)
+        sides["grad_sib"] = side(8, grad, grad, at.sibling)
 
     def parts(v):
         found = []
@@ -507,21 +528,27 @@
             v = v - found[-1].astype(F32)
         return found
 
-    feature = lax.broadcasted_iota(jnp.int32, (WIDTH, 128), 0)
-    head_of = (feature // 64 + 16 == lax.broadcasted_iota(jnp.int32, (WIDTH, 128), 1)).astype(BF)
-    sums = sum(dot(p, head_of) for p in parts(back.astype(F32) * m.attended_full[...]))
-    ext = image_own
-    for j, p in enumerate(parts(-(m.stat[...] + sums))):
-        to = lax.broadcasted_iota(jnp.int32, (128, 128), 1)
-        of = lax.broadcasted_iota(jnp.int32, (128, 128), 0)
-        spot = jnp.where(of < 12, 4 + 3 * of + j, jnp.where((of >= 16) & (of < 28), 3 * of - 8 + j, -1))
-        ext = ext + dot(p, (to == spot).astype(BF))
-    m.query_ext[own, :] = ext.astype(BF)
-    ext_far = side(12, m.query_ext.at[own], m.query_ext.at[own], at.across)
-    ext_sib = side(11, m.query_ext.at[own], m.query_ext.at[own], at.sibling)
-    start_up(range(4, DIMS))
-    m.resid_half[two, :] = m.resid_low[:, cut(core * 384, 384)]
-    resid_sib = side(14, m.resid_low.at[:, cut((1 - core) * 384, 384)], m.resid_half.at[two], at.sibling)
+    def extend():
+        feature = lax.broadcasted_iota(jnp.int32, (WIDTH, 128), 0)
+        head_of = (feature // 64 + 16 == lax.broadcasted_iota(jnp.int32, (WIDTH, 128), 1)).astype(BF)
+        means = m.attended_grad[own, :].astype(F32) * m.attended_full[...]
+        sums = sum(dot(p, head_of) for p in parts(means))
+        ext = image_own
+        for j, p in enumerate(parts(-(m.stat[...] + sums))):
+            to = lax.broadcasted_iota(jnp.int32, (128, 128), 1)
+            of = lax.broadcasted_iota(jnp.int32, (128, 128), 0)
+            spot = jnp.where(
+                of < 12, 4 + 3 * of + j, jnp.where((of >= 16) & (of < 28), 3 * of - 8 + j, -1)
+            )
+            ext = ext + dot(p, (to == spot).astype(BF))
+        m.query_ext[own, :] = ext.astype(BF)
+        ext = m.query_ext.at[own]
+        sides["ext_far"] = side(12, ext, ext, at.across)
+        sides["ext_sib"] = side(11, ext, ext, at.sibling)
+        m.resid_half[two, :] = m.resid_low[:, cut(core * 384, 384)]
+        sides["resid"] = side(
+            14, m.resid_low.at[:, cut((1 - core) * 384, 384)], m.resid_half.at[two], at.sibling
+        )
 
     def picks(i):
         a, b = lane - 4 - 6 * i, lane - 40 - 6 * i
@@ -533,27 +560,28 @@
             lambda v: jnp.concatenate((v * third, v * fourth), axis=0)
         )
 
-    def query_side(i, carry):
-        cols = rows_of(i * 128, 128)
-        of_scores, of_means = picks(i)
-        ext, k = m.query_ext[own, :], m.keys[:, cols]
-        p = jnp.exp(
-            dot_rt(beside(both(m.queries[own, cols]), of_scores(ext)), beside(k, m.key_ext[...]))
-        )
-        y = dot_rt(
-            beside(both(m.attended_grad[own, cols]), of_means(ext)),
-            beside(m.values[:, cols], m.key_ext[...]),
-        )
-        g = joined(dot((p * y).astype(BF), k)) * SCALE
-        m.vec[2:3, cols] = jnp.sum(g, axis=0, keepdims=True)
-        m.qkv_low[:, cols] = g.astype(BF)
-        return carry
-
-    def key_side(chip, first):
+    def query_side(pairs):
+        for i in pairs:
+            cols = slice(i * 128, (i + 1) * 128)
+            of_scores, of_means = picks(i)
+            ext, k = m.query_ext[own, :], m.keys[:, cols]
+            p = jnp.exp(
+                dot_rt(beside(both(m.queries[own, cols]), of_scores(ext)), beside(k, m.key_ext[...]))
+            )
+            y = dot_rt(
+                beside(both(m.attended_grad[own, cols]), of_means(ext)),
+                beside(m.values[:, cols], m.key_ext[...]),
+            )
+            g = joined(dot((p * y).astype(BF), k)) * SCALE
+            m.vec[2:3, cols] = jnp.sum(g, axis=0, keepdims=True)
+            m.qkv_low[:, cols] = g.astype(BF)
+        if PAIRS - 1 in pairs:
+            sides["query"] = share(15, 0, m.query_half)
+
+    def key_side(chip, first, pairs):
         rows = chip_rows(chip)
-
-        def step(i, carry):
-            cols = rows_of(i * 128, 128)
+        for i in pairs:
+            cols = slice(i * 128, (i + 1) * 128)
             of_scores, of_means = picks(i)
             q, g, ext = m.queries[rows, cols], m.attended_grad[rows, cols], m.key_ext[own, :]
             other = m.query_ext[rows, :]
@@ -568,11 +596,11 @@
                 dv = dv + m.value_grad[:, cols]
                 dk = dk + m.key_grad[:, cols]
                 m.vec[3:4, cols] = jnp.sum(dv, axis=0, keepdims=True)
-                m.qkv_low[:, cut(WIDTH + i * 128, 128)] = dk.astype(BF)
-                m.qkv_low[:, cut(2 * WIDTH + i * 128, 128)] = dv.astype(BF)
-            return carry
-
-        lax.fori_loop(0, PAIRS, step, 0, unroll=3)
+                m.qkv_low[:, WIDTH + i * 128 : WIDTH + (i + 1) * 128] = dk.astype(BF)
+                m.qkv_low[:, 2 * WIDTH + i * 128 : 2 * WIDTH + (i + 1) * 128] = dv.astype(BF)
+        if not first and PAIRS - 1 in pairs:
+            sides["keys"] = share(16, 1, m.keys_half.at[:, :384])
+            sides["values"] = share(17, 2, m.keys_half.at[:, 384:])
 
     def share(i, part, target):
         target.at[two][...] = m.qkv_low[:, cut(part * WIDTH + core * 384, 384)]
@@ -580,61 +608,54 @@
             i, m.qkv_low.at[:, cut(part * WIDTH + (1 - core) * 384, 384)], target.at[two], at.sibling
         )
 
-    lax.fori_loop(0, PAIRS, query_side, 0, unroll=3)
-    query_sib = share(15, 0, m.query_half)
-    ex.finish(DOWN, 0)
-    grad_sib.wait()
-    ext_sib.wait()
-    key_side(at.chip, True)
-    att_sib.wait()
-    resid_sib.wait()
-    query_sib.wait()
-    for k in range(DIMS):
-        grads[PROJ][block_of(k), :384] = dot_lt(m.attended[:, block_of(k)], m.resid_half[...]).astype(BF)
-        grads[PROJ][block_of(k), 384:] = dot_lt(
-            m.normed_in[chip_rows(at.chip), block_of(k)], m.query_half[...]
-        ).astype(BF)
-        ex.start(PROJ, k)
-    ex.finish(DOWN, 1)
-    grad_far.wait()
-    grad_pass = side(10, m.attended_grad.at[far], m.attended_grad.at[far], at.sibling)
-    ext_far.wait()
-    ext_pass = side(13, m.query_ext.at[far], m.query_ext.at[far], at.sibling)
-    ex.finish(UP, 0)
-    grad_pass.wait()
-    ext_pass.wait()
-    key_side(1 - at.chip, False)
-    key_sib = share(16, 1, m.keys_half.at[:, :384])
-    value_sib = share(17, 2, m.keys_half.at[:, 384:])
-    ex.finish(DOWN, 2)
-    key_sib.wait()
-    value_sib.wait()
-    for k in range(DIMS):
-        grads[KEYS][block_of(k), :] = dot_lt(
-            m.normed_in[chip_rows(at.chip), block_of(k)], m.keys_half[...]
-        ).astype(BF)
-        ex.start(KEYS, k)
-    ex.finish(PROJ, 0)
-    ex.finish(UP, 1)
-    ex.finish(DOWN, 3)
-
-    m.attn_grad[...] = dot_rt(m.qkv_low[...], m.qkv_w[...])
+    def near_ready():
+        sides["grad_sib"].wait()
+        sides["ext_sib"].wait()
+
+    def proj_ready():
+        att_sib.wait()
+        sides["resid"].wait()
+        sides["query"].wait()
+
+    def far_here():
+        sides["grad_far"].wait()
+        sides["grad_pass"] = side(
+            10, m.attended_grad.at[far], m.attended_grad.at[far], at.sibling
+        )
+        sides["ext_far"].wait()
+        sides["ext_pass"] = side(13, m.query_ext.at[far], m.query_ext.at[far], at.sibling)
+
+    def far_ready():
+        sides["grad_pass"].wait()
+        sides["ext_pass"].wait()
+
+    def keys_ready():
+        sides["keys"].wait()
+        sides["values"].wait()
 
     def keep_input(rows, back):
         input_grad[0, rows, :] = back.astype(BF)
 
-    norm_back(
-        lambda rows: m.attn_grad[rows, :],
-        lambda rows: m.resid_grad[rows, :],
-        attn_gain,
-        m.hat1,
-        m.fac1,
-        m.vec,
-        (0, 1),
-        keep_input,
-    )
-
-    def vec_start(s):
+    def input_back():
+        m.attn_grad[...] = dot_rt(m.qkv_low[...], m.qkv_w[...])
+        norm_back(
+            lambda rows: m.attn_grad[rows, :],
+            lambda rows: m.resid_grad[rows, :],
+            attn_gain,
+            m.hat1,
+            m.fac1,
+            m.vec,
+            (0, 1),
+            keep_input,
+        )
+
+    def vec_step(s):
+        if s > 0:
+            sides["vec"].wait()
+            m.vec[...] = m.vec[...] + m.vec_came[s - 1]
+        if s > DIMS:
+            vec_out[...] = m.vec[...]
+            return
         copy = pltpu.make_async_remote_copy(
             src_ref=m.vec,
             dst_ref=m.vec_came.at[s],
@@ -644,46 +665,90 @@
             device_id_type=MESH,
         )
         copy.start()
-        return copy
-
-    vec_copy = [vec_start(0)]
-
-    def vec_finish(s):
-        vec_copy[0].wait()
-        m.vec[...] = m.vec[...] + m.vec_came[s]
-        if s < DIMS:
-            vec_copy[0] = vec_start(s + 1)
+        sides["vec"] = copy
+
+    def feed_out():
+        m.out_part[...] = dot(m.hidden[...], m.down_w[...])
+        sides["out"] = side(7, m.out_part.at[two_other], m.out_came, at.sibling)
+
+    def close():
+        sides["out"].wait()
+        block_output[0] = (
+            m.resid[...] + (m.out_part[two, :] + m.out_came[...]) + down_bias[...]
+        ).astype(BF)
+
+    near, other_chip = at.chip, 1 - at.chip
+    pieces = dict(
+        mlp_back=mlp_back,
+        resid_back=resid_back,
+        extend=extend,
+        query1=lambda: query_side(range(3)),
+        query2=lambda: query_side(range(3, 6)),
+        near_ready=near_ready,
+        near1=lambda: key_side(near, True, range(3)),
+        near2=lambda: key_side(near, True, range(3, 6)),
+        proj_ready=proj_ready,
+        far_here=far_here,
+        far_ready=far_ready,
+        far1=lambda: key_side(other_chip, False, range(3)),
+        far2=lambda: key_side(other_chip, False, range(3, 6)),
+        keys_ready=keys_ready,
+        input_back=input_back,
+        feed_out=feed_out,
+        close=close,
+    )
+    for step in PLAN:
+        if isinstance(step, str):
+            pieces[step]()
+        elif len(step) == 1:
+            vec_step(step[0])
+        elif len(step) == 2:
+            start(*step)
         else:
-            vec_out[...] = m.vec[...]
-
-    ex.finish(PROJ, 1)
-    ex.finish(KEYS, 0)
-    m.out_part[...] = dot(m.hidden[...], m.down_w[...])
-    out_sib = side(7, m.out_part.at[two_other], m.out_came, at.sibling)
-    ex.finish(UP, 2)
-    ex.finish(PROJ, 2)
-    ex.finish(DOWN, 4)
-    out_sib.wait()
-    block_output[0] = (
-        m.resid[...] + (m.out_part[two, :] + m.out_came[...]) + down_bias[...]
-    ).astype(BF)
-
-    for n, (w, s) in enumerate(LAST):
-        ex.finish(w, s)
-        if n % 3 == 0 and n // 3 <= DIMS:
-            vec_finish(n // 3)
+            ex.finish(*step)
 
     for w in range(len(WIDTHS)):
-        for k in range(DIMS):
-            for part in range(2):
-                ex.copies[w, k, STEPS + part].wait()
-
-
-LAST = (
-    (KEYS, 1), (PROJ, 3), (UP, 3), (DOWN, 5), (KEYS, 2), (PROJ, 4), (UP, 4),
-    (DOWN, 6), (KEYS, 3), (PROJ, 5), (UP, 5), (PROJ, 6), (KEYS, 4), (UP, 6),
-    (DOWN, 7), (PROJ, 7), (KEYS, 5), (UP, 7), (DOWN, 8), (KEYS, 6), (PROJ, 8),
-    (UP, 8), (KEYS, 7), (DOWN, 9), (KEYS, 8), (PROJ, 9), (UP, 9), (KEYS, 9),
+        ex.done(w)
+
+
+PLAN = (
+    (0, 4), (0, 5), (1, 1), "mlp_back", (1, 2), (0, 1), (1, 0), (0, 2),
+    (1, 3), (0, 0), "resid_back", "extend", (0, 3), "query1", "query2", (1, 5),
+    (1, 1, 0), (0, 4, 0), "near_ready", "near1", "proj_ready", (1, 2, 0), (2, 4), (2, 3),
+    (1, 4), (1, 3, 0), (2, 2), (0, 5, 0), (2, 1), (1, 0, 0), (2, 0), (0, 1, 0),
+    (2, 5), "far_here", (0, 2, 0), "near2", (0, 0, 0), "far_ready", "far1", "far2",
+    (1, 5, 0), (1, 1, 1), "input_back", "keys_ready", (3, 5), (3, 1), (3, 2), (2, 3, 0),
+    (3, 0), (2, 0, 0), (0, 3, 0), (1, 2, 1), (3, 3), (0, 4, 1), (2, 4, 0), (1, 0, 1),
+    (0, 1, 1), (1, 4, 0), (1, 1, 2), (2, 1, 0), (0, 0, 1), (0, 2, 1), (1, 3, 1), (2, 2, 0),
+    (1, 5, 1), (2, 3, 1), (0, 5, 1), (2, 5, 0), (3, 1, 0), (3, 0, 0), (2, 0, 1), (3, 3, 0),
+    (2, 4, 1), (3, 5, 0), (0, 4, 2), (0, 3, 1), (3, 4), (2, 1, 1), (1, 2, 2), (1, 4, 1),
+    (1, 0, 2), (1, 5, 2), (0, 0, 2), (2, 5, 1), (1, 1, 3), (1, 3, 2), (3, 2, 0), (2, 2, 1),
+    (3, 1, 1), (2, 4, 2), (2, 3, 2), (0, 1, 2), (2, 0, 2), (0, 5, 2), (0, 2, 2), (0, 4, 3),
+    (3, 0, 1), (0, 3, 2), (3, 3, 1), (1, 0, 3), (1, 2, 3), (1, 4, 2), (0,), (2, 5, 2),
+    (3, 4, 0), (1, 5, 3), (1, 3, 3), (2, 2, 2), (2, 1, 2), (3, 2, 1), (2, 3, 3), (0, 1, 3),
+    (3, 5, 1), (0, 0, 3), (0, 2, 3), (0, 3, 3), (0, 5, 3), (1, 1, 4), (3, 0, 2), (1, 2, 4),
+    (1, 4, 3), (2, 0, 3), (0, 4, 4), (2, 5, 3), (3, 3, 2), (2, 1, 3), (1,), (2, 3, 4),
+    (3, 1, 2), (1, 3, 4), (3, 4, 1), (1, 5, 4), (3, 5, 2), (0, 0, 4), (0, 3, 4), (0, 1, 4),
+    (0, 2, 4), (0, 5, 4), (1, 0, 4), (3, 0, 3), (1, 4, 4), (3, 2, 2), (0, 4, 5), (2, 1, 4),
+    (1, 2, 5), (2, 3, 5), (2, 4, 3), (2, 0, 4), (1, 3, 5), (1, 1, 5), (3, 5, 3), (3, 4, 2),
+    (0, 0, 5), (1, 5, 5), (2, 2, 3), (2, 5, 4), (3, 1, 3), (0, 2, 5), (0, 5, 5), (3, 3, 3),
+    (0, 1, 5), (1, 4, 5), (1, 0, 5), (2,), (0, 3, 5), (0, 4, 6), (2, 3, 6), (2, 1, 5),
+    (3, 0, 4), (1, 2, 6), (2, 4, 4), (1, 3, 6), (1, 1, 6), (3, 4, 3), (3, 5, 4), (0, 0, 6),
+    (1, 5, 6), (2, 0, 5), (2, 5, 5), (3, 1, 4), (3, 2, 3), (0, 2, 6), (2, 2, 4), (0, 5, 6),
+    (0, 1, 6), (1, 4, 6), (1, 0, 6), (2, 3, 7), (0, 3, 6), (2, 1, 6), (2, 4, 5), (3, 4, 4),
+    (0, 4, 7), (1, 2, 7), (3,), (3, 5, 5), (1, 3, 7), (1, 1, 7), (3, 2, 4), (1, 5, 7),
+    (0, 0, 7), (3, 3, 4), (3, 1, 5), (3, 0, 5), (2, 2, 5), "feed_out", (0, 5, 7), (2, 0, 6),
+    (0, 3, 7), (1, 4, 7), (3, 4, 5), (1, 0, 7), (0, 1, 7), (0, 2, 7), (2, 4, 6), (3, 5, 6),
+    (2, 5, 6), (0, 4, 8), (1, 3, 8), (3, 2, 5), (1, 5, 8), (3, 3, 5), (0, 0, 8), (2, 0, 7),
+    (3, 0, 6), (1, 2, 8), (2, 3, 8), (2, 2, 6), (3, 4, 6), (2, 1, 7), (1, 1, 8), (3, 3, 6),
+    (3, 5, 7), (2, 4, 7), (3, 2, 6), (1, 0, 8), (0, 5, 8), (3, 1, 6), (0, 2, 8), (3, 0, 7),
+    (1, 4, 8), (2, 2, 7), (3, 2, 7), (1, 3, 9), (0, 1, 8), (0, 3, 8), (1, 1, 9), (1, 2, 9),
+    (4,), (3, 3, 7), (3, 4, 7), (2, 5, 7), (3, 5, 8), (3, 0, 8), (2, 4, 8), (2, 1, 8),
+    (0, 0, 9), (2, 0, 8), (3, 1, 7), (1, 4, 9), (0, 4, 9), (2, 2, 8), (2, 3, 9), (3, 2, 8),
+    (0, 5, 9), (1, 5, 9), (5,), (3, 4, 8), (3, 3, 8), (0, 2, 9), (1, 0, 9), (2, 5, 8),
+    (3, 1, 8), (0, 1, 9), (2, 2, 9), (2, 4, 9), (3, 0, 9), (2, 1, 9), (6,), (3, 5, 9),
+    (0, 3, 9), (3, 4, 9), (3, 3, 9), (3, 2, 9), (2, 0, 9), (2, 5, 9), (3, 1, 9), (7,),
+    "close",
 )
 
 
@@ -794,7 +859,6 @@
     down_bias,
 ):
     vmem = pl.BlockSpec(memory_space=pltpu.VMEM)
-    smem = pl.BlockSpec(memory_space=pltpu.SMEM)
     hbm = pl.BlockSpec(memory_space=pl.ANY)
     held = scratch()
     block_output, input_grad, wide, slim, vec = pl.pallas_call(
@@ -806,7 +870,7 @@
             pltpu.VMEM((2, 2, WIDTH, WIDTH), BF),
             pltpu.VMEM((16, WIDTH), F32),
         ],
-        in_specs=[smem, smem] + [vmem] * 11 + [hbm] * 4,
+        in_specs=[pl.BlockSpec(memory_space=pltpu.SMEM)] * 2 + [vmem] * 11 + [hbm] * 4,
         out_specs=[vmem] * 5,
         scratch_shapes=[held[name] for name in NAMES],
         compiler_params=pltpu.CompilerParams(

time: 117 us -> 108 us (0.923)
  Pallas kernels: 116 us -> 107 us
    pallas_call x1, Pallas kernels: 106 us -> 96.8 us  [body(): pl.pallas_call(kernel, out_shape=[pltpu.VMEM((1, TOK, WIDTH), BF), pltpu....]
where the time goes in v4:
time: 108 us
  Pallas kernels  107 us (99%)
    pallas_call x1, Pallas kernels, body(): pl.pallas_call(kernel, out_shape=[pltpu.VMEM((1, TOK, WIDTH), BF), pltpu....  96.8 us
    pallas_call x1, Pallas kernels, spread(): pl.pallas_call(spread_kernel, grid=(WIDTH // rows,), out_shape=[o[0] for...  10.1 us

profile of v4, /device:TPU:1, one launch (start us, length us, event | category | flops | bytes accessed | tf_op | source)
XLA Modules:
  0.0 107.7 jit_solution(18013393892783753818)
XLA Ops:
  0.7 96.8 %shard_map.280 = (bf16[1,128,768]{2,1,0:T(8,128)(2,1)S(1)}, bf16[1,128,768]{2,1,0:T(8,128)(2,1)S(1)}, bf16[2,2,768,1536]{3,2,1,0:T(8,128)(2,1)S(1)}, bf16[2,2,768,768]{3,2,1,0:T(8,128)(2,1)S(1)}, f32[16,768]{1,0:T(8,128)S(1)}) custom-call(s32[1,4]{1,0:T(1,128)} %lengths.1, s32[1,4]{1,0:T(1,128)} %order.1, bf16[1,128,768]{2,1,0:T(8,128)(2,1)} %x.1, ...), custom_call_target="tpu_custom_call" | custom-call | tf_op jit(solution)/shard_map/pallas_call | solution.py:864
  97.5 10.1 %shard_map.281 = (bf16[1,128,768]{2,1,0:T(8,128)(2,1)}, bf16[1,128,768]{2,1,0:T(8,128)(2,1)}, f32[768]{0:T(1024)}, f32[768]{0:T(1024)}, f32[768,2304]{1,0:T(8,12...) custom-call(bf16[2,2,768,1536]{3,2,1,0:T(8,128)(2,1)S(1)} %get-tuple, ...), custom_call_target="tpu_custom_call" | custom-call | tf_op jit(solution)/shard_map/pallas_call | solution.py:832

commit v5 on v4

--- a/solution.py
+++ b/solution.py
@@ -19,9 +19,9 @@
 EPSILON = 1e-6
 
 DIMS = 6
-STEPS = 10
 DOWN, UP, PROJ, KEYS = range(4)
 WIDTHS = (HALF, HALF, WIDTH, WIDTH)
+HALVINGS = (4, 3, 3, 3)
 
 TAIL = (
     0.14361835615286447,
@@ -113,19 +113,24 @@
         ]
 
     def slot(self, w, k, s):
+        held = self.landing[w].at[k]
         if s < 3:
-            return self.landing[w].at[k, pl.ds((0, 64, 96)[s], 64 >> s)]
+            return held.at[pl.ds((0, 64, 96)[s], 64 >> s)]
+        if HALVINGS[w] == 3:
+            return held.at[pl.ds(64 + 16 * s, 16)]
         width = WIDTHS[w] // 2
-        return self.landing[w].at[k, pl.ds((112, 112, 128)[s - 3], 16), pl.ds((0, width, 0)[s - 3], width)]
+        return held.at[pl.ds((112, 112, 128)[s - 3], 16), pl.ds((0, width, 0)[s - 3], width)]
 
     def start(self, w, k, s=0):
-        if s < 4:
+        last = HALVINGS[w] - 1
+        if s <= last:
             src, dst, d = self.block(w, k, s, False), self.slot(w, k, s), self.dim(k, s)
-        elif s < 6:
-            src, dst, d = self.block(w, k, 3, True), self.slot(w, k, s), self.dim(k, s)
+        elif s < DIMS:
+            src, dst, d = self.block(w, k, last, True), self.slot(w, k, s), self.dim(k, s)
         else:
-            src = dst = self.block(w, k, 9 - s, True, True)
-            d = self.dim(k, 9 - s)
+            t = last + DIMS - s
+            src = dst = self.block(w, k, t, True, True)
+            d = self.dim(k, t)
         copy = pltpu.make_async_remote_copy(
             src_ref=src,
             dst_ref=dst,
@@ -155,18 +160,19 @@
         self.crossing(w, self.whole[w].at[self.at.core], self.whole[w].at[1 - self.at.core]).wait()
 
     def finish(self, w, k, s):
+        steps, last = DIMS + HALVINGS[w], HALVINGS[w] - 1
         self.copies[w, k, s].wait()
-        if s < 6:
-            kept, slot = self.block(w, k, min(s, 3), True), self.slot(w, k, s)
+        if s < DIMS:
+            kept, slot = self.block(w, k, min(s, last), True), self.slot(w, k, s)
             total = (kept[...].astype(F32) + slot[...].astype(F32)).astype(BF)
-            if s < 5:
+            if s < DIMS - 1:
                 kept[...] = total
             else:
-                self.block(w, k, 3, True, True)[...] = total
-        if s < STEPS - 1:
+                self.block(w, k, last, True, True)[...] = total
+        if s < steps - 1:
             self.start(w, k, s + 1)
-        if s >= STEPS - 2:
-            self.over(w, k, s - (STEPS - 2))
+        if s >= steps - 2:
+            self.over(w, k, s - (steps - 2))
 
 
 def normalize(load, gain, shift, normed, factor, result, base):
@@ -217,6 +223,7 @@
         down_w=v((HALF, WIDTH), BF),
         lines=v((8, WIDTH), F32),
         up_bias_half=v((1, HALF), F32),
+        up_sum=v((1, HALF), F32),
         normed_in=v((LEN, WIDTH), BF),
         queries=v((LEN, WIDTH), BF),
         keys=v((LEN, WIDTH), BF),
@@ -254,13 +261,13 @@
         vec_came=v((DIMS + 1, 16, WIDTH), F32),
         grads_wide=v((2, WIDTH, HALF), BF),
         grads_slim=v((2, WIDTH, WIDTH), BF),
-        landing_wide=v((2, DIMS, 144, HALF), BF),
-        landing_slim=v((2, DIMS, 144, WIDTH), BF),
+        landing_wide=v((2, DIMS, 160, HALF), BF),
+        landing_slim=v((2, DIMS, 160, WIDTH), BF),
         send_sem=dma((sets, DIMS)),
-        recv_sem=dma((sets, DIMS, STEPS)),
+        recv_sem=dma((sets, DIMS, DIMS + max(HALVINGS))),
         over_sem=dma((2, sets)),
-        side_send=dma((18,)),
-        side_recv=dma((18,)),
+        side_send=dma((20,)),
+        side_recv=dma((20,)),
         vec_send=dma((DIMS + 1,)),
         vec_recv=dma((DIMS + 1,)),
         load_sem=dma((4,)),
@@ -343,7 +350,8 @@
     own = rows_of(seq * TOK, TOK)
     two = rows_of(core * TOK, TOK)
     two_other = rows_of((1 - core) * TOK, TOK)
-    far = rows_of(((1 - at.chip) * 2 + core) * TOK, TOK)
+    far_block = (1 - at.chip) * 2 + core
+    far = rows_of(far_block * TOK, TOK)
     chip_rows = lambda chip: rows_of(chip * 2 * TOK, 2 * TOK)
     cut = lambda start, size: pl.ds(pl.multiple_of(start, 128), size)
 
@@ -360,7 +368,10 @@
     m.cot2[two, :] = cot[0]
 
     pl.semaphore_wait(barrier, DIMS + 2)
-    in_far = side(1, m.normed_in.at[own], m.normed_in.at[own], at.across)
+    in_far = []
+    for i in range(2):
+        piece = m.normed_in.at[rows_of((seq * 2 + i) * 64, 64)]
+        in_far.append(side((1, 18)[i], piece, piece, at.across))
     in_sib = side(0, m.normed_in.at[own], m.normed_in.at[own], at.sibling)
     cot_sib = side(3, m.cot2.at[two], m.cot2.at[two], at.sibling)
 
@@ -397,23 +408,31 @@
     def beside(a, b):
         return jnp.concatenate((a, b), axis=1)
 
-    def project(chip):
-        rows = chip_rows(chip)
+    def project_keys(rows):
         a = m.normed_in[rows, :]
         m.keys[rows, :] = dot(a, m.qkv_w[:, WIDTH : 2 * WIDTH]).astype(BF)
         m.values[rows, :] = (dot(a, m.qkv_w[:, 2 * WIDTH :]) + value_bias[...]).astype(BF)
-        m.queries[rows, :] = ((dot(a, m.qkv_w[:, :WIDTH]) + query_bias[...]) * SCALE).astype(BF)
+
+    def project_queries(rows):
+        part = dot(m.normed_in[rows, :], m.qkv_w[:, :WIDTH])
+        m.queries[rows, :] = ((part + query_bias[...]) * SCALE).astype(BF)
 
     loads[0].wait()
     in_sib.wait()
-    project(at.chip)
+    project_keys(chip_rows(at.chip))
+    project_queries(chip_rows(at.chip))
     loads[1].wait()
     cot_sib.wait()
     m.hidden_grad[...] = dot_rt(m.cot2[...], m.down_w[...])
-    in_far.wait()
-    in_pass = side(2, m.normed_in.at[far], m.normed_in.at[far], at.sibling)
-    in_pass.wait()
-    project(1 - at.chip)
+    in_pass = []
+    for i in range(2):
+        in_far[i].wait()
+        piece = m.normed_in.at[rows_of((far_block * 2 + i) * 64, 64)]
+        in_pass.append(side((2, 19)[i], piece, piece, at.sibling))
+    project_keys(far)
+    for copy in in_pass:
+        copy.wait()
+    project_keys(rows_of(((1 - at.chip) * 2 + 1 - core) * TOK, TOK))
 
     def attend(i, carry):
         cols = rows_of(i * 128, 128)
@@ -443,27 +462,28 @@
     mlp_sib = side(4, m.mlp_in.at[two], m.mlp_in.at[two], at.sibling)
     att_sib = side(5, m.attended.at[two], m.attended.at[two], at.sibling)
     loads[3].wait()
+
+    def feed(rows, first):
+        for i in range(3):
+            cols = slice(i * 512, (i + 1) * 512)
+            u = dot(m.mlp_in[rows, :], m.up_w[:, cols]) + m.up_bias_half[:, cols]
+            t = 1.0 / (1.0 + 0.36 * jnp.abs(u))
+            tail = jnp.full_like(t, TAIL[-1])
+            for c in TAIL[-2::-1]:
+                tail = tail * t + c
+            e = jnp.exp(-0.5 * (u * u))
+            tail = tail * (t * e)
+            phi = jnp.where(u >= 0, 1.0 - tail, tail)
+            m.hidden[rows, cols] = (u * phi).astype(BF)
+            g = m.hidden_grad[rows, cols] * (phi + u * (DENSITY * e))
+            m.up_low[rows, cols] = g.astype(BF)
+            total = jnp.sum(g.reshape(TOK // 8, 8, 512), axis=0)
+            total = jnp.sum(total, axis=0, keepdims=True)
+            m.up_sum[:, cols] = total if first else m.up_sum[:, cols] + total
+
+    feed(two, True)
     mlp_sib.wait()
-
-    def feed(i, carry):
-        cols = rows_of(i * 512, 512)
-        u = dot(m.mlp_in[...], m.up_w[:, cols]) + m.up_bias_half[:, cols]
-        t = 1.0 / (1.0 + 0.36 * jnp.abs(u))
-        tail = jnp.full_like(t, TAIL[-1])
-        for c in TAIL[-2::-1]:
-            tail = tail * t + c
-        e = jnp.exp(-0.5 * (u * u))
-        tail = tail * (t * e)
-        phi = jnp.where(u >= 0, 1.0 - tail, tail)
-        m.hidden[:, cols] = (u * phi).astype(BF)
-        g = m.hidden_grad[:, cols] * (phi + u * (DENSITY * e))
-        m.up_low[:, cols] = g.astype(BF)
-        m.up_bias_half[:, cols] = jnp.sum(
-            jnp.sum(g.reshape(2 * TOK // 8, 8, 512), axis=0), axis=0, keepdims=True
-        )
-        return carry
-
-    lax.fori_loop(0, HALF // 512, feed, 0)
+    feed(two_other, False)
 
     def block_of(k):
         return slice(k * TOK, (k + 1) * TOK)
@@ -497,7 +517,7 @@
         for h in range(2):
             for t in range(2):
                 m.vec[8 + 2 * h + t : 9 + 2 * h + t, :] = jnp.where(
-                    core == h, m.up_bias_half[:, t * WIDTH : (t + 1) * WIDTH], 0.0
+                    core == h, m.up_sum[:, t * WIDTH : (t + 1) * WIDTH], 0.0
                 )
 
     def keep_resid(rows, back):
@@ -618,6 +638,7 @@
         sides["query"].wait()
 
     def far_here():
+        project_queries(chip_rows(1 - at.chip))
         sides["grad_far"].wait()
         sides["grad_pass"] = side(
             10, m.attended_grad.at[far], m.attended_grad.at[far], at.sibling
@@ -712,43 +733,40 @@
 
 
 PLAN = (
-    (0, 4), (0, 5), (1, 1), "mlp_back", (1, 2), (0, 1), (1, 0), (0, 2),
-    (1, 3), (0, 0), "resid_back", "extend", (0, 3), "query1", "query2", (1, 5),
-    (1, 1, 0), (0, 4, 0), "near_ready", "near1", "proj_ready", (1, 2, 0), (2, 4), (2, 3),
-    (1, 4), (1, 3, 0), (2, 2), (0, 5, 0), (2, 1), (1, 0, 0), (2, 0), (0, 1, 0),
-    (2, 5), "far_here", (0, 2, 0), "near2", (0, 0, 0), "far_ready", "far1", "far2",
-    (1, 5, 0), (1, 1, 1), "input_back", "keys_ready", (3, 5), (3, 1), (3, 2), (2, 3, 0),
-    (3, 0), (2, 0, 0), (0, 3, 0), (1, 2, 1), (3, 3), (0, 4, 1), (2, 4, 0), (1, 0, 1),
-    (0, 1, 1), (1, 4, 0), (1, 1, 2), (2, 1, 0), (0, 0, 1), (0, 2, 1), (1, 3, 1), (2, 2, 0),
-    (1, 5, 1), (2, 3, 1), (0, 5, 1), (2, 5, 0), (3, 1, 0), (3, 0, 0), (2, 0, 1), (3, 3, 0),
-    (2, 4, 1), (3, 5, 0), (0, 4, 2), (0, 3, 1), (3, 4), (2, 1, 1), (1, 2, 2), (1, 4, 1),
-    (1, 0, 2), (1, 5, 2), (0, 0, 2), (2, 5, 1), (1, 1, 3), (1, 3, 2), (3, 2, 0), (2, 2, 1),
-    (3, 1, 1), (2, 4, 2), (2, 3, 2), (0, 1, 2), (2, 0, 2), (0, 5, 2), (0, 2, 2), (0, 4, 3),
-    (3, 0, 1), (0, 3, 2), (3, 3, 1), (1, 0, 3), (1, 2, 3), (1, 4, 2), (0,), (2, 5, 2),
-    (3, 4, 0), (1, 5, 3), (1, 3, 3), (2, 2, 2), (2, 1, 2), (3, 2, 1), (2, 3, 3), (0, 1, 3),
-    (3, 5, 1), (0, 0, 3), (0, 2, 3), (0, 3, 3), (0, 5, 3), (1, 1, 4), (3, 0, 2), (1, 2, 4),
-    (1, 4, 3), (2, 0, 3), (0, 4, 4), (2, 5, 3), (3, 3, 2), (2, 1, 3), (1,), (2, 3, 4),
-    (3, 1, 2), (1, 3, 4), (3, 4, 1), (1, 5, 4), (3, 5, 2), (0, 0, 4), (0, 3, 4), (0, 1, 4),
-    (0, 2, 4), (0, 5, 4), (1, 0, 4), (3, 0, 3), (1, 4, 4), (3, 2, 2), (0, 4, 5), (2, 1, 4),
-    (1, 2, 5), (2, 3, 5), (2, 4, 3), (2, 0, 4), (1, 3, 5), (1, 1, 5), (3, 5, 3), (3, 4, 2),
-    (0, 0, 5), (1, 5, 5), (2, 2, 3), (2, 5, 4), (3, 1, 3), (0, 2, 5), (0, 5, 5), (3, 3, 3),
-    (0, 1, 5), (1, 4, 5), (1, 0, 5), (2,), (0, 3, 5), (0, 4, 6), (2, 3, 6), (2, 1, 5),
-    (3, 0, 4), (1, 2, 6), (2, 4, 4), (1, 3, 6), (1, 1, 6), (3, 4, 3), (3, 5, 4), (0, 0, 6),
-    (1, 5, 6), (2, 0, 5), (2, 5, 5), (3, 1, 4), (3, 2, 3), (0, 2, 6), (2, 2, 4), (0, 5, 6),
-    (0, 1, 6), (1, 4, 6), (1, 0, 6), (2, 3, 7), (0, 3, 6), (2, 1, 6), (2, 4, 5), (3, 4, 4),
-    (0, 4, 7), (1, 2, 7), (3,), (3, 5, 5), (1, 3, 7), (1, 1, 7), (3, 2, 4), (1, 5, 7),
-    (0, 0, 7), (3, 3, 4), (3, 1, 5), (3, 0, 5), (2, 2, 5), "feed_out", (0, 5, 7), (2, 0, 6),
-    (0, 3, 7), (1, 4, 7), (3, 4, 5), (1, 0, 7), (0, 1, 7), (0, 2, 7), (2, 4, 6), (3, 5, 6),
-    (2, 5, 6), (0, 4, 8), (1, 3, 8), (3, 2, 5), (1, 5, 8), (3, 3, 5), (0, 0, 8), (2, 0, 7),
-    (3, 0, 6), (1, 2, 8), (2, 3, 8), (2, 2, 6), (3, 4, 6), (2, 1, 7), (1, 1, 8), (3, 3, 6),
-    (3, 5, 7), (2, 4, 7), (3, 2, 6), (1, 0, 8), (0, 5, 8), (3, 1, 6), (0, 2, 8), (3, 0, 7),
-    (1, 4, 8), (2, 2, 7), (3, 2, 7), (1, 3, 9), (0, 1, 8), (0, 3, 8), (1, 1, 9), (1, 2, 9),
-    (4,), (3, 3, 7), (3, 4, 7), (2, 5, 7), (3, 5, 8), (3, 0, 8), (2, 4, 8), (2, 1, 8),
-    (0, 0, 9), (2, 0, 8), (3, 1, 7), (1, 4, 9), (0, 4, 9), (2, 2, 8), (2, 3, 9), (3, 2, 8),
-    (0, 5, 9), (1, 5, 9), (5,), (3, 4, 8), (3, 3, 8), (0, 2, 9), (1, 0, 9), (2, 5, 8),
-    (3, 1, 8), (0, 1, 9), (2, 2, 9), (2, 4, 9), (3, 0, 9), (2, 1, 9), (6,), (3, 5, 9),
-    (0, 3, 9), (3, 4, 9), (3, 3, 9), (3, 2, 9), (2, 0, 9), (2, 5, 9), (3, 1, 9), (7,),
-    "close",
+    (0, 4), (0, 5), (0, 1), (1, 2), "mlp_back", (0, 0), (0, 3), (0, 2),
+    (1, 3), (1, 0), (1, 1), "resid_back", "extend", "query1", (1, 4), "query2",
+    (0, 5, 0), "near_ready", (1, 5), (0, 0, 0), (0, 3, 0), "proj_ready", (1, 2, 0), (2, 2),
+    "near1", (2, 1), (2, 0), (2, 5), "near2", (0, 2, 0), (0, 4, 0), "far_here",
+    (2, 3), (1, 1, 0), (2, 4), (0, 1, 0), (1, 0, 0), "far_ready", "far1", "far2",
+    (0, 0, 1), (1, 5, 0), (1, 3, 0), (2, 1, 0), (0, 5, 1), (1, 4, 0), "keys_ready", (2, 2, 0),
+    (2, 0, 0), (0, 2, 1), (3, 0), (3, 4), (3, 1), (2, 5, 0), (0, 3, 1), (1, 1, 1),
+    (3, 5), (1, 0, 1), "input_back", (3, 2), (0, 1, 1), (2, 4, 0), (3, 3), (0, 4, 1),
+    (1, 5, 1), (1, 4, 1), (0, 5, 2), (2, 2, 1), (2, 3, 0), (2, 0, 1), (3, 0, 0), (0, 0, 2),
+    (0, 3, 2), (3, 1, 0), (0,), (1, 3, 1), (2, 1, 1), (1, 1, 2), (1, 2, 1), (1, 0, 2),
+    (2, 5, 1), (0, 2, 2), (1, 5, 2), (0, 4, 2), (3, 5, 0), (3, 4, 0), (2, 2, 2), (0, 5, 3),
+    (1, 4, 2), (0, 1, 2), (3, 2, 0), (2, 4, 1), (3, 3, 0), (2, 3, 1), (0, 3, 3), (2, 1, 2),
+    (3, 1, 1), (1, 3, 2), (1,), (2, 5, 2), (1, 1, 3), (0, 0, 3), (0, 2, 3), (2, 0, 2),
+    (1, 0, 3), (0, 4, 3), (3, 0, 1), (3, 5, 1), (1, 2, 2), (1, 5, 3), (3, 4, 1), (1, 4, 3),
+    (2, 4, 2), (2, 2, 3), (0, 5, 4), (0, 1, 3), (2, 3, 2), (3, 2, 1), (3, 3, 1), (0, 3, 4),
+    (3, 1, 2), (2, 5, 3), (1, 3, 3), (2, 0, 3), (1, 1, 4), (0, 4, 4), (2, 1, 3), (3, 5, 2),
+    (0, 0, 4), (3, 0, 2), (0, 2, 4), (1, 2, 3), (2,), (1, 0, 4), (1, 4, 4), (2, 2, 4),
+    (0, 5, 5), (2, 4, 3), (2, 3, 3), (1, 5, 4), (0, 1, 4), (0, 3, 5), (3, 2, 2), (2, 5, 4),
+    (3, 3, 2), (3, 1, 3), (3, 4, 2), (3, 5, 3), (1, 3, 4), (0, 0, 5), (0, 2, 5), (0, 4, 5),
+    (3, 0, 3), (1, 1, 5), (2, 1, 4), (1, 2, 4), (1, 0, 5), (1, 4, 5), (2, 2, 5), (3,),
+    (2, 0, 4), (0, 1, 5), (0, 5, 6), (1, 5, 5), (2, 3, 4), (0, 3, 6), (3, 2, 3), (3, 5, 4),
+    (3, 4, 3), (2, 4, 4), (2, 5, 5), (0, 2, 6), (3, 1, 4), (0, 4, 6), (0, 0, 6), (2, 1, 5),
+    (3, 0, 4), (1, 3, 5), (1, 2, 5), (1, 0, 6), (1, 1, 6), (1, 4, 6), (2, 2, 6), (4,),
+    (0, 5, 7), (0, 1, 6), (3, 4, 4), (2, 0, 5), (0, 3, 7), (2, 3, 5), (3, 2, 4), (3, 1, 5),
+    (2, 1, 6), (3, 3, 3), (0, 2, 7), (0, 4, 7), (0, 0, 7), (2, 4, 5), (1, 3, 6), (1, 5, 6),
+    (1, 2, 6), (3, 0, 5), (2, 2, 7), (2, 5, 6), (3, 5, 5), (3, 2, 5), (0, 5, 8), (2, 0, 6),
+    (3, 3, 4), (1, 4, 7), (0, 3, 8), (0, 1, 7), (1, 1, 7), (3, 4, 5), (1, 0, 7), "feed_out",
+    (3, 1, 6), (0, 2, 8), (2, 3, 6), (3, 3, 5), (3, 2, 6), (5,), (0, 4, 8), (2, 0, 7),
+    (3, 5, 6), (2, 4, 6), (3, 4, 6), (1, 3, 7), (1, 5, 7), (1, 2, 7), (3, 0, 6), (0, 0, 8),
+    (2, 1, 7), (1, 1, 8), (3, 3, 6), (0, 5, 9), (0, 1, 8), (2, 2, 8), (3, 1, 7), (0, 3, 9),
+    (3, 4, 7), (2, 4, 7), (2, 3, 7), (6,), (1, 0, 8), (1, 4, 8), (0, 2, 9), (3, 5, 7),
+    "close", (2, 5, 7), (2, 0, 8), (3, 2, 7), (0, 4, 9), (3, 0, 7), (3, 3, 7), (7,),
+    (2, 1, 8), (1, 3, 8), (1, 5, 8), (1, 2, 8), (0, 0, 9), (0, 1, 9), (3, 4, 8), (2, 3, 8),
+    (3, 5, 8), (3, 2, 8), (3, 1, 8), (3, 0, 8), (2, 4, 8), (3, 3, 8), (2, 5, 8),
 )
 
 

time: 108 us -> 102 us (0.944)
  Pallas kernels: 107 us -> 101 us
    pallas_call x1, Pallas kernels: 96.8 us -> 91 us  [body(): pl.pallas_call(kernel, out_shape=[pltpu.VMEM((1, TOK, WIDTH), BF), pltpu....]
where the time goes in v5:
time: 102 us
  Pallas kernels  101 us (99%)
    pallas_call x1, Pallas kernels, body(): pl.pallas_call(kernel, out_shape=[pltpu.VMEM((1, TOK, WIDTH), BF), pltpu....  91 us
    pallas_call x1, Pallas kernels, spread(): pl.pallas_call(spread_kernel, grid=(WIDTH // rows,), out_shape=[o[0] for...  10.1 us

profile of v5, /device:TPU:1, one launch (start us, length us, event | category | flops | bytes accessed | tf_op | source)
XLA Modules:
  0.0 101.9 jit_solution(6101670488043777869)
XLA Ops:
  0.7 91.0 %shard_map.280 = (bf16[1,128,768]{2,1,0:T(8,128)(2,1)S(1)}, bf16[1,128,768]{2,1,0:T(8,128)(2,1)S(1)}, bf16[2,2,768,1536]{3,2,1,0:T(8,128)(2,1)S(1)}, bf16[2,2,768,768]{3,2,1,0:T(8,128)(2,1)S(1)}, f32[16,768]{1,0:T(8,128)S(1)}) custom-call(s32[1,4]{1,0:T(1,128)} %lengths.1, s32[1,4]{1,0:T(1,128)} %order.1, bf16[1,128,768]{2,1,0:T(8,128)(2,1)} %x.1, ...), custom_call_target="tpu_custom_call" | custom-call | tf_op jit(solution)/shard_map/pallas_call | solution.py:882
  91.7 10.1 %shard_map.281 = (bf16[1,128,768]{2,1,0:T(8,128)(2,1)}, bf16[1,128,768]{2,1,0:T(8,128)(2,1)}, f32[768]{0:T(1024)}, f32[768]{0:T(1024)}, f32[768,2304]{1,0:T(8,12...) custom-call(bf16[2,2,768,1536]{3,2,1,0:T(8,128)(2,1)S(1)} %get-tuple, ...), custom_call_target="tpu_custom_call" | custom-call | tf_op jit(solution)/shard_map/pallas_call | solution.py:850

commit v6 on v5

--- a/solution.py
+++ b/solution.py
@@ -103,6 +103,14 @@
         held = self.whole[w].at[self.at.core] if whole else self.grads[w]
         bit = self.at.bits[self.dim(k, s)]
         pick = bit if mine else 1 - bit
+        if w == DOWN:
+            half = lambda p: pl.ds(pl.multiple_of(p * WIDTH, 128), WIDTH)
+            if s == 0:
+                return held.at[pl.ds(TOK * k, TOK), half(pick)]
+            low = TOK * k + pick * (64 >> (s - 1))
+            for t in range(1, s):
+                low = low + self.at.bits[self.dim(k, t)] * (64 >> (t - 1))
+            return held.at[pl.ds(pl.multiple_of(low, 16), 64 >> (s - 1)), half(self.at.bits[k])]
         if s < 3:
             size = 64 >> s
             return held.at[pl.ds(pl.multiple_of(self.rows(k, s) + pick * size, 16), size)]
@@ -114,6 +122,8 @@
 
     def slot(self, w, k, s):
         held = self.landing[w].at[k]
+        if w == DOWN:
+            return held.at[pl.ds((0, 64, 96, 112, 128)[s - 1], (64, 32, 16, 16, 16)[s - 1]), pl.ds(0, WIDTH)]
         if s < 3:
             return held.at[pl.ds((0, 64, 96)[s], 64 >> s)]
         if HALVINGS[w] == 3:
@@ -242,6 +252,8 @@
         cot2=v((2 * TOK, WIDTH), BF),
         hidden_grad=v((2 * TOK, HALF), F32),
         hidden=v((2 * TOK, HALF), BF),
+        cot_near=v((2, DIMS, TOK, WIDTH), BF),
+        hidden_near=v((DIMS, 2 * TOK, 128), BF),
         up_low=v((2 * TOK, HALF), BF),
         mlp_part=v((2 * TOK, WIDTH), F32),
         mlp_came=v((TOK, WIDTH), F32),
@@ -266,11 +278,13 @@
         send_sem=dma((sets, DIMS)),
         recv_sem=dma((sets, DIMS, DIMS + max(HALVINGS))),
         over_sem=dma((2, sets)),
-        side_send=dma((20,)),
-        side_recv=dma((20,)),
+        side_send=dma((22,)),
+        side_recv=dma((22,)),
         vec_send=dma((DIMS + 1,)),
         vec_recv=dma((DIMS + 1,)),
         load_sem=dma((4,)),
+        near_sem=dma((4,)),
+        slice_sem=dma((1 + DIMS,)),
     )
 
 
@@ -375,6 +389,19 @@
     in_sib = side(0, m.normed_in.at[own], m.normed_in.at[own], at.sibling)
     cot_sib = side(3, m.cot2.at[two], m.cot2.at[two], at.sibling)
 
+    def near_copy(i, src, dst, device):
+        return pltpu.make_async_remote_copy(
+            src_ref=src,
+            dst_ref=dst,
+            send_sem=m.near_sem.at[i],
+            recv_sem=m.near_sem.at[i + 1],
+            device_id=device,
+            device_id_type=MESH,
+        )
+
+    for d in range(DIMS):
+        near_copy(0, m.cot2.at[two], m.cot_near.at[core, d], at.partners[d]).start()
+
     ends = [lengths[0, 0]]
     for i in (1, 2):
         ends.append(ends[-1] + lengths[0, i])
@@ -461,7 +488,22 @@
     normalize(lambda rows: m.resid[rows, :], mlp_gain, mlp_shift, m.hat2, m.fac2, m.mlp_in, core * TOK)
     mlp_sib = side(4, m.mlp_in.at[two], m.mlp_in.at[two], at.sibling)
     att_sib = side(5, m.attended.at[two], m.attended.at[two], at.sibling)
+    near_copy(0, m.cot_near.at[core], m.cot_near.at[core], at.sibling).wait()
+    near_pass = near_copy(2, m.cot_near.at[core], m.cot_near.at[core], at.sibling)
+    near_pass.start()
     loads[3].wait()
+
+    def slice_copy(k, src, dst):
+        return pltpu.make_async_remote_copy(
+            src_ref=src,
+            dst_ref=dst,
+            send_sem=m.slice_sem.at[0],
+            recv_sem=m.slice_sem.at[1 + k],
+            device_id=at.partners[k],
+            device_id_type=MESH,
+        )
+
+    slices = []
 
     def feed(rows, first):
         for i in range(3):
@@ -480,6 +522,11 @@
             total = jnp.sum(g.reshape(TOK // 8, 8, 512), axis=0)
             total = jnp.sum(total, axis=0, keepdims=True)
             m.up_sum[:, cols] = total if first else m.up_sum[:, cols] + total
+            if not first:
+                for k in (2 * i, 2 * i + 1):
+                    units = cut(256 * k + 128 * (1 - at.bits[k]), 128)
+                    slices.append(slice_copy(k, m.hidden.at[:, units], m.hidden_near.at[k]))
+                    slices[k].start()
 
     feed(two, True)
     mlp_sib.wait()
@@ -491,12 +538,17 @@
     def start(w, k):
         block = block_of(k)
         if w == DOWN:
-            for h in range(2):
-                first = h * WIDTH + k * TOK
-                grads[w][block, h * WIDTH : (h + 1) * WIDTH] = dot_lt(
-                    m.hidden[:, first : first + TOK], m.cot2[...]
-                ).astype(BF)
-        elif w == UP:
+            if near_waits:
+                near_waits.pop().wait()
+            slices[k].wait_recv()
+            units = cut(256 * k + 128 * at.bits[k], 128)
+            total = dot_lt(m.hidden[:, units], m.cot2[...])
+            for c in range(2):
+                total = total + dot_lt(m.hidden_near[k, c * TOK : (c + 1) * TOK], m.cot_near[c, k])
+            grads[w][block, cut(at.bits[k] * WIDTH, WIDTH)] = total.astype(BF)
+            ex.start(w, k, 1)
+            return
+        if w == UP:
             grads[w][block, :] = dot_lt(m.mlp_in[:, block], m.up_low[...]).astype(BF)
         elif w == PROJ:
             grads[w][block, :384] = dot_lt(m.attended[:, block], m.resid_half[...]).astype(BF)
@@ -510,6 +562,7 @@
         ex.start(w, k)
 
     sides = {}
+    near_waits = [near_pass]
 
     def mlp_back():
         m.mlp_part[...] = dot_rt(m.up_low[...], m.up_w[...])
@@ -538,7 +591,9 @@
         )
         m.attended_grad[own, :] = dot_rt(m.resid_low[...], m.proj_w[...]).astype(BF)
         grad = m.attended_grad.at[own]
-        sides["grad_far"] = side(9, grad, grad, at.across)
+        for i in range(2):
+            piece = m.attended_grad.at[rows_of((seq * 2 + i) * 64, 64)]
+            sides["grad_far", i] = side((9, 20)[i], piece, piece, at.across)
         sides["grad_sib"] = side(8, grad, grad, at.sibling)
 
     def parts(v):
@@ -639,15 +694,16 @@
 
     def far_here():
         project_queries(chip_rows(1 - at.chip))
-        sides["grad_far"].wait()
-        sides["grad_pass"] = side(
-            10, m.attended_grad.at[far], m.attended_grad.at[far], at.sibling
-        )
+        for i in range(2):
+            sides["grad_far", i].wait()
+            piece = m.attended_grad.at[rows_of((far_block * 2 + i) * 64, 64)]
+            sides["grad_pass", i] = side((10, 21)[i], piece, piece, at.sibling)
         sides["ext_far"].wait()
         sides["ext_pass"] = side(13, m.query_ext.at[far], m.query_ext.at[far], at.sibling)
 
     def far_ready():
-        sides["grad_pass"].wait()
+        for i in range(2):
+            sides["grad_pass", i].wait()
         sides["ext_pass"].wait()
 
     def keys_ready():
@@ -730,43 +786,44 @@
 
     for w in range(len(WIDTHS)):
         ex.done(w)
+    slice_copy(0, m.hidden_near, m.hidden_near).wait_send()
 
 
 PLAN = (
-    (0, 4), (0, 5), (0, 1), (1, 2), "mlp_back", (0, 0), (0, 3), (0, 2),
-    (1, 3), (1, 0), (1, 1), "resid_back", "extend", "query1", (1, 4), "query2",
-    (0, 5, 0), "near_ready", (1, 5), (0, 0, 0), (0, 3, 0), "proj_ready", (1, 2, 0), (2, 2),
-    "near1", (2, 1), (2, 0), (2, 5), "near2", (0, 2, 0), (0, 4, 0), "far_here",
-    (2, 3), (1, 1, 0), (2, 4), (0, 1, 0), (1, 0, 0), "far_ready", "far1", "far2",
-    (0, 0, 1), (1, 5, 0), (1, 3, 0), (2, 1, 0), (0, 5, 1), (1, 4, 0), "keys_ready", (2, 2, 0),
-    (2, 0, 0), (0, 2, 1), (3, 0), (3, 4), (3, 1), (2, 5, 0), (0, 3, 1), (1, 1, 1),
-    (3, 5), (1, 0, 1), "input_back", (3, 2), (0, 1, 1), (2, 4, 0), (3, 3), (0, 4, 1),
-    (1, 5, 1), (1, 4, 1), (0, 5, 2), (2, 2, 1), (2, 3, 0), (2, 0, 1), (3, 0, 0), (0, 0, 2),
-    (0, 3, 2), (3, 1, 0), (0,), (1, 3, 1), (2, 1, 1), (1, 1, 2), (1, 2, 1), (1, 0, 2),
-    (2, 5, 1), (0, 2, 2), (1, 5, 2), (0, 4, 2), (3, 5, 0), (3, 4, 0), (2, 2, 2), (0, 5, 3),
-    (1, 4, 2), (0, 1, 2), (3, 2, 0), (2, 4, 1), (3, 3, 0), (2, 3, 1), (0, 3, 3), (2, 1, 2),
-    (3, 1, 1), (1, 3, 2), (1,), (2, 5, 2), (1, 1, 3), (0, 0, 3), (0, 2, 3), (2, 0, 2),
-    (1, 0, 3), (0, 4, 3), (3, 0, 1), (3, 5, 1), (1, 2, 2), (1, 5, 3), (3, 4, 1), (1, 4, 3),
-    (2, 4, 2), (2, 2, 3), (0, 5, 4), (0, 1, 3), (2, 3, 2), (3, 2, 1), (3, 3, 1), (0, 3, 4),
-    (3, 1, 2), (2, 5, 3), (1, 3, 3), (2, 0, 3), (1, 1, 4), (0, 4, 4), (2, 1, 3), (3, 5, 2),
-    (0, 0, 4), (3, 0, 2), (0, 2, 4), (1, 2, 3), (2,), (1, 0, 4), (1, 4, 4), (2, 2, 4),
-    (0, 5, 5), (2, 4, 3), (2, 3, 3), (1, 5, 4), (0, 1, 4), (0, 3, 5), (3, 2, 2), (2, 5, 4),
-    (3, 3, 2), (3, 1, 3), (3, 4, 2), (3, 5, 3), (1, 3, 4), (0, 0, 5), (0, 2, 5), (0, 4, 5),
-    (3, 0, 3), (1, 1, 5), (2, 1, 4), (1, 2, 4), (1, 0, 5), (1, 4, 5), (2, 2, 5), (3,),
-    (2, 0, 4), (0, 1, 5), (0, 5, 6), (1, 5, 5), (2, 3, 4), (0, 3, 6), (3, 2, 3), (3, 5, 4),
-    (3, 4, 3), (2, 4, 4), (2, 5, 5), (0, 2, 6), (3, 1, 4), (0, 4, 6), (0, 0, 6), (2, 1, 5),
-    (3, 0, 4), (1, 3, 5), (1, 2, 5), (1, 0, 6), (1, 1, 6), (1, 4, 6), (2, 2, 6), (4,),
-    (0, 5, 7), (0, 1, 6), (3, 4, 4), (2, 0, 5), (0, 3, 7), (2, 3, 5), (3, 2, 4), (3, 1, 5),
-    (2, 1, 6), (3, 3, 3), (0, 2, 7), (0, 4, 7), (0, 0, 7), (2, 4, 5), (1, 3, 6), (1, 5, 6),
-    (1, 2, 6), (3, 0, 5), (2, 2, 7), (2, 5, 6), (3, 5, 5), (3, 2, 5), (0, 5, 8), (2, 0, 6),
-    (3, 3, 4), (1, 4, 7), (0, 3, 8), (0, 1, 7), (1, 1, 7), (3, 4, 5), (1, 0, 7), "feed_out",
-    (3, 1, 6), (0, 2, 8), (2, 3, 6), (3, 3, 5), (3, 2, 6), (5,), (0, 4, 8), (2, 0, 7),
-    (3, 5, 6), (2, 4, 6), (3, 4, 6), (1, 3, 7), (1, 5, 7), (1, 2, 7), (3, 0, 6), (0, 0, 8),
-    (2, 1, 7), (1, 1, 8), (3, 3, 6), (0, 5, 9), (0, 1, 8), (2, 2, 8), (3, 1, 7), (0, 3, 9),
-    (3, 4, 7), (2, 4, 7), (2, 3, 7), (6,), (1, 0, 8), (1, 4, 8), (0, 2, 9), (3, 5, 7),
-    "close", (2, 5, 7), (2, 0, 8), (3, 2, 7), (0, 4, 9), (3, 0, 7), (3, 3, 7), (7,),
-    (2, 1, 8), (1, 3, 8), (1, 5, 8), (1, 2, 8), (0, 0, 9), (0, 1, 9), (3, 4, 8), (2, 3, 8),
-    (3, 5, 8), (3, 2, 8), (3, 1, 8), (3, 0, 8), (2, 4, 8), (3, 3, 8), (2, 5, 8),
+    "mlp_back", (1, 3), (1, 2), (1, 5), (1, 4), (1, 0), (1, 1), "resid_back",
+    "extend", "query1", "query2", (0, 5), "near_ready", (0, 1), (0, 2), (0, 4),
+    (0, 0), "proj_ready", (2, 0), (2, 3), "near1", (0, 3), (1, 1, 0), (1, 0, 0),
+    (2, 2), (1, 2, 0), (2, 1), "near2", (0, 5, 1), (1, 4, 0), (1, 5, 0), (2, 4),
+    (0, 2, 1), (0, 1, 1), (0, 0, 1), (2, 5), "far_here", (1, 1, 1), (2, 0, 0), (2, 3, 0),
+    (1, 0, 1), "far_ready", "far1", "far2", (1, 2, 1), (0, 4, 1), (2, 4, 0), (0, 0, 2),
+    (1, 5, 1), (2, 1, 0), (0, 3, 1), "keys_ready", (3, 0), (1, 3, 0), (3, 1), (0, 2, 2),
+    (0, 1, 2), (0, 5, 2), (3, 2), (2, 2, 0), (3, 4), (3, 3), (2, 3, 1), (1, 0, 2),
+    (1, 4, 1), (1, 2, 2), (2, 0, 1), (0, 4, 2), (2, 4, 1), (3, 5), (1, 5, 2), (2, 5, 0),
+    (1, 1, 2), "input_back", (0,), (3, 0, 0), (3, 1, 0), (0, 5, 3), (0, 2, 3), (1, 3, 1),
+    (1, 4, 2), (0, 3, 2), (3, 2, 0), (2, 3, 2), (0, 0, 3), (1, 2, 3), (2, 4, 2), (2, 1, 1),
+    (3, 3, 0), (2, 0, 2), (2, 5, 1), (2, 2, 1), (0, 4, 3), (3, 4, 0), (1, 0, 3), (3, 5, 0),
+    (3, 0, 1), (1,), (3, 1, 1), (1, 1, 3), (1, 5, 3), (0, 2, 4), (0, 5, 4), (1, 3, 2),
+    (1, 4, 3), (0, 0, 4), (3, 2, 1), (0, 3, 3), (0, 1, 3), (2, 5, 2), (2, 4, 3), (2, 3, 3),
+    (3, 3, 1), (0, 4, 4), (2, 0, 3), (2, 2, 2), (1, 2, 4), (3, 0, 2), (3, 4, 1), (3, 1, 2),
+    (2,), (2, 1, 2), (1, 0, 4), (3, 5, 1), (1, 1, 4), (0, 2, 5), (1, 5, 4), (0, 0, 5),
+    (0, 3, 4), (0, 5, 5), (3, 2, 2), (2, 5, 3), (1, 3, 3), (0, 1, 4), (2, 4, 4), (1, 4, 4),
+    (3, 0, 3), (2, 3, 4), (3, 3, 2), (3, 1, 3), (1, 2, 5), (2, 0, 4), (2, 2, 3), (3,),
+    (3, 5, 2), (0, 4, 5), (1, 0, 5), (2, 1, 3), (0, 3, 5), (3, 4, 2), (1, 1, 5), (0, 5, 6),
+    (1, 5, 5), (2, 5, 4), (0, 1, 5), (2, 4, 5), (1, 3, 4), (3, 0, 4), (0, 0, 6), (2, 3, 5),
+    (3, 1, 4), (0, 2, 6), (3, 2, 3), (3, 3, 3), (2, 0, 5), (3, 5, 3), (2, 2, 4), (0, 4, 6),
+    (1, 4, 5), (1, 2, 6), (0, 3, 6), "feed_out", (2, 5, 5), (2, 4, 6), (4,), (3, 0, 5),
+    (1, 0, 6), (2, 1, 4), (3, 1, 5), (3, 4, 3), (1, 1, 6), (1, 3, 5), (2, 3, 6), (1, 5, 6),
+    (0, 1, 6), (3, 3, 4), (3, 5, 4), (0, 4, 7), (2, 2, 5), (3, 2, 4), (0, 2, 7), (3, 0, 6),
+    (0, 3, 7), (2, 1, 5), (2, 5, 6), (3, 4, 4), (3, 1, 6), (5,), (0, 5, 7), (0, 0, 7),
+    (2, 3, 7), (1, 4, 6), (0, 1, 7), (2, 0, 6), (3, 2, 5), (1, 3, 6), (3, 5, 5), (3, 3, 5),
+    (3, 0, 7), (1, 2, 7), (0, 4, 8), (2, 5, 7), (2, 2, 6), (1, 1, 7), (2, 1, 6), (1, 5, 7),
+    (3, 2, 6), (3, 4, 5), "close", (6,), (0, 3, 8), (1, 0, 7), (7,), (3, 3, 6),
+    (1, 4, 7), (0, 1, 8), (2, 4, 7), (1, 3, 7), (3, 5, 6), (0, 0, 8), (3, 0, 8), (3, 4, 6),
+    (2, 2, 7), (3, 2, 7), (1, 2, 8), (0, 2, 8), (0, 4, 9), (0, 5, 8), (2, 0, 7), (2, 1, 7),
+    (2, 3, 8), (3, 3, 7), (2, 2, 8), (0, 3, 9), (3, 1, 7), (3, 5, 7), (1, 1, 8), (1, 0, 8),
+    (2, 5, 8), (3, 4, 7), (1, 5, 8), (0, 1, 9), (3, 2, 8), (1, 4, 8), (1, 3, 8), (2, 1, 8),
+    (0, 0, 9), (2, 4, 8), (0, 5, 9), (3, 3, 8), (3, 1, 8), (0, 2, 9), (2, 0, 8), (3, 5, 8),
+    (3, 4, 8),
 )
 
 
@@ -805,7 +862,7 @@
             source = slim[0, c, rows, 384:] if part == 0 else slim[1, c, rows, (part - 1) * 384 : part * 384]
             qkv[:, first : first + 384] = source.astype(F32)
         for h in range(2):
-            down[2 * c + h] = wide[0, c, rows, h * WIDTH : (h + 1) * WIDTH].astype(F32)
+            down[c, h] = wide[0, c, rows, h * WIDTH : (h + 1) * WIDTH].astype(F32)
 
     @pl.when(pl.program_id(0) == 0)
     def _():
@@ -819,7 +876,7 @@
             up_bias[t * WIDTH : (t + 1) * WIDTH] = vec[8 + t]
 
 
-SPREAD_ROWS = 64
+SPREAD_ROWS = 128
 
 
 def spread(*given):
@@ -842,8 +899,8 @@
         flat(HIDDEN),
         line(HIDDEN),
         (
-            jax.ShapeDtypeStruct((4, WIDTH, WIDTH), F32),
-            pl.BlockSpec((4, rows, WIDTH), lambda i: (0, i, 0)),
+            jax.ShapeDtypeStruct((2, 2 * DIMS, TOK, WIDTH), F32),
+            pl.BlockSpec((2, 2, TOK, WIDTH), lambda i: (0, i, 0, 0)),
         ),
         line(WIDTH),
     ]

time: 102 us -> 100 us (0.980)
  Pallas kernels: 101 us -> 99.5 us
    pallas_call x1, Pallas kernels: 91 us -> 89.7 us  [body(): pl.pallas_call(kernel, out_shape=[pltpu.VMEM((1, TOK, WIDTH), BF), pltpu....]
where the time goes in v6:
time: 100 us
  Pallas kernels  99.5 us (100%)
    pallas_call x1, Pallas kernels, body(): pl.pallas_call(kernel, out_shape=[pltpu.VMEM((1, TOK, WIDTH), BF), pltpu....  89.7 us
    pallas_call x1, Pallas kernels, spread(): pl.pallas_call(spread_kernel, grid=(WIDTH // rows,), out_shape=[o[0] for...  9.86 us

profile of v6, /device:TPU:1, one launch (start us, length us, event | category | flops | bytes accessed | tf_op | source)
XLA Modules:
  0.0 100.3 jit_solution(11373496998961208041)
XLA Ops:
  0.7 89.7 %shard_map.280 = (bf16[1,128,768]{2,1,0:T(8,128)(2,1)S(1)}, bf16[1,128,768]{2,1,0:T(8,128)(2,1)S(1)}, bf16[2,2,768,1536]{3,2,1,0:T(8,128)(2,1)S(1)}, bf16[2,2,768,768]{3,2,1,0:T(8,128)(2,1)S(1)}, f32[16,768]{1,0:T(8,128)S(1)}) custom-call(s32[1,4]{1,0:T(1,128)} %lengths.1, s32[1,4]{1,0:T(1,128)} %order.1, bf16[1,128,768]{2,1,0:T(8,128)(2,1)} %x.1, ...), custom_call_target="tpu_custom_call" | custom-call | tf_op jit(solution)/shard_map/pallas_call | solution.py:939
  90.3 9.9 %shard_map.281 = (bf16[1,128,768]{2,1,0:T(8,128)(2,1)}, bf16[1,128,768]{2,1,0:T(8,128)(2,1)}, f32[768]{0:T(1024)}, f32[768]{0:T(1024)}, f32[768,2304]{1,0:T(8,12...) custom-call(bf16[2,2,768,1536]{3,2,1,0:T(8,128)(2,1)S(1)} %get-tuple, ...), custom_call_target="tpu_custom_call" | custom-call | tf_op jit(solution)/shard_map/pallas_call | solution.py:907

commit v7 on v6

--- a/solution.py
+++ b/solution.py
@@ -145,7 +145,7 @@
             src_ref=src,
             dst_ref=dst,
             send_sem=self.send_sem.at[w, k],
-            recv_sem=self.recv_sem.at[w, k, s],
+            recv_sem=self.recv_sem.at[w, k, s - (w == DOWN)],
             device_id=self.at.partners[d],
             device_id_type=MESH,
         )
@@ -276,7 +276,7 @@
         landing_wide=v((2, DIMS, 160, HALF), BF),
         landing_slim=v((2, DIMS, 160, WIDTH), BF),
         send_sem=dma((sets, DIMS)),
-        recv_sem=dma((sets, DIMS, DIMS + max(HALVINGS))),
+        recv_sem=dma((sets, DIMS, DIMS + max(HALVINGS[0] - 1, *HALVINGS[1:]))),
         over_sem=dma((2, sets)),
         side_send=dma((22,)),
         side_recv=dma((22,)),

time: 100 us -> 100 us (level)
  no operation moved by 1% of the time
where the time goes in v7:
time: 100 us
  Pallas kernels  99.3 us (99%)
    pallas_call x1, Pallas kernels, body(): pl.pallas_call(kernel, out_shape=[pltpu.VMEM((1, TOK, WIDTH), BF), pltpu....  89.5 us
    pallas_call x1, Pallas kernels, spread(): pl.pallas_call(spread_kernel, grid=(WIDTH // rows,), out_shape=[o[0] for...  9.86 us

profile of v7, /device:TPU:1, one launch (start us, length us, event | category | flops | bytes accessed | tf_op | source)
XLA Modules:
  0.0 100.1 jit_solution(10111548633889777488)
XLA Ops:
  0.7 89.5 %shard_map.280 = (bf16[1,128,768]{2,1,0:T(8,128)(2,1)S(1)}, bf16[1,128,768]{2,1,0:T(8,128)(2,1)S(1)}, bf16[2,2,768,1536]{3,2,1,0:T(8,128)(2,1)S(1)}, bf16[2,2,768,768]{3,2,1,0:T(8,128)(2,1)S(1)}, f32[16,768]{1,0:T(8,128)S(1)}) custom-call(s32[1,4]{1,0:T(1,128)} %lengths.1, s32[1,4]{1,0:T(1,128)} %order.1, bf16[1,128,768]{2,1,0:T(8,128)(2,1)} %x.1, ...), custom_call_target="tpu_custom_call" | custom-call | tf_op jit(solution)/shard_map/pallas_call | solution.py:939
  90.1 9.9 %shard_map.281 = (bf16[1,128,768]{2,1,0:T(8,128)(2,1)}, bf16[1,128,768]{2,1,0:T(8,128)(2,1)}, f32[768]{0:T(1024)}, f32[768]{0:T(1024)}, f32[768,2304]{1,0:T(8,12...) custom-call(bf16[2,2,768,1536]{3,2,1,0:T(8,128)(2,1)S(1)} %get-tuple, ...), custom_call_target="tpu_custom_call" | custom-call | tf_op jit(solution)/shard_map/pallas_call | solution.py:907
